TPU v7x, 32 devices: a whole 2x2x4 slice. The times are simulated.
32 devices in a mesh: dp: 4 (over y, x), seq: 8 (over z, core).
Axes of the slice: x: 2, y: 2, z: 4, core: 2. Of those that a mesh axis runs over, the one named last changes fastest.
Arguments:
- hidden_input: bfloat16 [4, 1024, 768], P('dp', 'seq'), may hold values from -7.2 to 7.2
- triple_weight: bfloat16 [2, 768, 2304], P(None, ('dp', 'seq')), may hold values from -0.21875 to 0.21875
- mixer_weight: bfloat16 [2, 768, 768], P(None, ('dp', 'seq')), may hold values from -0.21875 to 0.21875
- expand_weight: bfloat16 [2, 768, 3072], P(None, ('dp', 'seq')), may hold values from -0.21875 to 0.21875
- shrink_weight: bfloat16 [2, 3072, 768], P(None, ('dp', 'seq')), may hold values from -0.109375 to 0.109375
- vector_params: bfloat16 [2, 12, 768], P(None, None, ('dp', 'seq')), may hold values from -1.5 to 1.5
- output_grad: bfloat16 [4, 1024, 768], P('dp', 'seq'), may hold values from -6 to 6
Outputs:
- hidden_output: bfloat16 [4, 1024, 768], P('dp', 'seq')
- input_grad: bfloat16 [4, 1024, 768], P('dp', 'seq')
- triple_grad: float32 [2, 768, 2304], P(None, ('dp', 'seq'))
- mixer_grad: float32 [2, 768, 768], P(None, ('dp', 'seq'))
- expand_grad: float32 [2, 768, 3072], P(None, ('dp', 'seq'))
- shrink_grad: float32 [2, 3072, 768], P(None, ('dp', 'seq'))
- vector_grad: float32 [2, 12, 768], P(None, None, ('dp', 'seq'))
- root_squares: float32 [2, 3], replicated
All inputs are finite; a program needn't handle non-finite values.
Results may differ from a plain program's by a relative error of at most 0.014.
Values may be sent and summed in bfloat16 or wider, within the bound.
No kernel may reach another device: no remote copies, remote signals or barrier semaphores. Data moves between devices by JAX's collectives and lax.ppermute only.
A program may use at most 448 MiB of HBM per device.

v0:
```python
import jax
import jax.numpy as jnp
from jax import lax
from jax.sharding import PartitionSpec as P

HEADS = 12
HEAD = 64
LAYERS = 2


EPSILON = 1e-12


def layer_norm(residual, gain_row, shift_row):
    center = residual - jnp.mean(residual, -1, keepdims=True)
    spread = jnp.mean(center * center, -1, keepdims=True)
    return center * lax.rsqrt(spread + EPSILON) * gain_row + shift_row


def gelu_exact(values):
    return jax.nn.gelu(values, approximate=False)


def split_heads(matrix):
    return matrix.reshape(matrix.shape[0], matrix.shape[1], HEADS, HEAD)


def scores_of(query_heads, key_piece):
    return jnp.einsum(
        "sqhd,skhd->shqk", query_heads, split_heads(key_piece), preferred_element_type=jnp.float32
    )


def forward_layer(hidden, params):
    triple, mixer, expand, shrink, vector_rows = params
    vectors = vector_rows.astype(jnp.float32)
    seq_count, row_count, model_width = hidden.shape
    flat_rows = hidden.reshape(seq_count * row_count, model_width)
    flat_low = flat_rows.astype(jnp.bfloat16)
    project = jnp.dot(flat_low, triple, preferred_element_type=jnp.float32)
    queries = (
        ((project[:, :model_width] + vectors[0]) * 0.125).astype(jnp.bfloat16).reshape(hidden.shape)
    )
    key_rows = project[:, model_width : 2 * model_width].astype(jnp.bfloat16).reshape(hidden.shape)
    value_rows = (
        (project[:, 2 * model_width :] + vectors[1]).astype(jnp.bfloat16).reshape(hidden.shape)
    )
    query_heads = split_heads(queries)
    start_max = jnp.full((seq_count, HEADS, row_count), -1e30, jnp.float32)
    whole_pair = None
    row_max = start_max
    scores = scores_of(query_heads, (lax.all_gather(key_rows, "seq", axis=1, tiled=True),)[0])
    new_max = jnp.maximum(row_max, jnp.max(scores, -1))
    row_total = jnp.sum(jnp.exp(scores - new_max[..., None]), -1)
    row_max, row_total = (new_max, row_total)
    log_total = row_max + jnp.log(row_total)
    scores = scores_of(query_heads, lax.all_gather(key_rows, "seq", axis=1, tiled=True))
    probability = jnp.exp(scores - log_total[..., None]).astype(jnp.bfloat16)
    mixed = jnp.einsum(
        "shqk,skhd->sqhd",
        probability,
        split_heads(lax.all_gather(value_rows, "seq", axis=1, tiled=True)),
        preferred_element_type=jnp.float32,
    )
    attended = mixed.reshape(seq_count * row_count, model_width)
    attended_low = attended.astype(jnp.bfloat16)
    attn_out = jnp.dot(attended_low, mixer, preferred_element_type=jnp.float32) + vectors[2]
    residual_one = flat_rows + attn_out
    normed = layer_norm(residual_one, vectors[3], vectors[4])
    normed_low = normed.astype(jnp.bfloat16)
    pre_act = jnp.dot(normed_low, expand, preferred_element_type=jnp.float32) + vectors[
        5:9
    ].reshape(-1)
    act_low = gelu_exact(pre_act).astype(jnp.bfloat16)
    ffn_out = jnp.dot(act_low, shrink, preferred_element_type=jnp.float32) + vectors[9]
    residual_two = normed + ffn_out
    output = layer_norm(residual_two, vectors[10], vectors[11])
    square_sums = jnp.stack(
        [jnp.sum(flat_rows * flat_rows), jnp.sum(attn_out * attn_out), jnp.sum(ffn_out * ffn_out)]
    )
    saved_state = (
        flat_low,
        queries,
        key_rows,
        value_rows,
        whole_pair,
        log_total,
        attended,
        attended_low,
        residual_one,
        normed_low,
        pre_act,
        act_low,
        residual_two,
    )
    return (output.reshape(hidden.shape), saved_state, square_sums)


def backward_layer(grad_state, params, saved_state):
    triple, mixer, expand, shrink, vector_rows = params
    vectors = vector_rows.astype(jnp.float32)
    (
        flat_low,
        queries,
        key_rows,
        value_rows,
        whole_pair,
        log_total,
        attended,
        attended_low,
        residual_one,
        normed_low,
        pre_act,
        act_low,
        residual_two,
    ) = saved_state
    seq_count, row_count, model_width = queries.shape
    grad_flat = grad_state.reshape(seq_count * row_count, model_width)
    _, pull_two = jax.vjp(layer_norm, residual_two, vectors[10], vectors[11])
    grad_residual_two, grad_gain_two, grad_shift_two = pull_two(grad_flat)
    grad_ffn = grad_residual_two.astype(jnp.bfloat16)
    grad_shrink = jnp.dot(act_low.T, grad_ffn, preferred_element_type=jnp.float32)
    grad_down_bias = jnp.sum(grad_ffn.astype(jnp.float32), 0)
    grad_act = jnp.dot(grad_ffn, shrink.T, preferred_element_type=jnp.float32)
    _, pull_gelu = jax.vjp(gelu_exact, pre_act)
    grad_pre = pull_gelu(grad_act)[0].astype(jnp.bfloat16)
    grad_expand = jnp.dot(normed_low.T, grad_pre, preferred_element_type=jnp.float32)
    grad_ffn_bias = jnp.sum(grad_pre.astype(jnp.float32), 0)
    grad_normed = grad_residual_two + jnp.dot(
        grad_pre, expand.T, preferred_element_type=jnp.float32
    )
    _, pull_one = jax.vjp(layer_norm, residual_one, vectors[3], vectors[4])
    grad_residual_one, grad_gain_one, grad_shift_one = pull_one(grad_normed)
    grad_attn = grad_residual_one.astype(jnp.bfloat16)
    grad_mixer = jnp.dot(attended_low.T, grad_attn, preferred_element_type=jnp.float32)
    grad_out_bias = jnp.sum(grad_attn.astype(jnp.float32), 0)
    grad_attended = jnp.dot(grad_attn, mixer.T, preferred_element_type=jnp.float32).astype(
        jnp.bfloat16
    )
    grad_attended = grad_attended.reshape(queries.shape)
    grad_heads = split_heads(grad_attended)
    row_delta = jnp.einsum(
        "sqhd,sqhd->shq",
        grad_heads.astype(jnp.float32),
        split_heads(attended.reshape(queries.shape)),
    )
    query_heads = split_heads(queries)
    key_piece = lax.all_gather(key_rows, "seq", axis=1, tiled=True)
    value_piece = lax.all_gather(value_rows, "seq", axis=1, tiled=True)
    scores = scores_of(query_heads, key_piece)
    probability = jnp.exp(scores - log_total[..., None])
    grad_prob = jnp.einsum(
        "sqhd,skhd->shqk", grad_heads, split_heads(value_piece), preferred_element_type=jnp.float32
    )
    grad_scores = (probability * (grad_prob - row_delta[..., None])).astype(jnp.bfloat16)
    grad_query = jnp.einsum(
        "shqk,skhd->sqhd", grad_scores, split_heads(key_piece), preferred_element_type=jnp.float32
    )
    whole_lse, whole_delta = (
        lax.all_gather(log_total, "seq", axis=2, tiled=True),
        lax.all_gather(row_delta, "seq", axis=2, tiled=True),
    )
    own_keys = split_heads(key_rows)
    own_values = split_heads(value_rows)
    query_piece = lax.all_gather(queries, "seq", axis=1, tiled=True)
    grad_piece = lax.all_gather(grad_attended, "seq", axis=1, tiled=True)
    query_part = split_heads(query_piece)
    grad_part = split_heads(grad_piece)
    scores = jnp.einsum("sqhd,skhd->shqk", query_part, own_keys, preferred_element_type=jnp.float32)
    probability = jnp.exp(scores - whole_lse[..., None])
    grad_values = jnp.einsum(
        "shqk,sqhd->skhd",
        probability.astype(jnp.bfloat16),
        grad_part,
        preferred_element_type=jnp.float32,
    )
    grad_prob = jnp.einsum(
        "sqhd,skhd->shqk", grad_part, own_values, preferred_element_type=jnp.float32
    )
    grad_scores = (probability * (grad_prob - whole_delta[..., None])).astype(jnp.bfloat16)
    grad_keys = jnp.einsum(
        "shqk,sqhd->skhd", grad_scores, query_part, preferred_element_type=jnp.float32
    )
    grad_keys, grad_values = (grad_keys, grad_values)
    flat_shape = (seq_count * row_count, model_width)
    grad_query_part = grad_query.astype(jnp.bfloat16).reshape(flat_shape) * 0.125
    grad_value_part = grad_values.astype(jnp.bfloat16).reshape(flat_shape)
    grad_project = jnp.concatenate(
        [grad_query_part, grad_keys.astype(jnp.bfloat16).reshape(flat_shape), grad_value_part], -1
    )
    grad_triple = jnp.dot(flat_low.T, grad_project, preferred_element_type=jnp.float32)
    grad_query_bias = jnp.sum(grad_query_part.astype(jnp.float32), 0)
    grad_value_bias = jnp.sum(grad_value_part.astype(jnp.float32), 0)
    grad_hidden = grad_residual_one + jnp.dot(
        grad_project, triple.T, preferred_element_type=jnp.float32
    )
    grad_vector = jnp.concatenate(
        [
            jnp.stack(
                [grad_query_bias, grad_value_bias, grad_out_bias, grad_gain_one, grad_shift_one]
            ),
            grad_ffn_bias.reshape(4, model_width),
            jnp.stack([grad_down_bias, grad_gain_two, grad_shift_two]),
        ],
        0,
    )
    terms = (grad_triple, grad_mixer, grad_expand, grad_shrink, grad_vector.T)
    return (grad_hidden.reshape(queries.shape), terms)


def per_device(
    hidden_input,
    triple_weight,
    mixer_weight,
    expand_weight,
    shrink_weight,
    vector_params,
    output_grad,
):
    hidden = hidden_input.astype(jnp.float32)
    kept_params = []
    kept_saved = []
    collected = []
    for layer_index in range(LAYERS):
        gathered = (
            lax.all_gather(triple_weight[layer_index], ("dp", "seq"), axis=0, tiled=True),
            lax.all_gather(mixer_weight[layer_index], ("dp", "seq"), axis=0, tiled=True),
            lax.all_gather(expand_weight[layer_index], ("dp", "seq"), axis=0, tiled=True),
            lax.all_gather(shrink_weight[layer_index], ("dp", "seq"), axis=0, tiled=True),
            lax.all_gather(vector_params[layer_index].T, ("dp", "seq"), axis=0, tiled=True),
        )
        params = (gathered[0], gathered[1], gathered[2], gathered[3], gathered[4].T)
        hidden, saved_state, square_sums = forward_layer(hidden, params)
        kept_params.append(params)
        kept_saved.append(saved_state)
        collected.append(square_sums)
    totals = lax.psum(jnp.stack(collected), ("dp", "seq"))
    element_count = (
        hidden.shape[0]
        * hidden.shape[1]
        * hidden.shape[2]
        * lax.axis_size("dp")
        * lax.axis_size("seq")
    )
    root_squares = jnp.sqrt(totals / element_count)
    grad_state = output_grad.astype(jnp.float32)
    term_list = [None] * LAYERS
    for layer_index in reversed(range(LAYERS)):
        gathered = (
            lax.all_gather(triple_weight[layer_index], ("dp", "seq"), axis=0, tiled=True),
            lax.all_gather(mixer_weight[layer_index], ("dp", "seq"), axis=0, tiled=True),
            lax.all_gather(expand_weight[layer_index], ("dp", "seq"), axis=0, tiled=True),
            lax.all_gather(shrink_weight[layer_index], ("dp", "seq"), axis=0, tiled=True),
            lax.all_gather(vector_params[layer_index].T, ("dp", "seq"), axis=0, tiled=True),
        )
        params = (gathered[0], gathered[1], gathered[2], gathered[3], gathered[4].T)
        grad_state, terms = backward_layer(grad_state, params, kept_saved[layer_index])
        terms = (
            lax.psum_scatter(terms[0], ("dp", "seq"), scatter_dimension=0, tiled=True),
            lax.psum_scatter(terms[1], ("dp", "seq"), scatter_dimension=0, tiled=True),
            lax.psum_scatter(terms[2], ("dp", "seq"), scatter_dimension=0, tiled=True),
            lax.psum_scatter(terms[3], ("dp", "seq"), scatter_dimension=0, tiled=True),
            lax.psum_scatter(terms[4], ("dp", "seq"), scatter_dimension=0, tiled=True),
        )
        term_list[layer_index] = terms
    stacked = tuple(
        (
            jnp.stack([term_list[layer_index][member] for layer_index in range(LAYERS)])
            for member in range(5)
        )
    )
    vector_grad = jnp.transpose(stacked[4], (0, 2, 1))
    return (
        hidden.astype(jnp.bfloat16),
        grad_state.astype(jnp.bfloat16),
        stacked[0],
        stacked[1],
        stacked[2],
        stacked[3],
        vector_grad,
        root_squares,
    )


def solution(mesh):
    return jax.shard_map(
        per_device,
        mesh=mesh,
        in_specs=(
            P("dp", "seq", None),
            P(None, ("dp", "seq"), None),
            P(None, ("dp", "seq"), None),
            P(None, ("dp", "seq"), None),
            P(None, ("dp", "seq"), None),
            P(None, None, ("dp", "seq")),
            P("dp", "seq", None),
        ),
        out_specs=(
            P("dp", "seq", None),
            P("dp", "seq", None),
            P(None, ("dp", "seq"), None),
            P(None, ("dp", "seq"), None),
            P(None, ("dp", "seq"), None),
            P(None, ("dp", "seq"), None),
            P(None, None, ("dp", "seq")),
            P(),
        ),
        check_vma=False,
    )
```

profile of v0, /device:TPU:0, one launch (start us, length us, event | category | flops | bytes accessed | tf_op | source)
XLA Modules:
  0.0 1973.0 jit_solution(1747883067043757473)
XLA Ops:
  10.3 43.9 %all-gather.20 = bf16[32,24,12]{1,2,0:T(8,128)(2,1)S(1)} all-gather(bf16[1,24,12]{1,2,0:T(8,128)(2,1)S(1)} %bitcast.359), channel_id=1, replica_groups=mesh['dp'=4,'seq'=8] {'dp','seq'}, dimensions={0}, use_global_device_ids=true | all-gather | bytes 19008 | tf_op jit(solution)/shard_map/all_gather | solution.py:230
  55.3 19.4 all-gather.39.cloned.1.call-done
  82.3 19.9 %all-gather.41.cloned.1.call-done = bf16[1024,768]{1,0:T(8,128)(2,1)} async-done(((bf16[128,768]{1,0:T(8,128)(2,1)}), bf16[1024,768]{1,0:T(8,128)(2,1)}) %all-gather.41.cloned.1.call-update) | async-done | bytes 1572880 | tf_op jit(solution)/shard_map/all_gather | solution.py:62
  103.9 24.6 %all-gather.43.cloned.1.call-done = bf16[1024,768]{1,0:T(8,128)(2,1)} async-done(((bf16[128,768]{1,0:T(8,128)(2,1)}), bf16[1024,768]{1,0:T(8,128)(2,1)}) %all-gather.43.cloned.1.call-update) | async-done | bytes 1572880 | tf_op jit(solution)/shard_map/all_gather | solution.py:57
  138.3 46.8 %all-gather.45.cloned.1.call-done = bf16[1,768,768]{2,1,0:T(8,128)(2,1)} async-done(((bf16[1,24,768]{2,1,0:T(8,128)(2,1)}), bf16[1,768,768]{2,1,0:T(8,128)(2,1)}) %all-gather.45.cloned.1.call-update) | async-done | bytes 1179664 | tf_op jit(solution)/shard_map/all_gather | solution.py:227
  187.7 63.4 %all-gather.47.cloned.1.call-done = bf16[1,768,3072]{2,1,0:T(8,128)(2,1)} async-done(((bf16[1,24,3072]{2,1,0:T(8,128)(2,1)}), bf16[1,768,3072]{2,1,0:T(8,128)(2,1)}) %all-gather.47.cloned.1.call-update) | async-done | bytes 4718608 | tf_op jit(solution)/shard_map/all_gather | solution.py:228
  251.1 8.4 multiply_convert_fusion.9
  259.5 57.6 %all-gather.49.cloned.1.call-done = bf16[1,3072,768]{2,1,0:T(8,128)(2,1)} async-done(((bf16[1,96,768]{2,1,0:T(8,128)(2,1)}), bf16[1,3072,768]{2,1,0:T(8,128)(2,1)}) %all-gather.49.cloned.1.call-update) | async-done | bytes 4718608 | tf_op jit(solution)/shard_map/all_gather | solution.py:229
  321.2 58.0 %all-gather.51.cloned.1.call-done = bf16[1,768,2304]{2,1,0:T(8,128)(2,1)} async-done(((bf16[1,24,2304]{2,1,0:T(8,128)(2,1)}), bf16[1,768,2304]{2,1,0:T(8,128)(2,1)}) %all-gather.51.cloned.1.call-update) | async-done | bytes 3538960 | tf_op jit(solution)/shard_map/all_gather | solution.py:226
  383.9 40.1 %all-gather.21 = bf16[32,24,12]{1,2,0:T(8,128)(2,1)S(1)} all-gather(bf16[1,24,12]{1,2,0:T(8,128)(2,1)S(1)} %bitcast.360), channel_id=1, replica_groups=mesh['dp'=4,'seq'=8] {'dp','seq'}, dimensions={0}, use_global_device_ids=true | all-gather | bytes 19008 | tf_op jit(solution)/shard_map/all_gather | solution.py:230
  437.9 11.3 all-gather.53.cloned.1.call-done
  451.9 5.4 bitcast_convert_fusion.1
  457.2 48.6 %all-gather.57.cloned.1.call-done = bf16[1,768,768]{2,1,0:T(8,128)(2,1)} async-done(((bf16[1,24,768]{2,1,0:T(8,128)(2,1)}), bf16[1,768,768]{2,1,0:T(8,128)(2,1)}) %all-gather.57.cloned.1.call-update) | async-done | bytes 1179664 | tf_op jit(solution)/shard_map/all_gather | solution.py:227
  510.1 62.0 %all-gather.59.cloned.1.call-done = bf16[1,768,3072]{2,1,0:T(8,128)(2,1)} async-done(((bf16[1,24,3072]{2,1,0:T(8,128)(2,1)}), bf16[1,768,3072]{2,1,0:T(8,128)(2,1)}) %all-gather.59.cloned.1.call-update) | async-done | bytes 4718608 | tf_op jit(solution)/shard_map/all_gather | solution.py:228
  572.1 8.6 multiply_convert_fusion.8
  580.6 57.4 %all-gather.61.cloned.1.call-done = bf16[1,3072,768]{2,1,0:T(8,128)(2,1)} async-done(((bf16[1,96,768]{2,1,0:T(8,128)(2,1)}), bf16[1,3072,768]{2,1,0:T(8,128)(2,1)}) %all-gather.61.cloned.1.call-update) | async-done | bytes 4718608 | tf_op jit(solution)/shard_map/all_gather | solution.py:229
  638.1 4.2 fusion.167
  657.6 15.2 all-gather.13
  676.2 15.1 all-gather.15
  691.3 7.5 convert_reduce_fusion.6
  701.6 5.1 fusion.183
  709.3 6.0 convert_reduce_fusion.5
  715.3 8.8 fusion.99
  724.1 4.6 multiply_reduce_fusion.6
  730.2 4.8 convert_reduce_fusion.1
  747.0 15.5 all-gather.17
  762.5 5.2 fusion.184
  781.4 7.1 convert_reduce_fusion.10
  798.8 4.1 concatenate.15
  809.1 6.4 convert_reduce_fusion.9
  826.9 5.2 fusion.141
  833.9 15.1 all-gather.19
  849.0 8.6 fusion.98
  857.6 5.0 convolution_bitcast_fusion
  862.6 8.0 copy.122
  871.8 5.1 fusion.157
  878.1 5.2 fusion.160
  884.4 5.1 fusion.188
  890.5 5.1 fusion.187
  900.8 41.0 %all-reduce.5.cloned.1.call-done = (f32[768,12]{0,1:T(8,128)}, f32[768,12]{0,1:T(8,128)}, f32[2,3]{1,0:T(2,128)}) async-done(((f32[768,12]{0,1:T(8,128)}, f32[768,12]{0,1:T(8,128)}, f32[2,3]{1,0:T(2,128)}), (f32[768,12]{0,1:T(8,128)}, f32[768,12]{0,1:T(8,128)}, f32[2,3]{1,0:T(2,128)})) %all-reduce.5.cloned.1.call-update) | async-done | bytes 73768
  945.2 101.8 %reduce-scatter.17.cloned.1.call-done = f32[24,768]{1,0:T(8,128)} async-done(((f32[768,768]{1,0:T(8,128)}), f32[24,768]{1,0:T(8,128)}) %reduce-scatter.17.cloned.1.call-update) | async-done | bytes 73744 | tf_op jit(solution)/shard_map/reduce_scatter | solution.py:260
  1046.9 104.1 %reduce-scatter.15.cloned.1.call-done = f32[24,768]{1,0:T(8,128)} async-done(((f32[768,768]{1,0:T(8,128)}), f32[24,768]{1,0:T(8,128)}) %reduce-scatter.15.cloned.1.call-update) | async-done | bytes 73744 | tf_op jit(solution)/shard_map/reduce_scatter | solution.py:260
  1152.7 122.1 %reduce-scatter.29.cloned.1.call-done = f32[24,2304]{1,0:T(8,128)} async-done(((f32[768,2304]{1,0:T(8,128)}), f32[24,2304]{1,0:T(8,128)}) %reduce-scatter.29.cloned.1.call-update) | async-done | bytes 221200
  1276.4 123.5 %reduce-scatter.27.cloned.1.call-done = f32[24,2304]{1,0:T(8,128)} async-done(((f32[768,2304]{1,0:T(8,128)}), f32[24,2304]{1,0:T(8,128)}) %reduce-scatter.27.cloned.1.call-update) | async-done | bytes 221200
  1402.4 138.4 %reduce-scatter.21.cloned.1.call-done = f32[24,3072]{1,0:T(8,128)} async-done(((f32[768,3072]{1,0:T(8,128)}), f32[24,3072]{1,0:T(8,128)}) %reduce-scatter.21.cloned.1.call-update) | async-done | bytes 294928 | tf_op jit(solution)/shard_map/reduce_scatter | solution.py:261
  1540.8 141.5 %reduce-scatter.19.cloned.1.call-done = f32[24,3072]{1,0:T(8,128)} async-done(((f32[768,3072]{1,0:T(8,128)}), f32[24,3072]{1,0:T(8,128)}) %reduce-scatter.19.cloned.1.call-update) | async-done | bytes 294928 | tf_op jit(solution)/shard_map/reduce_scatter | solution.py:261
  1684.1 138.5 %reduce-scatter.25.cloned.1.call-done = f32[96,768]{1,0:T(8,128)} async-done(((f32[3072,768]{1,0:T(8,128)}), f32[96,768]{1,0:T(8,128)}) %reduce-scatter.25.cloned.1.call-update) | async-done | bytes 294928 | tf_op jit(solution)/shard_map/reduce_scatter | solution.py:262
  1822.6 141.5 %reduce-scatter.23.cloned.1.call-done = f32[96,768]{1,0:T(8,128)} async-done(((f32[3072,768]{1,0:T(8,128)}), f32[96,768]{1,0:T(8,128)}) %reduce-scatter.23.cloned.1.call-update) | async-done | bytes 294928 | tf_op jit(solution)/shard_map/reduce_scatter | solution.py:262
  (335 shorter events, 157.9 us)
Async XLA Ops:
  7.2 67.5 %copy-start.15 = (bf16[1,128,768]{2,1,0:T(8,128)(2,1)S(1)}, bf16[1,128,768]{2,1,0:T(8,128)(2,1)}, u32[]{:S(2)}) copy-start(bf16[1,128,768]{2,1,0:T(8,128)(2,1)} %param.7) | copy-start | bytes 589828
  7.2 67.5 %all-gather.39.cloned.1.call-start = ((), (), s32[]{:S(2)}) async-start(), calls=%async_computation.14 | async-start | bytes 3649536 | tf_op jit(solution)/shard_map/all_gather | solution.py:226
  8.9 93.2 %all-gather.41.cloned.1.call-start = ((), (), s32[]{:S(2)}) async-start(), calls=%async_computation.15 | async-start | bytes 1769472 | tf_op jit(solution)/shard_map/all_gather | solution.py:62
  55.3 323.9 %copy-start.31 = (f32[768]{0:T(1024)}, f32[768]{0:T(1024)S(1)}, u32[]{:S(2)}) copy-start(f32[768]{0:T(1024)S(1)} %get-tuple-element.60) | copy-start | bytes 9220
  55.3 323.9 %copy-start.36 = (f32[768]{0:T(1024)}, f32[768]{0:T(1024)S(1)}, u32[]{:S(2)}) copy-start(f32[768]{0:T(1024)S(1)} %get-tuple-element.61) | copy-start | bytes 9220
  78.2 50.3 %all-gather.43.cloned.1.call-start = ((), (), s32[]{:S(2)}) async-start(), calls=%async_computation.16 | async-start | bytes 1769472 | tf_op jit(solution)/shard_map/all_gather | solution.py:57
  78.9 106.1 %all-gather.45.cloned.1.call-start = ((), (), s32[]{:S(2)}) async-start(), calls=%async_computation.17 | async-start | bytes 1216512 | tf_op jit(solution)/shard_map/all_gather | solution.py:227
  79.6 171.5 %all-gather.47.cloned.1.call-start = ((), (), s32[]{:S(2)}) async-start(), calls=%async_computation.18 | async-start | bytes 4866048 | tf_op jit(solution)/shard_map/all_gather | solution.py:228
  80.5 236.6 %all-gather.49.cloned.1.call-start = ((), (), s32[]{:S(2)}) async-start(), calls=%async_computation.19 | async-start | bytes 4866048 | tf_op jit(solution)/shard_map/all_gather | solution.py:229
  81.3 297.9 %all-gather.51.cloned.1.call-start = ((), (), s32[]{:S(2)}) async-start(), calls=%async_computation.20 | async-start | bytes 3649536 | tf_op jit(solution)/shard_map/all_gather | solution.py:226
  82.0 348.1 %all-gather.55.cloned.1.call-start = ((), (), s32[]{:S(2)}) async-start(), calls=%async_computation.22 | async-start | bytes 1769472 | tf_op jit(solution)/shard_map/all_gather | solution.py:57
  138.3 121.2 %copy-start.19 = (bf16[1,128,12,64]{1,3,2,0:T(8,128)(2,1)}, bf16[1,128,12,64]{1,3,2,0:T(8,128)(2,1)S(1)}, u32[]{:S(2)}) copy-start(bf16[1,128,12,64]{1,3,2,0:T(8,128)(2,1)S(1)} %get-tuple-element.121) | copy-start | bytes 589828
  187.5 129.6 %copy-start.39 = (f32[128]{0:T(128)}, f32[128]{0:T(128)S(1)}, u32[]{:S(2)}) copy-start(f32[128]{0:T(128)S(1)} %broadcast_multiply_fusion.3) | copy-start | bytes 1540
  187.7 63.5 %copy-start.56 = (f32[128]{0:T(128)}, f32[128]{0:T(128)S(1)}, u32[]{:S(2)}) copy-start(f32[128]{0:T(128)S(1)} %multiply_reduce_fusion.14) | copy-start | bytes 1540
  187.7 129.4 %copy-start.49 = (f32[128]{0:T(128)}, f32[128]{0:T(128)S(1)}, u32[]{:S(2)}) copy-start(f32[128]{0:T(128)S(1)} %fusion.147) | copy-start | bytes 1540
  251.1 66.0 %copy-start.45 = (f32[768]{0:T(1024)S(1)}, f32[768]{0:T(1024)}, u32[]{:S(2)}) copy-start(f32[768]{0:T(1024)} %get-tuple-element.62) | copy-start | bytes 9220
  321.0 60.9 %copy-start.47 = (f32[128]{0:T(128)}, f32[128]{0:T(128)S(1)}, u32[]{:S(2)}) copy-start(f32[128]{0:T(128)S(1)} %broadcast_multiply_fusion.2) | copy-start | bytes 1540
  321.2 60.7 %copy-start.58 = (f32[128]{0:T(128)}, f32[128]{0:T(128)S(1)}, u32[]{:S(2)}) copy-start(f32[128]{0:T(128)S(1)} %multiply_reduce_fusion.13) | copy-start | bytes 1540
  321.2 60.7 %copy-start.54 = (f32[128]{0:T(128)}, f32[128]{0:T(128)S(1)}, u32[]{:S(2)}) copy-start(f32[128]{0:T(128)S(1)} %fusion.148) | copy-start | bytes 1540
  383.8 65.4 %all-gather.53.cloned.1.call-start = ((), (), s32[]{:S(2)}) async-start(), calls=%async_computation.21 | async-start | bytes 1769472 | tf_op jit(solution)/shard_map/all_gather | solution.py:62
  426.9 78.9 %all-gather.57.cloned.1.call-start = ((), (), s32[]{:S(2)}) async-start(), calls=%async_computation.23 | async-start | bytes 1216512 | tf_op jit(solution)/shard_map/all_gather | solution.py:227
  427.5 144.6 %all-gather.59.cloned.1.call-start = ((), (), s32[]{:S(2)}) async-start(), calls=%async_computation.24 | async-start | bytes 4866048 | tf_op jit(solution)/shard_map/all_gather | solution.py:228
  428.2 209.8 %all-gather.61.cloned.1.call-start = ((), (), s32[]{:S(2)}) async-start(), calls=%async_computation.25 | async-start | bytes 4866048 | tf_op jit(solution)/shard_map/all_gather | solution.py:229
  428.8 270.0 %all-gather.63.cloned.1.call-start = ((), (), s32[]{:S(2)}) async-start(), calls=%async_computation.26 | async-start | bytes 1769472 | tf_op jit(solution)/shard_map/all_gather | solution.py:165
  430.0 276.7 %all-gather.65.cloned.1.call-start = ((), (), s32[]{:S(2)}) async-start(), calls=%async_computation.27 | async-start | bytes 1769472 | tf_op jit(solution)/shard_map/all_gather | solution.py:166
  437.9 14.0 copy-start.30
  638.0 6.8 slice-start
  638.0 5.2 copy-start.46
  638.0 6.8 slice-start.1
  638.0 6.8 copy-start.68
  653.5 90.9 %all-gather.67.cloned.1.call-start = ((), (), s32[]{:S(2)}) async-start(), calls=%async_computation.28 | async-start | bytes 1769472 | tf_op jit(solution)/shard_map/all_gather | solution.py:165
  654.1 153.3 %all-gather.69.cloned.1.call-start = ((), (), s32[]{:S(2)}) async-start(), calls=%async_computation.29 | async-start | bytes 1769472 | tf_op jit(solution)/shard_map/all_gather | solution.py:166
  724.1 5.6 copy-start.66
  724.1 10.9 slice-start.2
  729.7 5.3 copy-start.24
  730.2 4.9 copy-start.40
  730.2 4.9 copy-start.50
  741.1 200.7 %all-reduce.5.cloned.1.call-start = ((), (), s32[]{:S(2)}) async-start(), calls=%async_computation.32 | async-start | bytes 198656
  821.0 226.0 %reduce-scatter.17.cloned.1.call-start = ((), (), s32[]{:S(2)}) async-start(), calls=%async_computation.9 | async-start | bytes 2433024 | tf_op jit(solution)/shard_map/reduce_scatter | solution.py:260
  823.9 327.2 %reduce-scatter.15.cloned.1.call-start = ((), (), s32[]{:S(2)}) async-start(), calls=%async_computation.8 | async-start | bytes 2433024 | tf_op jit(solution)/shard_map/reduce_scatter | solution.py:260
  826.9 447.9 %reduce-scatter.29.cloned.1.call-start = ((), (), s32[]{:S(2)}) async-start(), calls=%async_computation.31 | async-start | bytes 7299072
  832.2 567.8 %reduce-scatter.27.cloned.1.call-start = ((), (), s32[]{:S(2)}) async-start(), calls=%async_computation.30 | async-start | bytes 7299072
  849.0 8.6 copy-start.16
  849.0 8.6 copy-start.26
  870.7 670.1 %reduce-scatter.21.cloned.1.call-start = ((), (), s32[]{:S(2)}) async-start(), calls=%async_computation.11 | async-start | bytes 9732096 | tf_op jit(solution)/shard_map/reduce_scatter | solution.py:261
  877.0 805.3 %reduce-scatter.19.cloned.1.call-start = ((), (), s32[]{:S(2)}) async-start(), calls=%async_computation.10 | async-start | bytes 9732096 | tf_op jit(solution)/shard_map/reduce_scatter | solution.py:261
  883.3 939.4 %reduce-scatter.25.cloned.1.call-start = ((), (), s32[]{:S(2)}) async-start(), calls=%async_computation.13 | async-start | bytes 9732096 | tf_op jit(solution)/shard_map/reduce_scatter | solution.py:262
  889.6 1074.6 %reduce-scatter.23.cloned.1.call-start = ((), (), s32[]{:S(2)}) async-start(), calls=%async_computation.12 | async-start | bytes 9732096 | tf_op jit(solution)/shard_map/reduce_scatter | solution.py:262
  (52 other events, 116.9 us)
Sparse Core Ops, SparseCore 0:
  11.6 63.0 all-gather.38
  78.3 23.8 all-gather.40
  103.8 24.5 all-gather.42
  131.3 53.7 all-gather.44
  188.5 62.5 all-gather.46
  254.6 62.4 all-gather.48
  320.1 59.0 all-gather.50
  383.9 24.2 all-gather.54
  427.0 22.1 all-gather.52
  452.1 53.7 all-gather.56
  509.4 62.5 all-gather.58
  575.5 62.4 all-gather.60
  639.7 23.8 all-gather.62
  665.1 25.0 all-gather.64
  691.6 24.3 all-gather.66
  741.2 24.5 all-gather.68
  821.1 120.5 all-reduce.4
  946.9 100.0 reduce-scatter.16
  1053.1 97.9 reduce-scatter.14
  1156.6 118.1 reduce-scatter.28
  1281.4 118.5 reduce-scatter.26
  1405.9 134.8 reduce-scatter.20
  1547.7 134.4 reduce-scatter.18
  1688.0 134.6 reduce-scatter.24
  1829.5 134.5 reduce-scatter.22
where the time goes:
time: 1980 us; the launch traced here: 1970 us
  waiting for transfers between devices  1520 us (77%)
  matrix products  161 us (8%)
  blocking collectives  145 us (7%)
  local copies, waits for them, and re-layouts  97.6 us (5%)
  other arithmetic  27.7 us (1%)
    unnamed x28, waiting for transfers between devices  290 us
    reduce_scatter x2, waiting for transfers between devices, per_device(): lax.psum_scatter(terms[3], ('dp', 'seq'), scatter_dimension=0, tiled=True)  280 us
    reduce_scatter x2, waiting for transfers between devices, per_device(): lax.psum_scatter(terms[2], ('dp', 'seq'), scatter_dimension=0, tiled=True)  280 us
    reduce_scatter x2, waiting for transfers between devices, per_device(): lax.psum_scatter(terms[1], ('dp', 'seq'), scatter_dimension=0, tiled=True)  206 us
    all_gather x2, waiting for transfers between devices, per_device(): lax.all_gather(expand_weight[layer_index], ('dp', 'seq'), axis=0, tiled=T...  125 us
    all_gather x2, waiting for transfers between devices, per_device(): lax.all_gather(shrink_weight[layer_index], ('dp', 'seq'), axis=0, tiled=T...  115 us
    all_gather x2, waiting for transfers between devices, per_device(): lax.all_gather(mixer_weight[layer_index], ('dp', 'seq'), axis=0, tiled=True)  95.4 us
    all_gather x2, blocking collectives, per_device(): lax.all_gather(vector_params[layer_index].T, ('dp', 'seq'), axis=0, tiled...  84.1 us
  transfers between devices with their start and end apart: 25, of which 20 were waited for; matrix products, arithmetic and copies ran while one was open for 13% of the time, Pallas kernels for 0%

commit v1 on v0

v1 whole, which is shorter than its diff:
```python
import jax
import jax.numpy as jnp
import numpy as np
from jax import lax
from jax.sharding import PartitionSpec as P

HEADS = 12
HEAD = 64
LAYERS = 2
VECS = 12
LANES = 128

EPSILON = 1e-12

BF = jnp.bfloat16
F32 = jnp.float32


def layer_norm(residual, gain_row, shift_row):
    center = residual - jnp.mean(residual, -1, keepdims=True)
    spread = jnp.mean(center * center, -1, keepdims=True)
    return center * lax.rsqrt(spread + EPSILON) * gain_row + shift_row


def gelu_exact(values):
    return jax.nn.gelu(values, approximate=False)


def matmul(left, right):
    return jnp.dot(left, right, preferred_element_type=F32)


def matmul_t(left, right):
    return lax.dot_general(left, right, (((1,), (1,)), ((), ())), preferred_element_type=F32)


def grad_matmul(left, right):
    return lax.dot_general(left, right, (((0,), (0,)), ((), ())), preferred_element_type=F32)


def chips_of():
    return lax.axis_size("seq") // 2


def core_swap(array):
    size = lax.axis_size("seq")
    return lax.ppermute(array, "seq", [(i, i ^ 1) for i in range(size)])


def chip_shift(array, step):
    size = lax.axis_size("seq")
    chips = size // 2
    pairs = [(i, ((i // 2 + step) % chips) * 2 + i % 2) for i in range(size)]
    return lax.ppermute(array, "seq", pairs)


def core_groups():
    size = lax.axis_size("seq")
    return [list(range(0, size, 2)), list(range(1, size, 2))]


def place():
    spot = lax.axis_index("seq")
    return spot // 2, spot % 2


def gather_chips(array):
    chips = chips_of()
    if chips > 4:
        return lax.all_gather(
            array, "seq", axis=0, tiled=True, axis_index_groups=core_groups()
        )
    chip, _ = place()
    rows = array.shape[0]
    whole = jnp.zeros((chips * rows, array.shape[1]), array.dtype)
    for step in range(chips):
        part = array if step == 0 else chip_shift(array, step)
        whole = lax.dynamic_update_slice(whole, part, (((chip - step) % chips) * rows, 0))
    return whole


def gather_weight(array):
    own = lax.all_gather(gather_chips(array), "dp", axis=0, tiled=True)
    return join_cores(own, core_swap(own), 0)


def join_cores(own, other, axis):
    _, core = place()
    return jnp.where(
        core == 0,
        jnp.concatenate([own, other], axis),
        jnp.concatenate([other, own], axis),
    )


def scatter_chips(array):
    chips = chips_of()
    if chips > 4:
        return lax.psum_scatter(
            array, "seq", scatter_dimension=0, tiled=True, axis_index_groups=core_groups()
        ).astype(F32)
    chip, _ = place()
    rows = array.shape[0] // chips
    total = None
    for step in range(chips):
        part = lax.dynamic_slice(
            array, (((chip + step) % chips) * rows, 0), (rows, array.shape[1])
        )
        if step > 0:
            part = chip_shift(part, step)
        total = part.astype(F32) if total is None else total + part.astype(F32)
    return total


def scatter_grad(array):
    part = lax.psum_scatter(array.astype(BF), "dp", scatter_dimension=0, tiled=True)
    return scatter_chips(part)


def half_of(array, index):
    width = array.shape[1] // 2
    return lax.dynamic_slice(array, (0, index * width), (array.shape[0], width))


def swap_matrix(width, block):
    spot = np.arange(width)
    target = ((spot // block) % 2) * (width // 2) + (spot // (2 * block)) * block + spot % block
    rows = lax.broadcasted_iota(jnp.int32, (width, width), 0)
    columns = lax.broadcasted_iota(jnp.int32, (width, width), 1)
    goal = ((rows // block) % 2) * (width // 2) + (rows // (2 * block)) * block + rows % block
    return (goal == columns).astype(BF)


def move(array, matrix):
    return jnp.dot(array, matrix, preferred_element_type=F32).astype(BF)


def move_back(array, matrix):
    return matmul_t(array, matrix).astype(BF)


def attend(queries, key_rows, value_rows):
    count = queries.shape[1] // HEAD
    outs = []
    logs = []
    for head in range(count):
        cut = slice(head * HEAD, (head + 1) * HEAD)
        scores = matmul_t(queries[:, cut], key_rows[:, cut])
        top = jnp.max(scores, -1, keepdims=True)
        log_total = top + jnp.log(jnp.sum(jnp.exp(scores - top), -1, keepdims=True))
        probability = jnp.exp(scores - log_total).astype(BF)
        outs.append(matmul(probability, value_rows[:, cut]))
        logs.append(log_total)
    return jnp.concatenate(outs, 1), jnp.concatenate(logs, 1)


def attend_back(queries, key_rows, value_rows, logs, mixed, grad_mixed):
    count = queries.shape[1] // HEAD
    grad_q, grad_k, grad_v = [], [], []
    for head in range(count):
        cut = slice(head * HEAD, (head + 1) * HEAD)
        grad_head = grad_mixed[:, cut]
        delta = jnp.sum(grad_head.astype(F32) * mixed[:, cut], -1, keepdims=True)
        probability = jnp.exp(
            matmul_t(queries[:, cut], key_rows[:, cut]) - logs[:, head : head + 1]
        )
        grad_prob = matmul_t(grad_head, value_rows[:, cut])
        grad_scores = (probability * (grad_prob - delta)).astype(BF)
        grad_q.append(matmul(grad_scores, key_rows[:, cut]))
        grad_k.append(grad_matmul(grad_scores, queries[:, cut]))
        grad_v.append(grad_matmul(probability.astype(BF), grad_head))
    return (
        jnp.concatenate(grad_q, 1).astype(BF),
        jnp.concatenate(grad_k + grad_v, 1).astype(BF),
    )


def forward_layer(hidden, params, perm):
    triple, mixer, expand, shrink, vectors, head_bias, ffn_bias = params
    rows, width = hidden.shape
    half = width // 2
    _, core = place()
    low = hidden.astype(BF)
    project = matmul(low, triple)
    queries = ((project[:, :width] + head_bias[0]) * 0.125).astype(BF)
    key_rows = project[:, width : 2 * width].astype(BF)
    value_rows = (project[:, 2 * width :] + head_bias[1]).astype(BF)
    trio = (queries, key_rows, value_rows)
    mine = jnp.concatenate([half_of(member, core) for member in trio], 1)
    sent = jnp.concatenate([half_of(member, 1 - core) for member in trio], 1)
    pair = jnp.concatenate([mine, core_swap(sent)], 0)
    pair_queries = pair[:, :half]
    pair_rest = pair[:, half:]
    chips = chips_of()
    if chips > 4:
        keyed = gather_chips(pair_rest)
    else:
        keyed = jnp.concatenate(
            [pair_rest] + [chip_shift(pair_rest, step) for step in range(1, chips)], 0
        )
    mixed, logs = attend(pair_queries, keyed[:, :half], keyed[:, half:])
    mixed_low = mixed.astype(BF)
    other = core_swap(mixed_low[rows:])
    attended = move(join_cores(mixed_low[:rows], other, 1), perm)
    attn_out = matmul(attended, mixer) + vectors[2]
    residual_one = hidden + attn_out
    normed = layer_norm(residual_one, vectors[3], vectors[4])
    normed_low = normed.astype(BF)
    pre_act = matmul(normed_low, expand) + ffn_bias
    act_low = gelu_exact(pre_act).astype(BF)
    ffn_out = matmul(act_low, shrink) + vectors[9]
    residual_two = normed + ffn_out
    output = layer_norm(residual_two, vectors[10], vectors[11])
    squares = jnp.stack(
        [jnp.sum(hidden * hidden), jnp.sum(attn_out * attn_out), jnp.sum(ffn_out * ffn_out)]
    )
    saved = (
        low, pair_queries, keyed, logs, mixed, attended,
        residual_one, normed_low, pre_act, act_low, residual_two,
    )
    return output, saved, squares


def backward_layer(grad_output, params, saved, perm, perm_wide):
    triple, mixer, expand, shrink, vectors, head_bias, ffn_bias = params
    (
        low, pair_queries, keyed, logs, mixed, attended,
        residual_one, normed_low, pre_act, act_low, residual_two,
    ) = saved
    rows, width = low.shape
    half = width // 2
    chips = chips_of()
    _, core = place()
    acts = jnp.concatenate(
        [half_of(member, 1 - core) for member in (low, attended, normed_low, act_low)], 1
    )
    acts = core_swap(acts)
    low_pair = jnp.concatenate([half_of(low, core), acts[:, :half]], 0)
    attended_pair = jnp.concatenate([half_of(attended, core), acts[:, half : 2 * half]], 0)
    normed_pair = jnp.concatenate([half_of(normed_low, core), acts[:, 2 * half : 3 * half]], 0)
    act_pair = jnp.concatenate([half_of(act_low, core), acts[:, 3 * half :]], 0)

    _, pull_two = jax.vjp(layer_norm, residual_two, vectors[10], vectors[11])
    grad_two, grad_gain_two, grad_shift_two = pull_two(grad_output)
    grad_ffn = grad_two.astype(BF)
    grad_act = matmul_t(grad_ffn, shrink)
    _, pull_gelu = jax.vjp(gelu_exact, pre_act)
    grad_pre = pull_gelu(grad_act)[0].astype(BF)
    grad_normed = grad_two + matmul_t(grad_pre, expand)
    _, pull_one = jax.vjp(layer_norm, residual_one, vectors[3], vectors[4])
    grad_one, grad_gain_one, grad_shift_one = pull_one(grad_normed)
    grad_attn = grad_one.astype(BF)
    grad_attended = move_back(matmul_t(grad_attn, mixer).astype(BF), perm)

    grad_ffn_nat = move_back(grad_ffn, perm)
    grad_attn_nat = move_back(grad_attn, perm)
    quarter = grad_pre.reshape(rows, 2, -1, half).transpose(0, 2, 1, 3).reshape(-1, width)
    grad_pre_nat = move_back(quarter, perm_wide).reshape(rows, -1)
    gave = jnp.concatenate([grad_ffn_nat, grad_pre_nat], 1)
    pair_ffn = jnp.concatenate([gave, core_swap(gave)], 0)
    grad_shrink = grad_matmul(act_pair, pair_ffn[:, :width])
    grad_expand = grad_matmul(normed_pair, pair_ffn[:, width:])

    other = core_swap(half_of(grad_attended, 1 - core))
    pair_grad = jnp.concatenate([half_of(grad_attended, core), other], 0)
    grad_q, grad_kv = attend_back(
        pair_queries, keyed[:, :half], keyed[:, half:], logs, mixed, pair_grad
    )
    span = 2 * rows
    if chips > 4:
        grad_kv = scatter_chips(grad_kv)
    else:
        total = grad_kv[:span].astype(F32)
        for step in range(1, chips):
            total = total + chip_shift(
                grad_kv[step * span : (step + 1) * span], -step
            ).astype(F32)
        grad_kv = total
    mine = jnp.concatenate([grad_q * 0.125, grad_kv.astype(BF)], 1)
    theirs = core_swap(mine)
    theirs = jnp.concatenate([theirs[rows:], theirs[:rows]], 0)
    pair_project = jnp.concatenate(
        [
            join_cores(mine[:, i * half : (i + 1) * half], theirs[:, i * half : (i + 1) * half], 1)
            for i in range(3)
        ],
        1,
    )
    grad_hidden = grad_one + matmul_t(pair_project[:rows], triple)
    grad_triple = grad_matmul(low_pair, pair_project)
    attn_pair = jnp.concatenate([grad_attn_nat, core_swap(grad_attn_nat)], 0)
    grad_mixer = grad_matmul(attended_pair, attn_pair)

    def sums(array):
        return jnp.sum(array.astype(F32), 0)

    bias_rows = jnp.concatenate(
        [
            sums(pair_project[:rows, :width])[None],
            sums(pair_project[:rows, 2 * width :])[None],
            sums(grad_pre_nat).reshape(-1, width),
        ],
        0,
    )
    count = width // (2 * lax.axis_size("dp") * chips)
    bias_rows = (
        bias_rows.reshape(bias_rows.shape[0], -1, 2, count)
        .transpose(0, 2, 1, 3)
        .reshape(bias_rows.shape)
    )
    grad_vector = jnp.concatenate(
        [
            bias_rows[:2],
            sums(grad_attn)[None],
            grad_gain_one[None],
            grad_shift_one[None],
            bias_rows[2:],
            sums(grad_ffn)[None],
            grad_gain_two[None],
            grad_shift_two[None],
        ],
        0,
    )
    grad_vector = half_of(grad_vector, core) + core_swap(half_of(grad_vector, 1 - core))
    high = grad_vector.astype(BF)
    rest = (grad_vector - high.astype(F32)).astype(BF)
    extra = jnp.concatenate([high, rest], 0).T
    extra = jnp.pad(extra, ((0, 0), (0, LANES - extra.shape[1])))
    attn_terms = jnp.concatenate([grad_triple.astype(BF), grad_mixer.astype(BF), extra], 1)
    return grad_hidden, attn_terms, grad_expand.astype(BF), grad_shrink.astype(BF)


def total_of(value):
    for axis in ("seq", "dp"):
        size = lax.axis_size(axis)
        step = 1
        while step < size:
            value = value + lax.ppermute(value, axis, [(i, i ^ step) for i in range(size)])
            step *= 2
    return value


def per_device(
    hidden_input,
    triple_weight,
    mixer_weight,
    expand_weight,
    shrink_weight,
    vector_params,
    output_grad,
):
    _, count, width = hidden_input.shape
    share = triple_weight.shape[1]
    wide_share = shrink_weight.shape[1]
    wide = expand_weight.shape[2]
    groups = wide // width
    perm = swap_matrix(width, share)
    perm_wide = swap_matrix(width, wide_share)

    mixer_moved = move(mixer_weight.reshape(-1, width), perm).reshape(mixer_weight.shape)
    shrink_moved = move(shrink_weight.reshape(-1, width), perm).reshape(shrink_weight.shape)
    expand_moved = move(expand_weight.reshape(-1, width), perm_wide)
    expand_moved = (
        expand_moved.reshape(LAYERS * share, groups, 2, width // 2)
        .transpose(0, 2, 1, 3)
        .reshape(expand_weight.shape)
    )
    vector_columns = vector_params.reshape(LAYERS * VECS, share).T
    vector_columns = jnp.pad(vector_columns, ((0, 0), (0, LANES - LAYERS * VECS)))
    packs = []
    for layer in range(LAYERS):
        attn = [triple_weight[layer], mixer_moved[layer]]
        if layer == 0:
            attn.append(vector_columns)
        packs.append(
            (
                gather_weight(jnp.concatenate(attn, 1)),
                gather_weight(expand_moved[layer]),
                gather_weight(shrink_moved[layer]),
            )
        )
    vectors = packs[0][0][:, 4 * width : 4 * width + LAYERS * VECS].T
    natural = move_back(vectors, perm)
    params = []
    for layer in range(LAYERS):
        rows = vectors[layer * VECS : (layer + 1) * VECS].astype(F32)
        plain = natural[layer * VECS : (layer + 1) * VECS]
        ffn_bias = (
            move(plain[5 : 5 + groups], perm_wide)
            .reshape(groups, 2, width // 2)
            .transpose(1, 0, 2)
            .reshape(1, wide)
        ).astype(F32)
        attn, expand, shrink = packs[layer]
        params.append(
            (
                attn[:, : 3 * width],
                attn[:, 3 * width : 4 * width],
                expand,
                shrink,
                rows,
                plain[:2].astype(F32),
                ffn_bias,
            )
        )

    hidden = matmul(hidden_input[0], perm)
    kept = []
    collected = []
    for layer in range(LAYERS):
        hidden, saved, squares = forward_layer(hidden, params[layer], perm)
        kept.append(saved)
        collected.append(squares)
    elements = count * width * lax.axis_size("dp") * lax.axis_size("seq")
    root_squares = jnp.sqrt(total_of(jnp.stack(collected)) / elements)
    hidden_output = move_back(hidden.astype(BF), perm)

    grad = matmul(output_grad[0], perm)
    terms = [None] * LAYERS
    for layer in reversed(range(LAYERS)):
        grad, attn, expand, shrink = backward_layer(
            grad, params[layer], kept[layer], perm, perm_wide
        )
        terms[layer] = (scatter_grad(attn), scatter_grad(expand), scatter_grad(shrink))
    input_grad = move_back(grad.astype(BF), perm)
    vector_grad = jnp.stack(
        [
            (
                terms[layer][0][:, 4 * width : 4 * width + VECS]
                + terms[layer][0][:, 4 * width + VECS : 4 * width + 2 * VECS]
            ).T
            for layer in range(LAYERS)
        ]
    )
    return (
        hidden_output[None],
        input_grad[None],
        jnp.stack([terms[layer][0][:, : 3 * width] for layer in range(LAYERS)]),
        jnp.stack([terms[layer][0][:, 3 * width : 4 * width] for layer in range(LAYERS)]),
        jnp.stack([terms[layer][1] for layer in range(LAYERS)]),
        jnp.stack([terms[layer][2] for layer in range(LAYERS)]),
        vector_grad,
        root_squares,
    )


def solution(mesh):
    return jax.shard_map(
        per_device,
        mesh=mesh,
        in_specs=(
            P("dp", "seq", None),
            P(None, ("dp", "seq"), None),
            P(None, ("dp", "seq"), None),
            P(None, ("dp", "seq"), None),
            P(None, ("dp", "seq"), None),
            P(None, None, ("dp", "seq")),
            P("dp", "seq", None),
        ),
        out_specs=(
            P("dp", "seq", None),
            P("dp", "seq", None),
            P(None, ("dp", "seq"), None),
            P(None, ("dp", "seq"), None),
            P(None, ("dp", "seq"), None),
            P(None, ("dp", "seq"), None),
            P(None, None, ("dp", "seq")),
            P(),
        ),
        check_vma=False,
    )
```

time: 1980 us -> 717 us (0.36)
  waiting for transfers between devices: 1520 us -> 292 us
  blocking collectives: 145 us -> 0 us
  starting transfers between devices: 1.66 us -> 113 us
  other arithmetic: 27.7 us -> 61.8 us
  local copies, waits for them, and re-layouts: 97.6 us -> 69.7 us
    reduce_scatter x6, waiting for transfers between devices: 766 us -> 0.08 us  [scatter_grad(): lax.psum_scatter(array.astype(BF), 'dp', scatter_dimension=0, tiled=True)]
    all_gather x16 -> x6, waiting for transfers between devices: 469 us -> 130 us  [gather_weight(): own = lax.all_gather(gather_chips(array), 'dp', axis=0, tiled=True)]
    unnamed x28 -> x12, waiting for transfers between devices: 290 us -> 0.2 us
    ppermute x0 -> x75, waiting for transfers between devices: none -> 162 us  [the longest x48 153 us: chip_shift(): return lax.ppermute(array, 'seq', pairs)]
    all_gather x6 -> x0, blocking collectives: 145 us -> none  [the longest x2 84.1 us: per_device(): lax.all_gather(vector_params[layer_index].T, ('dp', 'seq'), axis=0, tiled...]
    ppermute x0 -> x75, starting transfers between devices: none -> 112 us  [the longest x48 92.8 us: chip_shift(): return lax.ppermute(array, 'seq', pairs)]
    dot_general x35 -> x113, matrix products: 156 us -> 152 us  [the longest x40 62.3 us: matmul_t(): lax.dot_general(left, right, (((1,), (1,)), ((), ())), preferred_element_...]
  transfers between devices with their start and end apart: 25 -> 87, of which waited for: 20 -> 36; matrix products, arithmetic and copies ran while one was open for 13% -> 32% of each run, Pallas kernels for 0% -> 0%
where the time goes in v1:
time: 717 us; the launch traced here: 707 us
  waiting for transfers between devices  292 us (41%)
  matrix products  152 us (21%)
  starting transfers between devices  113 us (16%)
  local copies, waits for them, and re-layouts  69.7 us (10%)
  other arithmetic  61.8 us (9%)
  between operations  18.7 us (3%)
    ppermute x48, waiting for transfers between devices, chip_shift(): return lax.ppermute(array, 'seq', pairs)  153 us
    all_gather x6, waiting for transfers between devices, gather_weight(): own = lax.all_gather(gather_chips(array), 'dp', axis=0, tiled=True)  130 us
    ppermute x48, starting transfers between devices, chip_shift(): return lax.ppermute(array, 'seq', pairs)  92.8 us
    dot_general x40, matrix products, matmul_t(): lax.dot_general(left, right, (((1,), (1,)), ((), ())), preferred_element_...  62.3 us
    dot_general x34, matrix products, matmul(): return jnp.dot(left, right, preferred_element_type=F32)  51.6 us
    dot_general x32, matrix products, grad_matmul(): lax.dot_general(left, right, (((0,), (0,)), ((), ())), preferred_element_...  33.4 us
    unnamed x485, local copies, waits for them, and re-layouts  19.9 us
    select_n x8, other arithmetic, join_cores(): jnp.where(core == 0, jnp.concatenate([own, other], axis), jnp.concatenate...  14.6 us
  transfers between devices with their start and end apart: 87, of which 36 were waited for; matrix products, arithmetic and copies ran while one was open for 32% of the time, Pallas kernels for 0%

profile of v1, /device:TPU:0, one launch (start us, length us, event | category | flops | bytes accessed | tf_op | source)
XLA Modules:
  0.0 707.1 jit_solution(99975848152131075)
XLA Ops:
  20.3 5.5 collective-permute-done.18
  27.0 3.6 collective-permute-start
  33.1 3.3 collective-permute-done
  36.4 5.2 collective-permute-done.1
  45.3 3.8 collective-permute-start.9
  51.6 4.0 collective-permute-done.9
  55.7 5.1 collective-permute-done.10
  62.2 3.6 collective-permute-start.13
  68.3 3.1 collective-permute-done.13
  71.5 5.2 collective-permute-done.14
  77.7 3.6 collective-permute-start.26
  83.9 3.9 collective-permute-done.26
  87.8 5.2 collective-permute-done.27
  94.1 12.8 %all-gather.7.cloned.1.call-done = bf16[384,3200]{1,0:T(8,128)(2,1)} async-done(((bf16[96,3200]{1,0:T(8,128)(2,1)}), bf16[384,3200]{1,0:T(8,128)(2,1)}) %all-gather.7.cloned.1.call-update) | async-done | bytes 2457616 | tf_op jit(solution)/shard_map/all_gather | solution.py:83
  117.3 4.1 collective-permute-done.31
  122.3 24.5 %all-gather.9.cloned.1.call-done = bf16[384,3072]{1,0:T(8,128)(2,1)} async-done(((bf16[96,3072]{1,0:T(8,128)(2,1)}), bf16[384,3072]{1,0:T(8,128)(2,1)}) %all-gather.9.cloned.1.call-update) | async-done | bytes 2359312 | tf_op jit(solution)/shard_map/all_gather | solution.py:83
  146.8 39.2 %all-gather.11.cloned.1.call-done = bf16[1536,768]{1,0:T(8,128)(2,1)} async-done(((bf16[384,768]{1,0:T(8,128)(2,1)}), bf16[1536,768]{1,0:T(8,128)(2,1)}) %all-gather.11.cloned.1.call-update) | async-done | bytes 2359312 | tf_op jit(solution)/shard_map/all_gather | solution.py:83
  186.0 7.8 %maximum_select_fusion.3 = bf16[768,3072]{1,0:T(8,128)(2,1)} fusion(bf16[384,3072]{1,0:T(8,128)(2,1)} %collective-permute-done.20, bf16[384,3072]{1,0:T(8,128)(2,1)} %all-gather.13.cloned.1.call-done, pred[]{:T(512)S(6)} %eq.131), kind=kLoop, calls=%fused_computation.6 | loop fusion | flops 21233664 | bytes 9437185 | tf_op jit(solution)/shard_map/jit(_where)/select_n | solution.py:89
  193.9 4.9 maximum_select_fusion
  202.1 3.4 collective-permute-start.7
  211.1 14.1 %all-gather.15.cloned.1.call-done = bf16[384,3072]{1,0:T(8,128)(2,1)} async-done(((bf16[96,3072]{1,0:T(8,128)(2,1)}), bf16[384,3072]{1,0:T(8,128)(2,1)}) %all-gather.15.cloned.1.call-update) | async-done | bytes 2359312 | tf_op jit(solution)/shard_map/all_gather | solution.py:83
  225.2 39.2 %all-gather.17.cloned.1.call-done = bf16[1536,768]{1,0:T(8,128)(2,1)} async-done(((bf16[384,768]{1,0:T(8,128)(2,1)}), bf16[1536,768]{1,0:T(8,128)(2,1)}) %all-gather.17.cloned.1.call-update) | async-done | bytes 2359312 | tf_op jit(solution)/shard_map/all_gather | solution.py:83
  283.4 8.1 %multiply_convert_fusion.1 = (bf16[128,3072]{0,1:T(8,128)(2,1)S(1)}, f32[128,3072]{0,1:T(8,128)}, f32[128,3072]{0,1:T(8,128)}) fusion(f32[3072]{0:T(1024)S(1)} %reshape.387, bf16[128,768]{0,1:T(8,128)(2,1)S(1)} %fusion.189, bf16[384,3072]{1,0:T(8,128)(2,1)} %collective-permute-done.12, bf16[384,3072]{1,0:T(8,128)(2,1)S(1)} %copy-done.228, pred[]{:T(512)S(6)} %eq.131), kind=kOutput, calls=%fused_computation.74 | convolution fusion | flops 651165696 | bytes 8859649 | tf_op jit(solution)/shard_map/dot_general | solution.py:30
  291.6 5.4 fusion.423
  300.1 3.4 collective-permute-start.24
  308.1 4.9 collective-permute-done.24
  313.0 24.7 %collective-permute-done.23 = bf16[256,768]{1,0:T(8,128)(2,1)S(1)} collective-permute-done((bf16[256,768]{1,0:T(8,128)(2,1)S(1)}, bf16[256,768]{1,0:T(8,128)(2,1)S(1)}, u32[]{:S(2)}, u32[]{:S(2)}) %collective-permute-start.23) | collective-permute-done | bytes 393248 | tf_op jit(solution)/shard_map/ppermute | solution.py:54
  352.7 7.8 %multiply_convert_fusion = (bf16[128,3072]{0,1:T(8,128)(2,1)S(1)}, f32[128,3072]{0,1:T(8,128)S(1)}, f32[128,3072]{0,1:T(8,128)S(1)}) fusion(f32[3072]{0:T(1024)S(1)} %copy-done.202, bf16[128,768]{0,1:T(8,128)(2,1)S(1)} %fusion.191, bf16[384,3072]{1,0:T(8,128)(2,1)} %collective-permute-done.29, bf16[384,3072]{1,0:T(8,128)(2,1)S(1)} %copy-done.232, pred[]{:T(512)S(6)} %eq.131), kind=kOutput, calls=%fused_computation.61 | convolution fusion | flops 651165696 | bytes 8859649 | tf_op jit(solution)/shard_map/dot_general | solution.py:30
  365.5 5.2 add_convert_fusion.1
  370.7 7.4 %multiply_reduce_fusion.6 = (f32[768]{0:T(1024)}, f32[128]{0:T(128)S(1)}, f32[768]{0:T(1024)}, f32[128,768]{0,1:T(8,128)S(1)}) fusion(f32[128,768]{0,1:T(8,128)S(1)} %get-tuple-element.107, f32[128]{0:T(128)S(1)} %fusion.344, f32[128]{0:T(128)S(1)} %broadcast_multiply_fusion.3, f32[768]{0:T(1024)S(1)} %get-tuple-element.56, ...), kind=kOutput, calls=%fused_computation.384 | convolution fusion | flops 626194816 | bytes 6695937 | tf_op jit(solution)/shard_map/dot_general | solution.py:34
  391.4 3.1 copy.137
  434.9 5.9 collective-permute-done.37
  440.8 16.2 %collective-permute-done.36 = bf16[256,768]{0,1:T(8,128)(2,1)S(1)} collective-permute-done((bf16[256,768]{0,1:T(8,128)(2,1)S(1)}, bf16[256,768]{0,1:T(8,128)(2,1)S(1)}, u32[]{:S(2)}, u32[]{:S(2)}) %collective-permute-start.36) | collective-permute-done | bytes 393248 | tf_op jit(solution)/shard_map/ppermute | solution.py:54
  474.7 4.0 multiply_reduce_fusion.7
  480.2 5.0 add_convert_fusion
  485.3 6.9 multiply_reduce_fusion.8
  495.5 3.2 fusion.11
  502.9 3.3 copy.133
  523.3 8.8 %collective-permute-start.71 = (f32[2,3]{1,0:T(2,128)S(1)}, f32[2,3]{1,0:T(2,128)S(1)}, u32[]{:S(2)}, u32[]{:S(2)}) collective-permute-start(f32[2,3]{1,0:T(2,128)S(1)} %fusion.367), channel_id=1, source_target_pairs={{0,2},{1,3},{2,0},{3,1},{4,6},{5,7},{6,4},{7,5},{8,10},{9,11},{10,... | collective-permute-start | bytes 80 | tf_op jit(solution)/shard_map/ppermute | solution.py:338
  577.3 11.9 %collective-permute-done.41 = bf16[256,768]{0,1:T(8,128)(2,1)} collective-permute-done((bf16[256,768]{0,1:T(8,128)(2,1)}, bf16[256,768]{0,1:T(8,128)(2,1)}, u32[]{:S(2)}, u32[]{:S(2)}) %collective-permute-start.41) | collective-permute-done | bytes 393248 | tf_op jit(solution)/shard_map/ppermute | solution.py:54
  596.8 4.4 fusion.83
  604.4 10.0 %collective-permute-start.63 = (bf16[24,3072]{1,0:T(8,128)(2,1)S(1)}, bf16[24,3072]{1,0:T(8,128)(2,1)S(1)}, u32[]{:S(2)}, u32[]{:S(2)}) collective-permute-start(bf16[24,3072]{1,0:T(8,128)(2,1)S(1)} %get-tuple-element.150), channel_id=1, source_target_pairs={{0,6},{1,7},{2,0},{3,1},{4,2},{5,3},{6,4},{7,5},{8,14},{9,15},{10,... | collective-permute-start | bytes 442376 | tf_op jit(solution)/shard_map/ppermute | solution.py:54
  618.9 3.5 collective-permute-start.69
  626.0 8.9 %collective-permute-done.62 = bf16[24,3072]{1,0:T(8,128)(2,1)S(1)} collective-permute-done((bf16[24,3072]{1,0:T(8,128)(2,1)S(1)}, bf16[24,3072]{1,0:T(8,128)(2,1)S(1)}, u32[]{:S(2)}, u32[]{:S(2)}) %collective-permute-start.62) | collective-permute-done | bytes 147488 | tf_op jit(solution)/shard_map/ppermute | solution.py:54
  643.0 10.7 %collective-permute-done.54 = bf16[24,3200]{1,0:T(8,128)(2,1)S(1)} collective-permute-done((bf16[24,3200]{1,0:T(8,128)(2,1)S(1)}, bf16[24,3200]{1,0:T(8,128)(2,1)S(1)}, u32[]{:S(2)}, u32[]{:S(2)}) %collective-permute-start.54) | collective-permute-done | bytes 153632 | tf_op jit(solution)/shard_map/ppermute | solution.py:54
  663.0 5.0 collective-permute-start.64
  668.0 10.4 %collective-permute-done.58 = bf16[24,3072]{1,0:T(8,128)(2,1)S(1)} collective-permute-done((bf16[24,3072]{1,0:T(8,128)(2,1)S(1)}, bf16[24,3072]{1,0:T(8,128)(2,1)S(1)}, u32[]{:S(2)}, u32[]{:S(2)}) %collective-permute-start.58) | collective-permute-done | bytes 147488 | tf_op jit(solution)/shard_map/ppermute | solution.py:54
  687.0 9.5 %collective-permute-done.48 = bf16[24,3200]{1,0:T(8,128)(2,1)S(1)} collective-permute-done((bf16[24,3200]{1,0:T(8,128)(2,1)S(1)}, bf16[24,3200]{1,0:T(8,128)(2,1)S(1)}, u32[]{:S(2)}, u32[]{:S(2)}) %collective-permute-start.48) | collective-permute-done | bytes 153632 | tf_op jit(solution)/shard_map/ppermute | solution.py:54
  (1011 shorter events, 285.5 us)
Async XLA Ops:
  7.2 86.8 %all-gather.13.cloned.1.call-start = ((), (), s32[]{:S(2)}) async-start(), calls=%async_computation.9 | async-start | bytes 2949120 | tf_op jit(solution)/shard_map/all_gather | solution.py:83
  26.8 80.1 %all-gather.7.cloned.1.call-start = ((), (), s32[]{:S(2)}) async-start(), calls=%async_computation.6 | async-start | bytes 3072000 | tf_op jit(solution)/shard_map/all_gather | solution.py:83
  42.5 104.3 %all-gather.9.cloned.1.call-start = ((), (), s32[]{:S(2)}) async-start(), calls=%async_computation.7 | async-start | bytes 2949120 | tf_op jit(solution)/shard_map/all_gather | solution.py:83
  61.6 124.4 %all-gather.11.cloned.1.call-start = ((), (), s32[]{:S(2)}) async-start(), calls=%async_computation.8 | async-start | bytes 2949120 | tf_op jit(solution)/shard_map/all_gather | solution.py:83
  77.6 147.6 %all-gather.15.cloned.1.call-start = ((), (), s32[]{:S(2)}) async-start(), calls=%async_computation.10 | async-start | bytes 2949120 | tf_op jit(solution)/shard_map/all_gather | solution.py:83
  93.9 170.5 %all-gather.17.cloned.1.call-start = ((), (), s32[]{:S(2)}) async-start(), calls=%async_computation.11 | async-start | bytes 2949120 | tf_op jit(solution)/shard_map/all_gather | solution.py:83
  94.0 92.1 %collective-permute-start.20 = (bf16[384,3072]{1,0:T(8,128)(2,1)}, bf16[384,3072]{1,0:T(8,128)(2,1)}, u32[]{:S(2)}, u32[]{:S(2)}) collective-permute-start(bf16[384,3072]{1,0:T(8,128)(2,1)} %all-gather.13.cloned.1.call-done), channel_id=1, source_target_pairs={{0,1},{1,0},{2,3},{3,2},{4,5},{5,4},{6,7},{7,6},{8,9},{9,8},{10,11... | collective-permute-start | bytes 7077896 | tf_op jit(solution)/shard_map/ppermute | solution.py:47
  106.9 87.0 %collective-permute-start.3 = (bf16[384,3200]{1,0:T(8,128)(2,1)}, bf16[384,3200]{1,0:T(8,128)(2,1)}, u32[]{:S(2)}, u32[]{:S(2)}) collective-permute-start(bf16[384,3200]{1,0:T(8,128)(2,1)} %all-gather.7.cloned.1.call-done), channel_id=1, source_target_pairs={{0,1},{1,0},{2,3},{3,2},{4,5},{5,4},{6,7},{7,6},{8,9},{9,8},{10,11... | collective-permute-start | bytes 7372808 | tf_op jit(solution)/shard_map/ppermute | solution.py:47
  122.3 480.9 %reduce-scatter.13.cloned.1.call-start = ((), (), s32[]{:S(2)}) async-start(), calls=%async_computation.15 | async-start | bytes 2949120 | tf_op jit(solution)/shard_map/reduce_scatter | solution.py:116
  146.8 136.6 %collective-permute-start.12 = (bf16[384,3072]{1,0:T(8,128)(2,1)}, bf16[384,3072]{1,0:T(8,128)(2,1)}, u32[]{:S(2)}, u32[]{:S(2)}) collective-permute-start(bf16[384,3072]{1,0:T(8,128)(2,1)} %all-gather.9.cloned.1.call-done), channel_id=1, source_target_pairs={{0,1},{1,0},{2,3},{3,2},{4,5},{5,4},{6,7},{7,6},{8,9},{9,8},{10,11... | collective-permute-start | bytes 7077896 | tf_op jit(solution)/shard_map/ppermute | solution.py:47
  186.0 105.5 %collective-permute-start.16 = (bf16[1536,768]{1,0:T(8,128)(2,1)}, bf16[1536,768]{1,0:T(8,128)(2,1)}, u32[]{:S(2)}, u32[]{:S(2)}) collective-permute-start(bf16[1536,768]{1,0:T(8,128)(2,1)} %all-gather.11.cloned.1.call-done), channel_id=1, source_target_pairs={{0,1},{1,0},{2,3},{3,2},{4,5},{5,4},{6,7},{7,6},{8,9},{9,8},{10,11... | collective-permute-start | bytes 7077896 | tf_op jit(solution)/shard_map/ppermute | solution.py:47
  202.1 23.2 %collective-permute-start.7 = (bf16[256,768]{1,0:T(8,128)(2,1)S(1)}, bf16[256,768]{1,0:T(8,128)(2,1)S(1)}, u32[]{:S(2)}, u32[]{:S(2)}) collective-permute-start(bf16[256,768]{1,0:T(8,128)(2,1)S(1)} %slice.737), channel_id=1, source_target_pairs={{0,6},{1,7},{2,0},{3,1},{4,2},{5,3},{6,4},{7,5},{8,14},{9,15},{10,... | collective-permute-start | bytes 1179656 | tf_op jit(solution)/shard_map/ppermute | solution.py:54
  205.5 59.0 %collective-permute-start.6 = (bf16[256,768]{1,0:T(8,128)(2,1)S(1)}, bf16[256,768]{1,0:T(8,128)(2,1)}, u32[]{:S(2)}, u32[]{:S(2)}) collective-permute-start(bf16[256,768]{1,0:T(8,128)(2,1)S(1)} %slice.737), channel_id=1, source_target_pairs={{0,4},{1,5},{2,6},{3,7},{4,0},{5,1},{6,2},{7,3},{8,12},{9,13},{10,... | collective-permute-start | bytes 1179656 | tf_op jit(solution)/shard_map/ppermute | solution.py:54
  205.5 59.0 %collective-permute-start.5 = (bf16[256,768]{1,0:T(8,128)(2,1)S(1)}, bf16[256,768]{1,0:T(8,128)(2,1)}, u32[]{:S(2)}, u32[]{:S(2)}) collective-permute-start(bf16[256,768]{1,0:T(8,128)(2,1)S(1)} %slice.737), channel_id=1, source_target_pairs={{0,2},{1,3},{2,4},{3,5},{4,6},{5,7},{6,0},{7,1},{8,10},{9,11},{10,... | collective-permute-start | bytes 1179656 | tf_op jit(solution)/shard_map/ppermute | solution.py:54
  225.2 127.4 %collective-permute-start.29 = (bf16[384,3072]{1,0:T(8,128)(2,1)}, bf16[384,3072]{1,0:T(8,128)(2,1)}, u32[]{:S(2)}, u32[]{:S(2)}) collective-permute-start(bf16[384,3072]{1,0:T(8,128)(2,1)} %all-gather.15.cloned.1.call-done), channel_id=1, source_target_pairs={{0,1},{1,0},{2,3},{3,2},{4,5},{5,4},{6,7},{7,6},{8,9},{9,8},{10,11... | collective-permute-start | bytes 7077896 | tf_op jit(solution)/shard_map/ppermute | solution.py:47
  264.4 96.1 %collective-permute-start.33 = (bf16[1536,768]{1,0:T(8,128)(2,1)}, bf16[1536,768]{1,0:T(8,128)(2,1)S(1)}, u32[]{:S(2)}, u32[]{:S(2)}) collective-permute-start(bf16[1536,768]{1,0:T(8,128)(2,1)} %all-gather.17.cloned.1.call-done), channel_id=1, source_target_pairs={{0,1},{1,0},{2,3},{3,2},{4,5},{5,4},{6,7},{7,6},{8,9},{9,8},{10,11... | collective-permute-start | bytes 7077896 | tf_op jit(solution)/shard_map/ppermute | solution.py:47
  303.5 34.2 %collective-permute-start.23 = (bf16[256,768]{1,0:T(8,128)(2,1)S(1)}, bf16[256,768]{1,0:T(8,128)(2,1)S(1)}, u32[]{:S(2)}, u32[]{:S(2)}) collective-permute-start(bf16[256,768]{1,0:T(8,128)(2,1)S(1)} %slice.771), channel_id=1, source_target_pairs={{0,4},{1,5},{2,6},{3,7},{4,0},{5,1},{6,2},{7,3},{8,12},{9,13},{10,... | collective-permute-start | bytes 1179656 | tf_op jit(solution)/shard_map/ppermute | solution.py:54
  303.5 34.2 %collective-permute-start.22 = (bf16[256,768]{1,0:T(8,128)(2,1)S(1)}, bf16[256,768]{1,0:T(8,128)(2,1)S(1)}, u32[]{:S(2)}, u32[]{:S(2)}) collective-permute-start(bf16[256,768]{1,0:T(8,128)(2,1)S(1)} %slice.771), channel_id=1, source_target_pairs={{0,2},{1,3},{2,4},{3,5},{4,6},{5,7},{6,0},{7,1},{8,10},{9,11},{10,... | collective-permute-start | bytes 1179656 | tf_op jit(solution)/shard_map/ppermute | solution.py:54
  313.0 35.7 %collective-permute-start.44 = (bf16[128,2688]{0,1:T(8,128)(2,1)S(1)}, bf16[128,2688]{0,1:T(8,128)(2,1)S(1)}, u32[]{:S(2)}, u32[]{:S(2)}) collective-permute-start(bf16[128,2688]{0,1:T(8,128)(2,1)S(1)} %pad_maximum_fusion.6), channel_id=1, source_target_pairs={{0,1},{1,0},{2,3},{3,2},{4,5},{5,4},{6,7},{7,6},{8,9},{9,8},{10,11... | collective-permute-start | bytes 2064392 | tf_op jit(solution)/shard_map/ppermute | solution.py:47
  415.9 201.9 %reduce-scatter.17.cloned.1.call-start = ((), (), s32[]{:S(2)}) async-start(), calls=%async_computation.17 | async-start | bytes 2949120 | tf_op jit(solution)/shard_map/reduce_scatter | solution.py:116
  427.7 29.3 %collective-permute-start.36 = (bf16[256,768]{0,1:T(8,128)(2,1)S(1)}, bf16[256,768]{0,1:T(8,128)(2,1)S(1)}, u32[]{:S(2)}, u32[]{:S(2)}) collective-permute-start(bf16[256,768]{0,1:T(8,128)(2,1)S(1)} %get-tuple-element.119), channel_id=1, source_target_pairs={{0,4},{1,5},{2,6},{3,7},{4,0},{5,1},{6,2},{7,3},{8,12},{9,13},{10,... | collective-permute-start | bytes 1179656 | tf_op jit(solution)/shard_map/ppermute | solution.py:54
  429.7 27.3 %collective-permute-start.35 = (bf16[256,768]{0,1:T(8,128)(2,1)S(1)}, bf16[256,768]{0,1:T(8,128)(2,1)S(1)}, u32[]{:S(2)}, u32[]{:S(2)}) collective-permute-start(bf16[256,768]{0,1:T(8,128)(2,1)S(1)} %get-tuple-element.117), channel_id=1, source_target_pairs={{0,6},{1,7},{2,0},{3,1},{4,2},{5,3},{6,4},{7,5},{8,14},{9,15},{10,... | collective-permute-start | bytes 1179656 | tf_op jit(solution)/shard_map/ppermute | solution.py:54
  468.2 167.7 %reduce-scatter.9.cloned.1.call-start = ((), (), s32[]{:S(2)}) async-start(), calls=%async_computation.13 | async-start | bytes 3072000 | tf_op jit(solution)/shard_map/reduce_scatter | solution.py:116
  473.1 22.3 %collective-permute-start.52 = (f32[12,384]{1,0:T(8,128)S(1)}, f32[12,384]{1,0:T(8,128)S(1)}, u32[]{:S(2)}, u32[]{:S(2)}) collective-permute-start(f32[12,384]{1,0:T(8,128)S(1)} %constant_dynamic-slice_fusion.19), channel_id=1, source_target_pairs={{0,1},{1,0},{2,3},{3,2},{4,5},{5,4},{6,7},{7,6},{8,9},{9,8},{10,11... | collective-permute-start | bytes 55304 | tf_op jit(solution)/shard_map/ppermute | solution.py:47
  498.7 156.1 %reduce-scatter.11.cloned.1.call-start = ((), (), s32[]{:S(2)}) async-start(), calls=%async_computation.14 | async-start | bytes 2949120 | tf_op jit(solution)/shard_map/reduce_scatter | solution.py:116
  502.6 41.1 %collective-permute-start.39 = (bf16[128,384]{0,1:T(8,128)(2,1)}, bf16[128,384]{0,1:T(8,128)(2,1)S(1)}, u32[]{:S(2)}, u32[]{:S(2)}) collective-permute-start(bf16[128,384]{0,1:T(8,128)(2,1)} %get-tuple-element.208), channel_id=1, source_target_pairs={{0,1},{1,0},{2,3},{3,2},{4,5},{5,4},{6,7},{7,6},{8,9},{9,8},{10,11... | collective-permute-start | bytes 294920 | tf_op jit(solution)/shard_map/ppermute | solution.py:47
  516.5 75.8 %collective-permute-start.45 = (bf16[128,768]{1,0:T(8,128)(2,1)}, bf16[128,768]{1,0:T(8,128)(2,1)}, u32[]{:S(2)}, u32[]{:S(2)}) collective-permute-start(bf16[128,768]{1,0:T(8,128)(2,1)} %convolution_convert_fusion.15), channel_id=1, source_target_pairs={{0,1},{1,0},{2,3},{3,2},{4,5},{5,4},{6,7},{7,6},{8,9},{9,8},{10,11... | collective-permute-start | bytes 589832 | tf_op jit(solution)/shard_map/ppermute | solution.py:47
  519.7 28.8 %collective-permute-start.56 = (bf16[128,3840]{1,0:T(8,128)(2,1)S(1)}, bf16[128,3840]{1,0:T(8,128)(2,1)S(1)}, u32[]{:S(2)}, u32[]{:S(2)}) collective-permute-start(bf16[128,3840]{1,0:T(8,128)(2,1)S(1)} %pad_maximum_fusion.4), channel_id=1, source_target_pairs={{0,1},{1,0},{2,3},{3,2},{4,5},{5,4},{6,7},{7,6},{8,9},{9,8},{10,11... | collective-permute-start | bytes 2949128 | tf_op jit(solution)/shard_map/ppermute | solution.py:47
  542.3 48.7 %collective-permute-start.74 = (f32[2,3]{1,0:T(2,128)}, f32[2,3]{1,0:T(2,128)}, u32[]{:S(2)}, u32[]{:S(2)}) collective-permute-start(f32[2,3]{1,0:T(2,128)} %add.964), channel_id=1, source_target_pairs={{0,16},{8,24},{16,0},{24,8},{1,17},{9,25},{17,1},{25,9},{2,18},{10... | collective-permute-start | bytes 80 | tf_op jit(solution)/shard_map/ppermute | solution.py:338
  551.8 108.1 %reduce-scatter.15.cloned.1.call-start = ((), (), s32[]{:S(2)}) async-start(), calls=%async_computation.16 | async-start | bytes 2949120 | tf_op jit(solution)/shard_map/reduce_scatter | solution.py:116
  561.9 15.4 %collective-permute-start.42 = (bf16[256,768]{0,1:T(8,128)(2,1)}, bf16[256,768]{0,1:T(8,128)(2,1)}, u32[]{:S(2)}, u32[]{:S(2)}) collective-permute-start(bf16[256,768]{0,1:T(8,128)(2,1)} %get-tuple-element.115), channel_id=1, source_target_pairs={{0,2},{1,3},{2,4},{3,5},{4,6},{5,7},{6,0},{7,1},{8,10},{9,11},{10,... | collective-permute-start | bytes 1179656 | tf_op jit(solution)/shard_map/ppermute | solution.py:54
  564.0 25.3 %collective-permute-start.41 = (bf16[256,768]{0,1:T(8,128)(2,1)}, bf16[256,768]{0,1:T(8,128)(2,1)}, u32[]{:S(2)}, u32[]{:S(2)}) collective-permute-start(bf16[256,768]{0,1:T(8,128)(2,1)} %get-tuple-element.116), channel_id=1, source_target_pairs={{0,4},{1,5},{2,6},{3,7},{4,0},{5,1},{6,2},{7,3},{8,12},{9,13},{10,... | collective-permute-start | bytes 1179656 | tf_op jit(solution)/shard_map/ppermute | solution.py:54
  566.3 23.0 %collective-permute-start.40 = (bf16[256,768]{0,1:T(8,128)(2,1)S(1)}, bf16[256,768]{0,1:T(8,128)(2,1)}, u32[]{:S(2)}, u32[]{:S(2)}) collective-permute-start(bf16[256,768]{0,1:T(8,128)(2,1)S(1)} %get-tuple-element.114), channel_id=1, source_target_pairs={{0,6},{1,7},{2,0},{3,1},{4,2},{5,3},{6,4},{7,5},{8,14},{9,15},{10,... | collective-permute-start | bytes 1179656 | tf_op jit(solution)/shard_map/ppermute | solution.py:54
  574.3 106.0 %reduce-scatter.7.cloned.1.call-start = ((), (), s32[]{:S(2)}) async-start(), calls=%async_computation.12 | async-start | bytes 3072000 | tf_op jit(solution)/shard_map/reduce_scatter | solution.py:116
  604.4 18.9 %collective-permute-start.63 = (bf16[24,3072]{1,0:T(8,128)(2,1)S(1)}, bf16[24,3072]{1,0:T(8,128)(2,1)S(1)}, u32[]{:S(2)}, u32[]{:S(2)}) collective-permute-start(bf16[24,3072]{1,0:T(8,128)(2,1)S(1)} %get-tuple-element.150), channel_id=1, source_target_pairs={{0,6},{1,7},{2,0},{3,1},{4,2},{5,3},{6,4},{7,5},{8,14},{9,15},{10,... | collective-permute-start | bytes 442376 | tf_op jit(solution)/shard_map/ppermute | solution.py:54
  614.4 20.5 %collective-permute-start.62 = (bf16[24,3072]{1,0:T(8,128)(2,1)S(1)}, bf16[24,3072]{1,0:T(8,128)(2,1)S(1)}, u32[]{:S(2)}, u32[]{:S(2)}) collective-permute-start(bf16[24,3072]{1,0:T(8,128)(2,1)S(1)} %get-tuple-element.151), channel_id=1, source_target_pairs={{0,4},{1,5},{2,6},{3,7},{4,0},{5,1},{6,2},{7,3},{8,12},{9,13},{10,... | collective-permute-start | bytes 442376 | tf_op jit(solution)/shard_map/ppermute | solution.py:54
  614.7 20.2 %collective-permute-start.61 = (bf16[24,3072]{1,0:T(8,128)(2,1)S(1)}, bf16[24,3072]{1,0:T(8,128)(2,1)S(1)}, u32[]{:S(2)}, u32[]{:S(2)}) collective-permute-start(bf16[24,3072]{1,0:T(8,128)(2,1)S(1)} %get-tuple-element.149), channel_id=1, source_target_pairs={{0,2},{1,3},{2,4},{3,5},{4,6},{5,7},{6,0},{7,1},{8,10},{9,11},{10,... | collective-permute-start | bytes 442376 | tf_op jit(solution)/shard_map/ppermute | solution.py:54
  618.9 21.2 %collective-permute-start.69 = (bf16[96,768]{1,0:T(8,128)(2,1)S(1)}, bf16[96,768]{1,0:T(8,128)(2,1)S(1)}, u32[]{:S(2)}, u32[]{:S(2)}) collective-permute-start(bf16[96,768]{1,0:T(8,128)(2,1)S(1)} %get-tuple-element.144), channel_id=1, source_target_pairs={{0,6},{1,7},{2,0},{3,1},{4,2},{5,3},{6,4},{7,5},{8,14},{9,15},{10,... | collective-permute-start | bytes 442376 | tf_op jit(solution)/shard_map/ppermute | solution.py:54
  622.4 19.6 %collective-permute-start.68 = (bf16[96,768]{1,0:T(8,128)(2,1)S(1)}, bf16[96,768]{1,0:T(8,128)(2,1)S(1)}, u32[]{:S(2)}, u32[]{:S(2)}) collective-permute-start(bf16[96,768]{1,0:T(8,128)(2,1)S(1)} %get-tuple-element.145), channel_id=1, source_target_pairs={{0,4},{1,5},{2,6},{3,7},{4,0},{5,1},{6,2},{7,3},{8,12},{9,13},{10,... | collective-permute-start | bytes 442376 | tf_op jit(solution)/shard_map/ppermute | solution.py:54
  623.3 18.8 %collective-permute-start.67 = (bf16[96,768]{1,0:T(8,128)(2,1)S(1)}, bf16[96,768]{1,0:T(8,128)(2,1)S(1)}, u32[]{:S(2)}, u32[]{:S(2)}) collective-permute-start(bf16[96,768]{1,0:T(8,128)(2,1)S(1)} %get-tuple-element.143), channel_id=1, source_target_pairs={{0,2},{1,3},{2,4},{3,5},{4,6},{5,7},{6,0},{7,1},{8,10},{9,11},{10,... | collective-permute-start | bytes 442376 | tf_op jit(solution)/shard_map/ppermute | solution.py:54
  637.1 16.7 %collective-permute-start.54 = (bf16[24,3200]{1,0:T(8,128)(2,1)S(1)}, bf16[24,3200]{1,0:T(8,128)(2,1)S(1)}, u32[]{:S(2)}, u32[]{:S(2)}) collective-permute-start(bf16[24,3200]{1,0:T(8,128)(2,1)S(1)} %get-tuple-element.139), channel_id=1, source_target_pairs={{0,4},{1,5},{2,6},{3,7},{4,0},{5,1},{6,2},{7,3},{8,12},{9,13},{10,... | collective-permute-start | bytes 460808 | tf_op jit(solution)/shard_map/ppermute | solution.py:54
  656.3 22.0 %collective-permute-start.58 = (bf16[24,3072]{1,0:T(8,128)(2,1)S(1)}, bf16[24,3072]{1,0:T(8,128)(2,1)S(1)}, u32[]{:S(2)}, u32[]{:S(2)}) collective-permute-start(bf16[24,3072]{1,0:T(8,128)(2,1)S(1)} %get-tuple-element.148), channel_id=1, source_target_pairs={{0,4},{1,5},{2,6},{3,7},{4,0},{5,1},{6,2},{7,3},{8,12},{9,13},{10,... | collective-permute-start | bytes 442376 | tf_op jit(solution)/shard_map/ppermute | solution.py:54
  657.9 20.5 %collective-permute-start.57 = (bf16[24,3072]{1,0:T(8,128)(2,1)S(1)}, bf16[24,3072]{1,0:T(8,128)(2,1)S(1)}, u32[]{:S(2)}, u32[]{:S(2)}) collective-permute-start(bf16[24,3072]{1,0:T(8,128)(2,1)S(1)} %get-tuple-element.146), channel_id=1, source_target_pairs={{0,2},{1,3},{2,4},{3,5},{4,6},{5,7},{6,0},{7,1},{8,10},{9,11},{10,... | collective-permute-start | bytes 442376 | tf_op jit(solution)/shard_map/ppermute | solution.py:54
  661.0 20.4 %collective-permute-start.66 = (bf16[96,768]{1,0:T(8,128)(2,1)S(1)}, bf16[96,768]{1,0:T(8,128)(2,1)S(1)}, u32[]{:S(2)}, u32[]{:S(2)}) collective-permute-start(bf16[96,768]{1,0:T(8,128)(2,1)S(1)} %get-tuple-element.141), channel_id=1, source_target_pairs={{0,6},{1,7},{2,0},{3,1},{4,2},{5,3},{6,4},{7,5},{8,14},{9,15},{10,... | collective-permute-start | bytes 442376 | tf_op jit(solution)/shard_map/ppermute | solution.py:54
  663.0 21.7 %collective-permute-start.65 = (bf16[96,768]{1,0:T(8,128)(2,1)S(1)}, bf16[96,768]{1,0:T(8,128)(2,1)S(1)}, u32[]{:S(2)}, u32[]{:S(2)}) collective-permute-start(bf16[96,768]{1,0:T(8,128)(2,1)S(1)} %get-tuple-element.142), channel_id=1, source_target_pairs={{0,4},{1,5},{2,6},{3,7},{4,0},{5,1},{6,2},{7,3},{8,12},{9,13},{10,... | collective-permute-start | bytes 442376 | tf_op jit(solution)/shard_map/ppermute | solution.py:54
  663.0 21.7 %collective-permute-start.64 = (bf16[96,768]{1,0:T(8,128)(2,1)S(1)}, bf16[96,768]{1,0:T(8,128)(2,1)S(1)}, u32[]{:S(2)}, u32[]{:S(2)}) collective-permute-start(bf16[96,768]{1,0:T(8,128)(2,1)S(1)} %get-tuple-element.140), channel_id=1, source_target_pairs={{0,2},{1,3},{2,4},{3,5},{4,6},{5,7},{6,0},{7,1},{8,10},{9,11},{10,... | collective-permute-start | bytes 442376 | tf_op jit(solution)/shard_map/ppermute | solution.py:54
  681.4 15.2 %collective-permute-start.48 = (bf16[24,3200]{1,0:T(8,128)(2,1)S(1)}, bf16[24,3200]{1,0:T(8,128)(2,1)S(1)}, u32[]{:S(2)}, u32[]{:S(2)}) collective-permute-start(bf16[24,3200]{1,0:T(8,128)(2,1)S(1)} %get-tuple-element.136), channel_id=1, source_target_pairs={{0,4},{1,5},{2,6},{3,7},{4,0},{5,1},{6,2},{7,3},{8,12},{9,13},{10,... | collective-permute-start | bytes 460808 | tf_op jit(solution)/shard_map/ppermute | solution.py:54
  681.5 15.1 %collective-permute-start.47 = (bf16[24,3200]{1,0:T(8,128)(2,1)S(1)}, bf16[24,3200]{1,0:T(8,128)(2,1)S(1)}, u32[]{:S(2)}, u32[]{:S(2)}) collective-permute-start(bf16[24,3200]{1,0:T(8,128)(2,1)S(1)} %get-tuple-element.134), channel_id=1, source_target_pairs={{0,2},{1,3},{2,4},{3,5},{4,6},{5,7},{6,0},{7,1},{8,10},{9,11},{10,... | collective-permute-start | bytes 460808 | tf_op jit(solution)/shard_map/ppermute | solution.py:54
  (281 other events, 2754.9 us)
Sparse Core Ops, SparseCore 0:
  26.9 39.8 all-gather.12
  68.6 38.2 all-gather.6
  109.3 37.4 all-gather.8
  148.5 37.4 all-gather.10
  187.7 37.4 all-gather.14
  226.9 37.4 all-gather.16
  416.0 36.7 reduce-scatter.12
  468.4 44.2 reduce-scatter.16
  515.7 38.2 reduce-scatter.8
  556.9 37.3 reduce-scatter.10
  597.4 37.3 reduce-scatter.14
  637.8 38.1 reduce-scatter.6

commit v2 on v1

--- a/solution.py
+++ b/solution.py
@@ -1,7 +1,12 @@
+import functools
+import math
+
 import jax
 import jax.numpy as jnp
 import numpy as np
 from jax import lax
+from jax.experimental import pallas as pl
+from jax.experimental.pallas import tpu as pltpu
 from jax.sharding import PartitionSpec as P
 
 HEADS = 12
@@ -11,6 +16,8 @@
 LANES = 128
 
 EPSILON = 1e-12
+ROOT_HALF = 2.0 ** -0.5
+ROOT_TAU = (2.0 * math.pi) ** -0.5
 
 BF = jnp.bfloat16
 F32 = jnp.float32
@@ -122,13 +129,15 @@
     return lax.dynamic_slice(array, (0, index * width), (array.shape[0], width))
 
 
+def one_hot(goal):
+    return jnp.asarray(np.asarray(goal[:, None] == np.arange(goal.size)[None], np.float32), BF)
+
+
 def swap_matrix(width, block):
     spot = np.arange(width)
-    target = ((spot // block) % 2) * (width // 2) + (spot // (2 * block)) * block + spot % block
-    rows = lax.broadcasted_iota(jnp.int32, (width, width), 0)
-    columns = lax.broadcasted_iota(jnp.int32, (width, width), 1)
-    goal = ((rows // block) % 2) * (width // 2) + (rows // (2 * block)) * block + rows % block
-    return (goal == columns).astype(BF)
+    return one_hot(
+        ((spot // block) % 2) * (width // 2) + (spot // (2 * block)) * block + spot % block
+    )
 
 
 def move(array, matrix):
@@ -340,7 +349,7 @@
     return value
 
 
-def per_device(
+def plain_device(
     hidden_input,
     triple_weight,
     mixer_weight,
@@ -444,6 +453,1149 @@
     )
 
 
+ANY = pl.BlockSpec(memory_space=pl.ANY)
+VMEM = pl.BlockSpec(memory_space=pltpu.VMEM)
+VMEM_BYTES = 56 * 1024 * 1024
+HINT = 4
+SIDE_HINT = 40
+SIDE = ("feed_terms", "attend_terms", "fold", "split", "input_back")
+
+
+def shape(dims, kind):
+    return jax.ShapeDtypeStruct(dims, kind)
+
+
+def run(kernel, name, outs, placed, streamed=(), scratch=(), flops=0):
+    hint = SIDE_HINT if name in SIDE else HINT
+    size = sum(
+        math.prod(member.shape) * member.dtype.itemsize
+        for member in [*outs, *placed, *streamed]
+    )
+    return pl.pallas_call(
+        kernel,
+        name=name,
+        out_shape=list(outs),
+        in_specs=[VMEM] * len(placed) + [ANY] * len(streamed),
+        out_specs=[VMEM] * len(outs),
+        scratch_shapes=list(scratch),
+        compiler_params=pltpu.CompilerParams(vmem_limit_bytes=VMEM_BYTES),
+        cost_estimate=pl.CostEstimate(
+            flops=int(flops * hint), bytes_accessed=int(size * hint), transcendentals=0
+        ),
+    )(*placed, *streamed)
+
+
+def spot_in():
+    index = lax.axis_index("seq")
+    return index // 2, index % 2
+
+
+def fetch_left(pieces, target, sems, columns, goal):
+    _, core = spot_in()
+    _, high = dp_place()
+    rows = pieces[0].shape[0]
+    copies = []
+    for index, piece in enumerate(pieces):
+        part = core if index < 2 else 1 - core
+        side = high if index % 2 == 0 else 1 - high
+        start = pl.multiple_of((part * 2 + side) * rows, 16)
+        copy = pltpu.make_async_copy(
+            piece.at[:, columns], target.at[pl.ds(start, rows), goal], sems.at[index]
+        )
+        copy.start()
+        copies.append(copy)
+    return copies
+
+
+def fetch_whole(pieces, target, sems, columns, goal):
+    _, core = spot_in()
+    rows = pieces[0].shape[0]
+    copies = []
+    for index, piece in enumerate(pieces):
+        part = core if index == 0 else 1 - core
+        start = pl.multiple_of(part * rows, 16)
+        copy = pltpu.make_async_copy(
+            piece.at[:, columns], target.at[pl.ds(start, rows), goal], sems.at[index]
+        )
+        copy.start()
+        copies.append(copy)
+    return copies
+
+
+def fetch_right(pieces, target, sems, columns, goal):
+    _, core = spot_in()
+    bit, _ = dp_place()
+    rows = pieces[0].shape[0] // 2
+    copies = []
+    for index, piece in enumerate(pieces):
+        part = core if index < 2 else 1 - core
+        side = bit if index % 2 == 0 else 1 - bit
+        for row in range(2):
+            start = pl.multiple_of((part * 4 + row * 2 + side) * rows, 16)
+            copy = pltpu.make_async_copy(
+                piece.at[row * rows : (row + 1) * rows, columns],
+                target.at[pl.ds(start, rows), goal],
+                sems.at[2 * index + row],
+            )
+            copy.start()
+            copies.append(copy)
+    return copies
+
+
+def wait_all(copies):
+    for copy in copies:
+        copy.wait()
+
+
+def half_at(ref, part):
+    half = ref.shape[1] // 2
+    return ref[:, pl.ds(pl.multiple_of(part * half, LANES), half)]
+
+
+def column_sum(values):
+    return jnp.sum(values, 0, keepdims=True)
+
+
+def fetch_project(pieces, weight, left_sems, right_sems, width):
+    first, last = slice(0, 2 * width), slice(2 * width, 3 * width)
+    copies = fetch_left(pieces[:4], weight, left_sems, first, first)
+    return copies + fetch_right(pieces[4:], weight, right_sems, slice(0, width), last)
+
+
+def project_kernel(first, chips, source, perm, bias, *rest):
+    pieces, low_out, rest = rest[:8], rest[8], rest[9:]
+    outs, (weight, stage, left_sems, right_sems) = rest[:chips], rest[chips:]
+    chip, _ = spot_in()
+    width = perm.shape[0]
+    copies = fetch_project(pieces, weight, left_sems, right_sems, width)
+    if first:
+        low = matmul(source[...], perm[...]).astype(BF)
+    else:
+        low = source[...].astype(BF)
+    low_out[...] = low
+    wait_all(copies)
+    group = width // chips
+    for section in range(3):
+        part = matmul(low, weight[:, section * width : (section + 1) * width])
+        if section == 0:
+            part = (part + bias[0:1]) * 0.125
+        if section == 2:
+            part = part + bias[1:2]
+        part = part.astype(BF)
+        for index in range(chips):
+            stage[index, :, section * group : (section + 1) * group] = part[
+                :, index * group : (index + 1) * group
+            ]
+    for step in range(chips):
+        outs[step][...] = stage[lax.rem(chip + step, chips)]
+
+
+def project_fast(first, chips, source, perm, bias, pieces):
+    rows, width = source.shape
+    group = 3 * width // chips
+    out = run(
+        functools.partial(project_kernel, first, chips),
+        "project",
+        [shape((rows, width), BF)] + [shape((rows, group), BF)] * chips,
+        [source, perm, bias],
+        pieces,
+        [
+            pltpu.VMEM((width, 3 * width), BF),
+            pltpu.VMEM((chips, rows, group), BF),
+            pltpu.SemaphoreType.DMA((4,)),
+            pltpu.SemaphoreType.DMA((8,)),
+        ],
+        flops=6 * rows * width * width,
+    )
+    return out[0], out[1:]
+
+
+def fill_heads(blocks, others, group, queries, keys, values):
+    rows = blocks[0].shape[0]
+    for index, block in enumerate(blocks):
+        cut = slice(index * rows, (index + 1) * rows)
+        queries[cut, :] = block[:, :group]
+        keys[cut, :] = block[:, group : 2 * group]
+        values[cut, :] = block[:, 2 * group :]
+    base = len(blocks) * rows
+    for index, block in enumerate(others):
+        cut = slice(base + index * rows, base + (index + 1) * rows)
+        keys[cut, :] = block[:, group : 2 * group]
+        values[cut, :] = block[:, 2 * group :]
+
+
+def chunks_of(total):
+    size = min(total, 256)
+    return [slice(start, start + size) for start in range(0, total, size)]
+
+
+def attend_kernel(chips, *refs):
+    blocks, others = refs[:chips], refs[chips : 2 * chips]
+    mixed, logs = refs[2 * chips : 2 * chips + 2]
+    outs = refs[2 * chips + 2 : 3 * chips + 2]
+    queries, keys, values = refs[3 * chips + 2 :]
+    rows = blocks[0].shape[0]
+    group = queries.shape[1]
+    fill_heads(blocks, others, group, queries, keys, values)
+    for head in range(group // HEAD):
+        cut = slice(head * HEAD, (head + 1) * HEAD)
+        key_head = keys[:, cut]
+        value_head = values[:, cut]
+        for part in chunks_of(chips * rows):
+            scores = matmul_t(queries[part, cut], key_head)
+            top = jnp.max(scores, -1, keepdims=True)
+            power = jnp.exp(scores - top)
+            total = jnp.sum(power, -1, keepdims=True)
+            mixed[part, cut] = matmul(power.astype(BF), value_head) * (1.0 / total)
+            logs[part, head : head + 1] = top + jnp.log(total)
+    for index in range(chips):
+        outs[index][...] = mixed[index * rows : (index + 1) * rows, :].astype(BF)
+
+
+def attend_fast(chips, blocks, others):
+    rows, wide = blocks[0].shape
+    group = wide // 3
+    span = chips * rows
+    out = run(
+        functools.partial(attend_kernel, chips),
+        "attend",
+        [shape((span, group), F32), shape((span, LANES), F32)]
+        + [shape((rows, group), BF)] * chips,
+        [*blocks, *others],
+        (),
+        [
+            pltpu.VMEM((span, group), BF),
+            pltpu.VMEM((2 * span, group), BF),
+            pltpu.VMEM((2 * span, group), BF),
+        ],
+        flops=8 * span * span * group,
+    )
+    return out[0], out[1], out[2:]
+
+
+def norm_in(residual):
+    center = residual - jnp.mean(residual, -1, keepdims=True)
+    spread = jnp.mean(center * center, -1, keepdims=True)
+    scale = lax.rsqrt(spread + EPSILON)
+    return center * scale, scale
+
+
+def shrink_cut(index, wide, width):
+    count = wide // width
+    core, block = index // count, index % count
+    half = width // 2
+    return (
+        slice(core * half, (core + 1) * half),
+        slice(block * width, (block + 1) * width),
+    )
+
+
+def fetch_feed(weights, mixer, expand, shrink, sems):
+    width, wide = expand.shape
+    every, full = slice(0, width), slice(0, wide)
+    mixer_copies = fetch_right(weights[:4], mixer, sems[0], slice(width, 2 * width), every)
+    if len(weights) == 6:
+        return (
+            mixer_copies,
+            fetch_whole(weights[4:], expand, sems[1], full, full),
+            fetch_whole(weights[4:], shrink, sems[2], slice(wide, 2 * wide), full),
+        )
+    return (
+        mixer_copies,
+        fetch_left(weights[4:8], expand, sems[1], full, full),
+        fetch_right(weights[8:], shrink, sems[2], full, full),
+    )
+
+
+def feed_kernel(chips, many, hidden, low, perm, rows_in, wide_bias, *refs):
+    pieces, refs = refs[:chips], refs[chips:]
+    weights, refs = refs[:many], refs[many:]
+    (out, attended, normed_low, pre_out, act_out, hat_one, scale_one, hat_two, scale_two,
+     sent, squares) = refs[:11]
+    stage, mixer, expand, shrink, *sems = refs[11:]
+    chip, core = spot_in()
+    width = perm.shape[0]
+    wide = expand.shape[1]
+    group = width // chips
+    mixer_copies, expand_copies, shrink_copies = fetch_feed(
+        weights, mixer, expand, shrink, sems
+    )
+    for step in range(chips):
+        stage[lax.rem(chip + step, chips)] = pieces[step][...]
+    moved = matmul(stage[0], perm[:group, :])
+    for index in range(1, chips):
+        moved += matmul(stage[index], perm[index * group : (index + 1) * group, :])
+    moved = moved.astype(BF)
+    attended[...] = moved
+    wait_all(mixer_copies)
+    attn_out = matmul(moved, mixer[...]) + rows_in[2:3]
+    start = hidden[...].astype(F32)
+    hat, scale = norm_in(start + attn_out)
+    hat_one[...] = hat
+    scale_one[...] = jnp.broadcast_to(scale, scale_one.shape)
+    normed = hat * rows_in[3:4] + rows_in[4:5]
+    normed_b = normed.astype(BF)
+    normed_low[...] = normed_b
+    squares[...] = jnp.zeros_like(squares)
+    squares[0:1, :] = column_sum(start * start)
+    squares[1:2, :] = column_sum(attn_out * attn_out)
+    wait_all(expand_copies)
+    wait_all(shrink_copies)
+    half = width // 2
+    total = None
+    for index in range(wide // width):
+        cut = slice(index * width, (index + 1) * width)
+        pre = matmul(normed_b, expand[:, cut]) + wide_bias[:, cut]
+        pre_out[:, cut] = pre
+        act = (0.5 * pre * (1.0 + lax.erf(pre * ROOT_HALF))).astype(BF)
+        act_out[:, cut] = act
+        for side in range(2):
+            rows, columns = shrink_cut(2 * index + side, wide, width)
+            term = matmul(act[:, side * half : (side + 1) * half], shrink[rows, columns])
+            total = term if total is None else total + term
+    ffn_out = total + rows_in[9:10]
+    squares[2:3, :] = column_sum(ffn_out * ffn_out)
+    hat, scale = norm_in(normed + ffn_out)
+    hat_two[...] = hat
+    scale_two[...] = jnp.broadcast_to(scale, scale_two.shape)
+    out[...] = hat * rows_in[10:11] + rows_in[11:12]
+    for index, member in enumerate((low, attended, normed_low)):
+        sent[:, index * half : (index + 1) * half] = half_at(member, 1 - core)
+    sent[:, 3 * half :] = half_at(act_out, 1 - core)
+
+
+def feed_fast(chips, hidden, low, perm, vectors, wide_bias, pieces, weights):
+    rows, width = hidden.shape
+    wide = wide_bias.shape[1]
+    return run(
+        functools.partial(feed_kernel, chips, len(weights)),
+        "feed",
+        [
+            shape((rows, width), F32),
+            shape((rows, width), BF),
+            shape((rows, width), BF),
+            shape((rows, wide), F32),
+            shape((rows, wide), BF),
+            shape((rows, width), F32),
+            shape((rows, LANES), F32),
+            shape((rows, width), F32),
+            shape((rows, LANES), F32),
+            shape((rows, (3 * width + wide) // 2), BF),
+            shape((8, width), F32),
+        ],
+        [hidden, low, perm, vectors, wide_bias, *pieces],
+        weights,
+        [
+            pltpu.VMEM((chips, rows, width // chips), BF),
+            pltpu.VMEM((width, width), BF),
+            pltpu.VMEM((width, wide), BF),
+            pltpu.VMEM((width, wide), BF),
+            pltpu.SemaphoreType.DMA((8,)),
+            pltpu.SemaphoreType.DMA((4,)),
+            pltpu.SemaphoreType.DMA((8,)),
+        ],
+        flops=4 * rows * width * (wide + width),
+    )
+
+
+def norm_back(grad, hat, scale):
+    first = jnp.mean(grad, -1, keepdims=True)
+    second = jnp.mean(grad * hat, -1, keepdims=True)
+    return (grad - first - hat * second) * scale
+
+
+def feed_back_kernel(
+    first, chips, many, source, perm, perm_wide, vectors, hat_one, scale_one, hat_two, scale_two,
+    pre_in, *refs
+):
+    weights, refs = refs[:many], refs[many:]
+    grad_one_out, gave, attn_nat, sums = refs[:4]
+    outs = refs[4 : 4 + chips]
+    stage, grad_pre, mixer, expand, shrink, *sems = refs[4 + chips :]
+    chip, _ = spot_in()
+    width = perm.shape[0]
+    wide = expand.shape[1]
+    group = width // chips
+    half = width // 2
+    mixer_copies, expand_copies, shrink_copies = fetch_feed(
+        weights, mixer, expand, shrink, sems
+    )
+    grad = matmul(source[...], perm[...]) if first else source[...]
+    hat = hat_two[...]
+    sums[...] = jnp.zeros_like(sums)
+    sums[10:11, :] = column_sum(grad * hat)
+    sums[11:12, :] = column_sum(grad)
+    grad_two = norm_back(grad * vectors[10:11], hat, scale_two[:, 0:1])
+    grad_ffn = grad_two.astype(BF)
+    sums[9:10, :] = column_sum(grad_ffn.astype(F32))
+    gave[:, :width] = matmul_t(grad_ffn, perm[...]).astype(BF)
+    wait_all(shrink_copies)
+    wait_all(expand_copies)
+    grad_normed = grad_two
+    for index in range(wide // width):
+        cut = slice(index * width, (index + 1) * width)
+        pre = pre_in[:, cut]
+        slope = 0.5 * (1.0 + lax.erf(pre * ROOT_HALF)) + pre * (
+            jnp.exp(-0.5 * pre * pre) * ROOT_TAU
+        )
+        sides = []
+        for side in range(2):
+            rows, columns = shrink_cut(2 * index + side, wide, width)
+            sides.append(matmul_t(grad_ffn, shrink[rows, columns]))
+        part = (jnp.concatenate(sides, 1) * slope).astype(BF)
+        grad_pre[:, cut] = part
+        grad_normed += matmul_t(part, expand[:, cut])
+    groups = wide // width
+    piece = half // groups
+    for index in range(groups):
+        joined = jnp.concatenate(
+            [
+                grad_pre[:, spot * half + index * piece : spot * half + (index + 1) * piece]
+                for spot in range(2 * groups)
+            ],
+            1,
+        )
+        moved = matmul_t(joined, perm_wide[...])
+        sums[5 + index : 6 + index, :] = column_sum(moved)
+        gave[:, (index + 1) * width : (index + 2) * width] = moved.astype(BF)
+    hat = hat_one[...]
+    sums[3:4, :] = column_sum(grad_normed * hat)
+    sums[4:5, :] = column_sum(grad_normed)
+    grad_one = norm_back(grad_normed * vectors[3:4], hat, scale_one[:, 0:1])
+    grad_one_out[...] = grad_one
+    grad_attn = grad_one.astype(BF)
+    sums[2:3, :] = column_sum(grad_attn.astype(F32))
+    attn_nat[...] = matmul_t(grad_attn, perm[...]).astype(BF)
+    wait_all(mixer_copies)
+    grad_mixed = matmul_t(grad_attn, mixer[...]).astype(BF)
+    for index in range(chips):
+        stage[index] = matmul_t(
+            grad_mixed, perm[index * group : (index + 1) * group, :]
+        ).astype(BF)
+    for step in range(chips):
+        outs[step][...] = stage[lax.rem(chip + step, chips)]
+
+
+def feed_back_fast(first, chips, source, perm, perm_wide, vectors, saved, weights):
+    rows, width = source.shape
+    wide = saved[-1].shape[1]
+    out = run(
+        functools.partial(feed_back_kernel, first, chips, len(weights)),
+        "feed_back",
+        [
+            shape((rows, width), F32),
+            shape((rows, width + wide), BF),
+            shape((rows, width), BF),
+            shape((16, width), F32),
+        ]
+        + [shape((rows, width // chips), BF)] * chips,
+        [source, perm, perm_wide, vectors, *saved],
+        weights,
+        [
+            pltpu.VMEM((chips, rows, width // chips), BF),
+            pltpu.VMEM((rows, wide), BF),
+            pltpu.VMEM((width, width), BF),
+            pltpu.VMEM((width, wide), BF),
+            pltpu.VMEM((width, wide), BF),
+            pltpu.SemaphoreType.DMA((8,)),
+            pltpu.SemaphoreType.DMA((4,)),
+            pltpu.SemaphoreType.DMA((8,)),
+        ],
+        flops=4 * rows * width * (wide + 2 * width),
+    )
+    return out[0], out[1], out[2], out[3], out[4:]
+
+
+def attend_back_kernel(chips, *refs):
+    blocks, refs = refs[:chips], refs[chips:]
+    others, refs = refs[:chips], refs[chips:]
+    grads, refs = refs[:chips], refs[chips:]
+    mixed, logs, grad_q, near, far, queries, keys, values, grad_in, key_sum, value_sum = refs
+    rows = blocks[0].shape[0]
+    group = queries.shape[1]
+    span = chips * rows
+    fill_heads(blocks, others, group, queries, keys, values)
+    for index in range(chips):
+        grad_in[index * rows : (index + 1) * rows, :] = grads[index][...]
+    for head in range(group // HEAD):
+        cut = slice(head * HEAD, (head + 1) * HEAD)
+        key_head = keys[:, cut]
+        value_head = values[:, cut]
+        for place_in, part in enumerate(chunks_of(span)):
+            query = queries[part, cut]
+            grad = grad_in[part, cut]
+            delta = jnp.sum(grad.astype(F32) * mixed[part, cut], -1, keepdims=True)
+            probability = jnp.exp(matmul_t(query, key_head) - logs[part, head : head + 1])
+            slope = matmul_t(grad, value_head) - delta
+            grad_scores = (probability * slope).astype(BF)
+            grad_q[part, cut] = (matmul(grad_scores, key_head) * 0.125).astype(BF)
+            key_term = grad_matmul(grad_scores, query)
+            value_term = grad_matmul(probability.astype(BF), grad)
+            if place_in == 0:
+                key_sum[:, cut] = key_term
+                value_sum[:, cut] = value_term
+            else:
+                key_sum[:, cut] += key_term
+                value_sum[:, cut] += value_term
+    near[:, :group] = key_sum[:span, :]
+    near[:, group:] = value_sum[:span, :]
+    far[:, :group] = key_sum[span:, :].astype(BF)
+    far[:, group:] = value_sum[span:, :].astype(BF)
+
+
+def attend_back_fast(chips, blocks, others, grads, mixed, logs):
+    rows, wide = blocks[0].shape
+    group = wide // 3
+    span = chips * rows
+    return run(
+        functools.partial(attend_back_kernel, chips),
+        "attend_back",
+        [
+            shape((span, group), BF),
+            shape((span, 2 * group), F32),
+            shape((span, 2 * group), BF),
+        ],
+        [*blocks, *others, *grads, mixed, logs],
+        (),
+        [
+            pltpu.VMEM((span, group), BF),
+            pltpu.VMEM((2 * span, group), BF),
+            pltpu.VMEM((2 * span, group), BF),
+            pltpu.VMEM((span, group), BF),
+            pltpu.VMEM((2 * span, group), F32),
+            pltpu.VMEM((2 * span, group), F32),
+        ],
+        flops=20 * span * span * group,
+    )
+
+
+def combine_kernel(grad_q, near, far, *outs):
+    rows, wide = outs[0].shape
+    group = wide // 3
+    for index, out in enumerate(outs):
+        cut = slice(index * rows, (index + 1) * rows)
+        out[:, :group] = grad_q[cut, :]
+        out[:, group:] = (near[cut, :] + far[cut, :].astype(F32)).astype(BF)
+
+
+def combine_fast(chips, grad_q, near, far):
+    span, group = grad_q.shape
+    return run(
+        combine_kernel,
+        "combine",
+        [shape((span // chips, 3 * group), BF)] * chips,
+        [grad_q, near, far],
+    )
+
+
+def exact_move(values, perm):
+    high = values.astype(BF)
+    rest = values - high.astype(F32)
+    middle = rest.astype(BF)
+    low = (rest - middle.astype(F32)).astype(BF)
+    return matmul(high, perm) + matmul(middle, perm) + matmul(low, perm)
+
+
+def collect(chips, stage, pieces, project):
+    chip, _ = spot_in()
+    width = project.shape[1] // 3
+    group = width // chips
+    for step in range(chips):
+        stage[lax.rem(chip + step, chips)] = pieces[step][...]
+    for section in range(3):
+        cut = slice(section * group, (section + 1) * group)
+        joined = jnp.concatenate([stage[index][:, cut] for index in range(chips)], 1)
+        project[:, section * width : (section + 1) * width] = joined
+
+
+def through_project(grad, project, weight):
+    width = grad.shape[1]
+    for section in range(3):
+        cut = slice(section * width, (section + 1) * width)
+        grad += matmul_t(project[:, cut], weight[:, cut])
+    return grad
+
+
+def project_back_kernel(chips, grad_one, perm, sums, *refs):
+    pieces, refs = refs[:chips], refs[chips:]
+    weights, refs = refs[:8], refs[8:]
+    out, project, vector_out, stage, weight, left_sems, right_sems = refs
+    copies = fetch_project(weights, weight, left_sems, right_sems, perm.shape[0])
+    collect(chips, stage, pieces, project)
+    wait_all(copies)
+    out[...] = through_project(grad_one[...], project, weight)
+    vector_rows(project, sums, perm, vector_out)
+
+
+def collect_kernel(chips, perm, sums, *refs):
+    pieces, refs = refs[:chips], refs[chips:]
+    project, vector_out, stage = refs
+    collect(chips, stage, pieces, project)
+    vector_rows(project, sums, perm, vector_out)
+
+
+def collect_fast(chips, perm, sums, pieces):
+    rows, group = pieces[0].shape
+    return run(
+        functools.partial(collect_kernel, chips),
+        "collect",
+        [shape((rows, chips * group), BF), shape(sums.shape, F32)],
+        [perm, sums, *pieces],
+        (),
+        [pltpu.VMEM((chips, rows, group), BF)],
+    )
+
+
+def input_back_kernel(grad_one, perm, project, *refs):
+    weights, refs = refs[:8], refs[8:]
+    out, weight, left_sems, right_sems = refs
+    wait_all(fetch_project(weights, weight, left_sems, right_sems, perm.shape[0]))
+    grad = through_project(grad_one[...], project, weight)
+    out[...] = matmul_t(grad.astype(BF), perm[...]).astype(BF)
+
+
+def input_back_fast(grad_one, perm, project, weights):
+    rows, width = grad_one.shape
+    return run(
+        input_back_kernel,
+        "input_back",
+        [shape((rows, width), BF)],
+        [grad_one, perm, project],
+        weights,
+        [
+            pltpu.VMEM((width, 3 * width), BF),
+            pltpu.SemaphoreType.DMA((4,)),
+            pltpu.SemaphoreType.DMA((8,)),
+        ],
+        flops=6 * rows * width * width,
+    )[0]
+
+
+def vector_rows(project, sums, perm, vector_out):
+    width = perm.shape[0]
+    vector_out[...] = sums[...]
+    vector_out[0:1, :] = column_sum(project[:, :width].astype(F32))
+    vector_out[1:2, :] = column_sum(project[:, 2 * width :].astype(F32))
+    moved = exact_move(vector_out[0:8, :], perm[...])
+    vector_out[0:2, :] = moved[0:2, :]
+    vector_out[5:8, :] = moved[5:8, :]
+    moved = exact_move(vector_out[8:16, :], perm[...])
+    vector_out[8:9, :] = moved[0:1, :]
+
+
+def project_back_fast(chips, grad_one, perm, sums, pieces, weights):
+    rows, width = grad_one.shape
+    return run(
+        functools.partial(project_back_kernel, chips),
+        "project_back",
+        [
+            shape((rows, width), F32),
+            shape((rows, 3 * width), BF),
+            shape((16, width), F32),
+        ],
+        [grad_one, perm, sums, *pieces],
+        weights,
+        [
+            pltpu.VMEM((chips, rows, 3 * width // chips), BF),
+            pltpu.VMEM((width, 3 * width), BF),
+            pltpu.SemaphoreType.DMA((4,)),
+            pltpu.SemaphoreType.DMA((8,)),
+        ],
+        flops=6 * rows * width * width,
+    )
+
+
+def feed_terms_kernel(normed, act, gave, theirs, gave_theirs, out):
+    _, core = spot_in()
+    width = normed.shape[1]
+    half = width // 2
+    left = jnp.concatenate([half_at(normed, core), theirs[:, 2 * half : 3 * half]], 0)
+    count = act.shape[1] // width
+    for index in range(count):
+        cut = slice(index * width, (index + 1) * width)
+        far = slice((index + 1) * width, (index + 2) * width)
+        right = jnp.concatenate([gave[:, far], gave_theirs[:, far]], 0)
+        out[:, cut] = grad_matmul(left, right).astype(BF)
+    left = jnp.concatenate([half_at(act, core), theirs[:, 3 * half :]], 0)
+    right = jnp.concatenate([gave[:, :width], gave_theirs[:, :width]], 0)
+    for index in range(count):
+        cut = slice(index * half, (index + 1) * half)
+        spot = slice((count + index) * width, (count + index + 1) * width)
+        out[:, spot] = grad_matmul(left[:, cut], right).astype(BF)
+
+
+def feed_terms_fast(normed, act, gave, theirs, gave_theirs):
+    rows, width = normed.shape
+    wide = act.shape[1]
+    return run(
+        feed_terms_kernel,
+        "feed_terms",
+        [shape((width // 2, 2 * wide), BF)],
+        [normed, act, gave, theirs, gave_theirs],
+        flops=4 * rows * width * wide,
+    )[0]
+
+
+def attend_terms_kernel(
+    low, attended, project, attn_nat, vector, theirs, project_theirs, attn_theirs,
+    vector_theirs, left_keep, left_sent, right_keep, right_sent
+):
+    _, core = spot_in()
+    bit, high = dp_place()
+    width = low.shape[1]
+    half = width // 2
+    block = half // 4
+
+    def put_left(columns, value):
+        value = value.astype(BF)
+        for side in range(2):
+            first = value[2 * side * block : (2 * side + 1) * block]
+            second = value[(2 * side + 1) * block : (2 * side + 2) * block]
+            rows = slice(side * block, (side + 1) * block)
+            left_keep[rows, columns] = jnp.where(bit == 0, first, second)
+            left_sent[rows, columns] = jnp.where(bit == 0, second, first)
+
+    def put_right(columns, value):
+        value = value.astype(BF)
+        first, second = value[: 2 * block], value[2 * block :]
+        right_keep[:, columns] = jnp.where(high == 0, first, second)
+        right_sent[:, columns] = jnp.where(high == 0, second, first)
+
+    left = jnp.concatenate([half_at(low, core), theirs[:, :half]], 0)
+    for index in range(3):
+        cut = slice(index * width, (index + 1) * width)
+        right = jnp.concatenate([project[:, cut], project_theirs[:, cut]], 0)
+        if index < 2:
+            put_left(cut, grad_matmul(left, right))
+        else:
+            put_right(slice(0, width), grad_matmul(left, right))
+    left = jnp.concatenate([half_at(attended, core), theirs[:, half : 2 * half]], 0)
+    right = jnp.concatenate([attn_nat[...], attn_theirs[...]], 0)
+    put_right(slice(width, 2 * width), grad_matmul(left, right))
+    rows = half_at(vector, core) + half_at(vector_theirs, core)
+    upper = rows.astype(BF)
+    rest = (rows - upper.astype(F32)).astype(BF)
+    count = rows.shape[0]
+    line = lax.broadcasted_iota(jnp.int32, (count, LANES), 0)
+    lane = lax.broadcasted_iota(jnp.int32, (count, LANES), 1)
+    extra = grad_matmul(upper, (lane == line).astype(BF))
+    extra += grad_matmul(rest, (lane == line + count).astype(BF))
+    put_right(slice(2 * width, 2 * width + LANES), extra)
+
+
+def attend_terms_fast(*args):
+    rows, width = args[0].shape
+    return run(
+        attend_terms_kernel,
+        "attend_terms",
+        [shape((width // 4, 2 * width), BF)] * 2
+        + [shape((width // 4, 2 * width + LANES), BF)] * 2,
+        list(args),
+        flops=16 * rows * width * width // 2,
+    )
+
+
+def after(array, *others):
+    return lax.optimization_barrier((array, *others))[0]
+
+
+def chips_parts(array):
+    return [array] + [chip_shift(array, step) for step in range(1, chips_of())]
+
+
+def chips_gather(array):
+    return lax.all_gather(
+        array, "seq", axis=0, tiled=True, axis_index_groups=core_groups()
+    )
+
+
+def chips_join(parts):
+    chips = chips_of()
+    chip, _ = place()
+    return jnp.concatenate(
+        [
+            lax.select_n(chip, *[parts[(spot - index) % chips] for spot in range(chips)])
+            for index in range(chips)
+        ],
+        0,
+    )
+
+
+def dp_swap(array, bit):
+    size = lax.axis_size("dp")
+    return lax.ppermute(array, "dp", [(i, i ^ bit) for i in range(size)])
+
+
+def dp_place():
+    spot = lax.axis_index("dp")
+    return spot % 2, spot // 2
+
+
+def join_pair(bit, own, other):
+    return jnp.where(
+        bit == 0, jnp.concatenate([own, other], 0), jnp.concatenate([other, own], 0)
+    )
+
+
+def square_first(part, cut):
+    left, right = part[:, :cut], part[:, cut:]
+    return left, dp_swap(left, 1), right, dp_swap(right, 2)
+
+
+def square_second(left, left_far, right, right_far):
+    bit, high = dp_place()
+    left_far, right_far = lax.optimization_barrier((left_far, right_far))
+    left = join_pair(bit, left, left_far)
+    right = join_pair(high, right, right_far)
+    return left, dp_swap(left, 2), right, dp_swap(right, 1)
+
+
+def square_pieces(left, left_far, right, right_far):
+    near = [core_swap(left), core_swap(right)]
+    left_far, right_far = lax.optimization_barrier((left_far, right_far))
+    return [
+        left, left_far, near[0], core_swap(left_far),
+        right, right_far, near[1], core_swap(right_far),
+    ]
+
+
+def vectors_kernel(groups, perm, perm_wide, *refs):
+    pieces, refs = refs[:4], refs[4:]
+    moved_out, plain_out, wide_out, stage, sems = refs
+    width = perm.shape[0]
+    start = pieces[0].shape[1] - LANES
+    wait_all(
+        fetch_right(pieces, stage, sems, slice(start, start + LANES), slice(0, LANES))
+    )
+    columns = stage[...]
+    line = lax.broadcasted_iota(jnp.int32, (width, width), 0)
+    spot = lax.broadcasted_iota(jnp.int32, (width, width), 1)
+    moved_out[...] = grad_matmul(columns, (line == spot).astype(BF))
+    plain = lax.dot_general(
+        columns, perm[...], (((0,), (1,)), ((), ())), preferred_element_type=F32
+    )
+    plain_out[...] = plain
+    wide = matmul(plain.astype(BF), perm_wide[...])
+    piece = width // (2 * groups)
+    for layer in range(LAYERS):
+        for index in range(groups):
+            row = layer * VECS + 5 + index
+            for part in range(2 * groups):
+                goal = part * groups * piece + index * piece
+                wide_out[layer : layer + 1, goal : goal + piece] = wide[
+                    row : row + 1, part * piece : (part + 1) * piece
+                ]
+
+
+def vectors_fast(groups, perm, perm_wide, pieces):
+    width = perm.shape[0]
+    return run(
+        functools.partial(vectors_kernel, groups),
+        "vectors",
+        [shape((LANES, width), F32)] * 2 + [shape((8, groups * width), F32)],
+        [perm, perm_wide],
+        pieces,
+        [pltpu.VMEM((width, LANES), BF), pltpu.SemaphoreType.DMA((8,))],
+    )
+
+
+def fold_kernel(*refs):
+    bit, high = dp_place()
+    for index, flag in enumerate((high, bit)):
+        keep, came, keep_out, sent_out = (refs[index * 2], refs[index * 2 + 1],
+                                          refs[4 + index * 2], refs[5 + index * 2])
+        rows = keep.shape[0] // 2
+        total = keep[...].astype(F32) + came[...].astype(F32)
+        keep_out[...] = jnp.where(flag == 0, total[:rows], total[rows:]).astype(BF)
+        sent_out[...] = jnp.where(flag == 0, total[rows:], total[:rows]).astype(BF)
+
+
+def split_kernel(chips, *refs):
+    left, left_far, right, right_far = refs[:4]
+    own, sends, total = refs[4], refs[5 : 4 + chips], refs[4 + chips]
+    chip, _ = spot_in()
+    cut = left.shape[1]
+    rows = left.shape[0] // chips
+    for index in range(chips):
+        span = slice(index * rows, (index + 1) * rows)
+        total[index, :, :cut] = left[span, :].astype(F32) + left_far[span, :].astype(F32)
+        total[index, :, cut:] = right[span, :].astype(F32) + right_far[span, :].astype(F32)
+    own[...] = total[chip]
+    for step in range(1, chips):
+        sends[step - 1][...] = total[lax.rem(chip + step, chips)].astype(BF)
+
+
+def square_fold(parts):
+    left, left_sent, right, right_sent = parts
+    rows = left.shape[0] // 2
+    kinds = [shape((rows, member.shape[1]), BF) for member in (left, left, right, right)]
+    return run(
+        fold_kernel, "fold", kinds,
+        [left, dp_swap(left_sent, 1), right, dp_swap(right_sent, 2)],
+    )
+
+
+def square_split(parts):
+    chips = chips_of()
+    left, left_sent, right, right_sent = parts
+    share = left.shape[0] // chips
+    width = left.shape[1] + right.shape[1]
+    return run(
+        functools.partial(split_kernel, chips),
+        "split",
+        [shape((share, width), F32)] + [shape((share, width), BF)] * (chips - 1),
+        [left, dp_swap(left_sent, 2), right, dp_swap(right_sent, 1)],
+        (),
+        [pltpu.VMEM((chips, share, width), F32)],
+    )
+
+
+def square_total(parts):
+    total = parts[0]
+    for step in range(1, len(parts)):
+        total = total + chip_shift(parts[step], step).astype(F32)
+    return total
+
+
+def piece_matrix(width, block, count):
+    spot = np.arange(width)
+    inner = spot % block
+    return one_hot(
+        ((spot // block) % 2) * (width // 2)
+        + (inner % count) * (width // (2 * count))
+        + (spot // (2 * block)) * (block // count)
+        + inner // count
+    )
+
+
+def fast_device(
+    hidden_input,
+    triple_weight,
+    mixer_weight,
+    expand_weight,
+    shrink_weight,
+    vector_params,
+    output_grad,
+):
+    _, count, width = hidden_input.shape
+    chips = chips_of()
+    _, core = place()
+    share = triple_weight.shape[1]
+    wide_share = shrink_weight.shape[1]
+    wide = expand_weight.shape[2]
+    groups = wide // width
+    perm = swap_matrix(width, share)
+    perm_wide = piece_matrix(width, wide_share, groups)
+    mixer_moved = move(mixer_weight.reshape(-1, width), perm).reshape(mixer_weight.shape)
+    shrink_moved = move(shrink_weight.reshape(-1, width), perm).reshape(shrink_weight.shape)
+    pieces = 2 * groups
+    expand_moved = (
+        move(expand_weight.reshape(-1, width), perm_wide)
+        .reshape(LAYERS * share, groups, pieces, width // pieces)
+        .transpose(0, 2, 1, 3)
+        .reshape(expand_weight.shape)
+    )
+    shrink_moved = shrink_moved.reshape(LAYERS, share, groups * width)
+    vector_columns = vector_params.reshape(LAYERS * VECS, share).T
+    vector_columns = jnp.pad(vector_columns, ((0, 0), (0, LANES - LAYERS * VECS)))
+
+    feed_parts = [
+        jnp.concatenate([expand_moved[layer], shrink_moved[layer]], 1) for layer in range(LAYERS)
+    ]
+    attn_one = jnp.concatenate([triple_weight[1], mixer_moved[1]], 1)
+    parts = chips_parts(jnp.concatenate([triple_weight[0], mixer_moved[0], vector_columns], 1))
+    parts[-1] = after(parts[-1], feed_parts[0])
+    attn_zero = chips_join(parts)
+    attn_zero = square_pieces(*square_second(*square_first(attn_zero, 2 * width)))
+    feed_zero = chips_gather(feed_parts[0])
+    attn_one = chips_parts(after(attn_one, attn_zero[0], attn_zero[4]))
+    feed_zero = square_first(after(feed_zero, *attn_zero), wide)
+    moved_rows, plain_rows, wide_rows = vectors_fast(groups, perm, perm_wide, attn_zero[4:])
+    rows_of = []
+    for layer in range(LAYERS):
+        cut = slice(layer * VECS, (layer + 1) * VECS)
+        rows_of.append(
+            (moved_rows[cut], plain_rows[cut], wide_rows[layer : layer + 1])
+        )
+
+    def project(layer, hidden, pieces):
+        low, blocks = project_fast(layer == 0, chips, hidden, perm, rows_of[layer][1], pieces)
+        blocks = [blocks[0]] + [chip_shift(blocks[step], step) for step in range(1, chips)]
+        return low, blocks
+
+    def attend_blocks(blocks):
+        others = [core_swap(block) for block in blocks]
+        mixed, logs, pieces = attend_fast(chips, blocks, others)
+        pieces = [pieces[0]] + [chip_shift(pieces[step], -step) for step in range(1, chips)]
+        return (blocks, others, mixed, logs), pieces
+
+    def feed(layer, hidden, low, pieces, weights):
+        rows, _, ffn_bias = rows_of[layer]
+        (
+            hidden, attended, normed, pre_act, act, hat_one, scale_one, hat_two, scale_two,
+            sent, squares,
+        ) = feed_fast(chips, hidden, low, perm, rows, ffn_bias, pieces, weights)
+        return (
+            hidden,
+            (hat_one, scale_one, hat_two, scale_two, pre_act),
+            (low, attended, normed, act, core_swap(sent)),
+            jnp.sum(squares[:3], -1),
+        )
+
+    low, blocks = project(0, hidden_input[0], attn_zero)
+    feed_zero = [after(feed_zero[0], low), *feed_zero[1:]]
+    feed_zero = square_second(*feed_zero)
+    blocks[0] = after(blocks[0], feed_zero[0], feed_zero[2])
+    feed_one = chips_gather(after(feed_parts[1], *blocks))
+    attn_one[-1] = after(attn_one[-1], low)
+    attn_one = chips_join(attn_one)
+    attend_zero, pieces = attend_blocks(blocks)
+    attn_one = square_first(after(attn_one, attend_zero[2]), 2 * width)
+    attn_one = square_second(*attn_one)
+    feed_one = lax.all_gather(
+        after(feed_one, attn_one[0], attn_one[2]), "dp", axis=0, tiled=True
+    )
+    feed_zero = square_pieces(*feed_zero)
+    pieces[0] = after(pieces[0], attn_one[0], attn_one[2])
+    hidden, feed_saved_zero, acts_zero, squares_zero = feed(
+        0, low, low, pieces, attn_zero[4:] + feed_zero
+    )
+    attn_one = square_pieces(*attn_one)
+    low, blocks = project(1, hidden, attn_one)
+    attend_one, pieces = attend_blocks(blocks)
+    feed_one = after(feed_one, attend_one[2])
+    feed_one = [feed_one, core_swap(feed_one)]
+    hidden, feed_saved_one, acts_one, squares_one = feed(
+        1, hidden, low, pieces, attn_one[4:] + feed_one
+    )
+    packs = [attn_zero + feed_zero, attn_one + feed_one]
+    kept = [(attend_zero, feed_saved_zero, acts_zero), (attend_one, feed_saved_one, acts_one)]
+    collected = [squares_zero, squares_one]
+    elements = count * width * lax.axis_size("dp") * lax.axis_size("seq")
+    hidden_output = move_back(hidden.astype(BF), perm)
+
+    totals = jnp.stack(collected)
+    sum_steps = [("seq", 1), ("seq", 2), ("seq", 4), ("dp", 1), ("dp", 2)]
+    sum_steps = [step for step in sum_steps if step[1] < lax.axis_size(step[0])]
+
+    def sum_more(totals, token):
+        if sum_steps:
+            axis, bit = sum_steps.pop(0)
+            size = lax.axis_size(axis)
+            pairs = [(i, i ^ bit) for i in range(size)]
+            totals = totals + lax.ppermute(after(totals, token), axis, pairs)
+        return totals
+
+    def scatter_feed(term):
+        part = lax.psum_scatter(term, "dp", scatter_dimension=0, tiled=True)
+        part = lax.psum_scatter(
+            part, "seq", scatter_dimension=0, tiled=True, axis_index_groups=core_groups()
+        )
+        return part.astype(F32)
+
+    def back_feed(layer, grad):
+        (_, feed_saved, acts), weights = kept[layer], packs[layer]
+        grad_one, gave, attn_nat, sums, grads = feed_back_fast(
+            layer == LAYERS - 1, chips, grad, perm, perm_wide, rows_of[layer][0], feed_saved,
+            weights[4:],
+        )
+        grads = [grads[0]] + [chip_shift(grads[step], step) for step in range(1, chips)]
+        _, _, normed, act, theirs = acts
+        feed_term = feed_terms_fast(normed, act, gave, theirs, core_swap(gave))
+        return grad_one, attn_nat, sums, grads, feed_term
+
+    def back_attend(layer, grads):
+        blocks, others, mixed, logs = kept[layer][0]
+        return attend_back_fast(chips, blocks, others, grads, mixed, logs)
+
+    def back_combine(grad_q, near, far):
+        pieces = combine_fast(chips, grad_q, near, far)
+        return [pieces[0]] + [chip_shift(pieces[step], -step) for step in range(1, chips)]
+
+    def back_project(layer, grad_one, sums, pieces):
+        return project_back_fast(chips, grad_one, perm, sums, pieces, packs[layer][:8])
+
+    def back_terms(layer, project_grad, attn_nat, vector, far):
+        low, attended, _, _, theirs = kept[layer][2]
+        return attend_terms_fast(
+            low, attended, project_grad, attn_nat, vector, theirs, *far
+        )
+
+    def swap_all(*members):
+        return [core_swap(member) for member in members]
+
+    grad_one, attn_nat, sums, grads, feed_term = back_feed(1, output_grad[0])
+    totals = sum_more(totals, grad_one)
+    feed_sum_one = lax.psum_scatter(feed_term, "dp", scatter_dimension=0, tiled=True)
+    grads[0] = after(grads[0], feed_term, totals)
+    grad_q, near, far = back_attend(1, grads)
+    totals = sum_more(totals, grad_q)
+    pieces = back_combine(after(grad_q, totals), near, core_swap(far))
+    totals = sum_more(totals, pieces[0])
+    pieces[0] = after(pieces[0], totals)
+    grad, project_grad, vector = back_project(1, grad_one, sums, pieces)
+    far_one = swap_all(project_grad, attn_nat, vector)
+    terms_args = (project_grad, attn_nat, vector)
+
+    grad_one, attn_nat, sums, grads, feed_term = back_feed(0, grad)
+    attn_terms = back_terms(1, *terms_args, far_one)
+    totals = sum_more(totals, grad_one)
+    grads[0] = after(grads[0], feed_term, attn_terms[0], totals)
+    grad_q, near, far = back_attend(0, grads)
+    feed_sum_zero = scatter_feed(feed_term)
+    totals = sum_more(totals, grad_q)
+    pieces = back_combine(grad_q, near, core_swap(far))
+    folded = square_fold(attn_terms)
+    pieces[0] = after(pieces[0], folded[0], totals)
+    project_grad, vector = collect_fast(chips, perm, sums, pieces)
+    far_zero = swap_all(project_grad, attn_nat, vector)
+    attn_terms = back_terms(0, project_grad, attn_nat, vector, far_zero)
+    input_grad = input_back_fast(
+        after(grad_one, attn_terms[0]), perm, project_grad, packs[0][:8]
+    )
+    split_one = square_split([after(folded[0], attn_terms[0]), *folded[1:]])
+    feed_sum_one = after(feed_sum_one, attn_terms[0])
+    feed_sum_one = scatter_chips(feed_sum_one)
+    attn_terms = [
+        attn_terms[0], after(attn_terms[1], split_one[0], input_grad), *attn_terms[2:]
+    ]
+    folded = square_fold(attn_terms)
+    attn_sum_one = square_total(split_one)
+    folded = [after(folded[0], attn_sum_one, feed_sum_one), *folded[1:]]
+    attn_sum_zero = square_total(square_split(folded))
+    terms = [(attn_sum_zero, feed_sum_zero), (attn_sum_one, feed_sum_one)]
+    grad = input_grad
+    root_squares = jnp.sqrt(totals / elements)
+    vector_grad = jnp.stack(
+        [
+            (
+                terms[layer][0][:, 4 * width : 4 * width + VECS]
+                + terms[layer][0][:, 4 * width + 16 : 4 * width + 16 + VECS]
+            ).T
+            for layer in range(LAYERS)
+        ]
+    )
+    return (
+        hidden_output[None],
+        grad[None],
+        jnp.stack([terms[layer][0][:, : 3 * width] for layer in range(LAYERS)]),
+        jnp.stack([terms[layer][0][:, 3 * width : 4 * width] for layer in range(LAYERS)]),
+        jnp.stack([terms[layer][1][:, :wide] for layer in range(LAYERS)]),
+        jnp.stack(
+            [terms[layer][1][:, wide:].reshape(wide_share, width) for layer in range(LAYERS)]
+        ),
+        vector_grad,
+        root_squares,
+    )
+
+
+def per_device(*args):
+    chips = chips_of()
+    if chips in (2, 4) and HEADS % chips == 0 and lax.axis_size("dp") == 4:
+        return fast_device(*args)
+    return plain_device(*args)
+
+
 def solution(mesh):
     return jax.shard_map(
         per_device,

time: 717 us -> 525 us (0.73)
  matrix products: 152 us -> 3.76 us
  Pallas kernels: 0 us -> 138 us
  waiting for transfers between devices: 292 us -> 228 us
  other arithmetic: 61.8 us -> 10.5 us
  local copies, waits for them, and re-layouts: 69.7 us -> 29.2 us
  starting transfers between devices: 113 us -> 90 us
    pallas_call x0 -> x24, Pallas kernels: none -> 138 us  [run(): pl.pallas_call(kernel, name=name, out_shape=list(outs), in_specs=[VMEM] *...]
    ppermute x5 -> x25, waiting for transfers between devices: 6.65 us -> 121 us  [the longest x20 105 us: dp_swap(): return lax.ppermute(array, 'dp', [(i, i ^ bit) for i in range(size)])]
    all_gather x6 -> x3, waiting for transfers between devices: 130 us -> 18 us  [the longest x2 18 us: chips_gather(): lax.all_gather(array, 'seq', axis=0, tiled=True, axis_index_groups=core_g...]
    dot_general x66 -> x0, matrix products: 85 us -> none  [the longest x34 51.6 us: matmul(): return jnp.dot(left, right, preferred_element_type=F32)]
    ppermute x48 -> x39, waiting for transfers between devices: 153 us -> 72.9 us  [chip_shift(): return lax.ppermute(array, 'seq', pairs)]
    dot_general x40 -> x1, matrix products: 62.3 us -> 1.22 us  [matmul_t(): lax.dot_general(left, right, (((1,), (1,)), ((), ())), preferred_element_...]
    ppermute x48 -> x39, starting transfers between devices: 92.8 us -> 50.5 us  [chip_shift(): return lax.ppermute(array, 'seq', pairs)]
    ppermute x5 -> x25, starting transfers between devices: 14.4 us -> 32.5 us  [the longest x20 26.2 us: dp_swap(): return lax.ppermute(array, 'dp', [(i, i ^ bit) for i in range(size)])]
  transfers between devices with their start and end apart: 87 -> 103, of which waited for: 36 -> 40; matrix products, arithmetic and copies ran while one was open for 32% -> 3% of each run, Pallas kernels for 0% -> 22%
where the time goes in v2:
time: 525 us; the launch traced here: 516 us
  waiting for transfers between devices  228 us (43%)
  Pallas kernels  138 us (26%)
  starting transfers between devices  90 us (17%)
  local copies, waits for them, and re-layouts  29.2 us (6%)
  between operations  16 us (3%)
  other arithmetic  10.5 us (2%)
    pallas_call x24, Pallas kernels, run(): pl.pallas_call(kernel, name=name, out_shape=list(outs), in_specs=[VMEM] *...  138 us
    ppermute x20, waiting for transfers between devices, dp_swap(): return lax.ppermute(array, 'dp', [(i, i ^ bit) for i in range(size)])  105 us
    ppermute x39, waiting for transfers between devices, chip_shift(): return lax.ppermute(array, 'seq', pairs)  72.9 us
    ppermute x39, starting transfers between devices, chip_shift(): return lax.ppermute(array, 'seq', pairs)  50.5 us
    ppermute x20, starting transfers between devices, dp_swap(): return lax.ppermute(array, 'dp', [(i, i ^ bit) for i in range(size)])  26.2 us
    unnamed x198, local copies, waits for them, and re-layouts  18.9 us
    all_gather x2, waiting for transfers between devices, chips_gather(): lax.all_gather(array, 'seq', axis=0, tiled=True, axis_index_groups=core_g...  18 us
    ppermute x5, waiting for transfers between devices, sum_more(): totals = totals + lax.ppermute(after(totals, token), axis, pairs)  16.1 us
  transfers between devices with their start and end apart: 103, of which 40 were waited for; matrix products, arithmetic and copies ran while one was open for 3% of the time, Pallas kernels for 22%

profile of v2, /device:TPU:0, one launch (start us, length us, event | category | flops | bytes accessed | tf_op | source)
XLA Modules:
  0.0 515.6 jit_solution(5992519714566626916)
XLA Ops:
  10.0 4.1 collective-permute-start.1
  23.0 2.9 collective-permute-done
  29.4 6.0 %collective-permute-done.3 = bf16[96,1536]{1,0:T(8,128)(2,1)S(1)} collective-permute-done((bf16[96,1536]{1,0:T(8,128)(2,1)S(1)}, bf16[96,1536]{1,0:T(8,128)(2,1)S(1)}, u32[]{:S(2)}, u32[]{:S(2)}) %collective-permute-start.3) | collective-permute-done | bytes 294944 | tf_op jit(solution)/shard_map/ppermute | solution.py:1226
  39.7 11.4 %collective-permute-done.5.rest_1_.refs_1_ = bf16[192,1536]{1,0:T(8,128)(2,1)} collective-permute-done((bf16[192,1536]{1,0:T(8,128)(2,1)}, bf16[192,1536]{1,0:T(8,128)(2,1)}, u32[]{:S(2)}, u32[]{:S(2)}) %collective-permute-start.5) | collective-permute-done | bytes 589856 | tf_op jit(solution)/shard_map/ppermute | solution.py:1226
  54.3 6.2 %all-gather.4.cloned.1.call-done = bf16[96,6144]{1,0:T(8,128)(2,1)} async-done(((bf16[24,6144]{1,0:T(8,128)(2,1)}), bf16[96,6144]{1,0:T(8,128)(2,1)}) %all-gather.4.cloned.1.call-update) | async-done | bytes 1179664 | tf_op jit(solution)/shard_map/all_gather | solution.py:1207
  68.5 4.4 vectors.1
  74.4 5.0 project.2
  80.3 3.3 collective-permute-start.14
  85.4 3.3 collective-permute-done.13.refs_1_
  88.7 4.4 collective-permute-done.14.refs_2_
  96.6 5.6 %attend.2 = (f32[512,192]{1,0:T(8,128)}, f32[512,128]{1,0:T(8,128)}, bf16[128,192]{1,0:T(8,128)(2,1)}, bf16[128,192]{1,0:T(8,128)(2,1)}, bf16[128,192]{1,0:T(8,128)(2,1)}, /*index=5*/bf16[128,192]{1,0:T(8,128)(2,1)}) custom-call(bf16[128,576]{1,0:T(8,128)(2,1)} %get-tuple-element.166.refs_0_, bf16[128,576]{1,0:T(8,128)(2,1)} %copy-done.67, ...), custom_call_target="tpu_custom_call" | custom-call | flops 1610612736 | bytes 8126464 | tf_op jit(solution)/shard_map/attend/pallas_call | solution.py:474
  103.4 8.0 %collective-permute-done.23 = bf16[96,1536]{1,0:T(8,128)(2,1)S(1)} collective-permute-done((bf16[96,1536]{1,0:T(8,128)(2,1)S(1)}, bf16[96,1536]{1,0:T(8,128)(2,1)S(1)}, u32[]{:S(2)}, u32[]{:S(2)}) %collective-permute-start.23) | collective-permute-done | bytes 294944 | tf_op jit(solution)/shard_map/ppermute | solution.py:1226
  112.0 11.8 %all-gather.6.cloned.1.call-done = bf16[96,6144]{1,0:T(8,128)(2,1)} async-done(((bf16[24,6144]{1,0:T(8,128)(2,1)}), bf16[96,6144]{1,0:T(8,128)(2,1)}) %all-gather.6.cloned.1.call-update) | async-done | bytes 1179664 | tf_op jit(solution)/shard_map/all_gather | solution.py:1207
  129.8 36.2 %collective-permute-done.28.refs_9_.refs_5_ = bf16[192,3072]{1,0:T(8,128)(2,1)S(1)} collective-permute-done((bf16[192,3072]{1,0:T(8,128)(2,1)}, bf16[192,3072]{1,0:T(8,128)(2,1)S(1)}, u32[]{:S(2)}, u32[]{:S(2)}) %collective-permute-start.28) | collective-permute-done | bytes 1179680 | tf_op jit(solution)/shard_map/ppermute | solution.py:1226
  168.0 3.8 collective-permute-done.26.refs_2_
  171.8 14.6 %collective-permute-done.34.rest_1_.refs_5_ = bf16[192,1536]{1,0:T(8,128)(2,1)S(1)} collective-permute-done((bf16[192,1536]{1,0:T(8,128)(2,1)S(1)}, bf16[192,1536]{1,0:T(8,128)(2,1)S(1)}, u32[]{:S(2)}, u32[]{:S(2)}) %collective-permute-start.34) | collective-permute-done | bytes 589856 | tf_op jit(solution)/shard_map/ppermute | solution.py:1226
  190.9 3.8 collective-permute-done.27.refs_3_
  198.5 9.8 %feed.2 = (f32[128,768]{1,0:T(8,128)}, bf16[128,768]{1,0:T(8,128)(2,1)}, bf16[128,768]{1,0:T(8,128)(2,1)}, f32[128,3072]{1,0:T(8,128)}, bf16[128,3072]{1,0:T(8,1...) custom-call(bf16[128,768]{1,0:T(8,128)(2,1)} %get-tuple-element.158., ...), custom_call_target="tpu_custom_call" | custom-call | flops 6039797760 | bytes 74350592 | tf_op jit(solution)/shard_map/feed/pallas_call | solution.py:474
  209.8 5.0 project.3
  215.1 3.6 collective-permute-start.42
  218.7 5.4 %collective-permute-done.40.refs_1_ = bf16[128,576]{1,0:T(8,128)(2,1)S(1)} collective-permute-done((bf16[128,576]{1,0:T(8,128)(2,1)}, bf16[128,576]{1,0:T(8,128)(2,1)S(1)}, u32[]{:S(2)}, u32[]{:S(2)}) %collective-permute-start.40) | collective-permute-done | bytes 147488 | tf_op jit(solution)/shard_map/ppermute | solution.py:61
  224.1 6.1 %collective-permute-done.41.refs_2_ = bf16[128,576]{1,0:T(8,128)(2,1)S(1)} collective-permute-done((bf16[128,576]{1,0:T(8,128)(2,1)}, bf16[128,576]{1,0:T(8,128)(2,1)S(1)}, u32[]{:S(2)}, u32[]{:S(2)}) %collective-permute-start.41) | collective-permute-done | bytes 147488 | tf_op jit(solution)/shard_map/ppermute | solution.py:61
  232.9 5.6 %attend.3 = (f32[512,192]{1,0:T(8,128)}, f32[512,128]{1,0:T(8,128)}, bf16[128,192]{1,0:T(8,128)(2,1)}, bf16[128,192]{1,0:T(8,128)(2,1)}, bf16[128,192]{1,0:T(8,128)(2,1)}, /*index=5*/bf16[128,192]{1,0:T(8,128)(2,1)}) custom-call(bf16[128,576]{1,0:T(8,128)(2,1)} %get-tuple-element.187.refs_0_, bf16[128,576]{1,0:T(8,128)(2,1)} %copy-done.74, ...), custom_call_target="tpu_custom_call" | custom-call | flops 1610612736 | bytes 8126464 | tf_op jit(solution)/shard_map/attend/pallas_call | solution.py:474
  244.1 5.4 %collective-permute-done.48.refs_2_ = bf16[128,192]{1,0:T(8,128)(2,1)S(1)} collective-permute-done((bf16[128,192]{1,0:T(8,128)(2,1)}, bf16[128,192]{1,0:T(8,128)(2,1)S(1)}, u32[]{:S(2)}, u32[]{:S(2)}) %collective-permute-start.48) | collective-permute-done | bytes 49184 | tf_op jit(solution)/shard_map/ppermute | solution.py:61
  251.7 9.9 %feed.3 = (f32[128,768]{1,0:T(8,128)}, bf16[128,768]{1,0:T(8,128)(2,1)}, bf16[128,768]{1,0:T(8,128)(2,1)}, f32[128,3072]{1,0:T(8,128)}, bf16[128,3072]{1,0:T(8,1...) custom-call(f32[128,768]{1,0:T(8,128)} %get-tuple-element.183.source, ...), custom_call_target="tpu_custom_call" | custom-call | flops 6039797760 | bytes 74350592 | tf_op jit(solution)/shard_map/feed/pallas_call | solution.py:474
  261.7 13.2 %feed_back.2 = (f32[128,768]{1,0:T(8,128)}, bf16[128,3840]{1,0:T(8,128)(2,1)}, bf16[128,768]{1,0:T(8,128)(2,1)}, f32[16,768]{1,0:T(8,128)}, bf16[128,192]{1,0:T(...) custom-call(bf16[128,768]{1,0:T(8,128)(2,1)} %bitcast.64, ...), custom_call_target="tpu_custom_call" | custom-call | flops 7247757312 | bytes 74792960 | tf_op jit(solution)/shard_map/feed_back/pallas_call | solution.py:474
  280.7 5.6 %feed_terms.2 = bf16[384,6144]{1,0:T(8,128)(2,1)} custom-call(bf16[128,768]{1,0:T(8,128)(2,1)} %get-tuple-element.208.normed, bf16[128,3072]{1,0:T(8,128)(2,1)} %get-tuple-element.209.act, bf16[128,3840]{1,0:T(8,128)(2,1)} %get-tuple-element.210.gave, bf16[128,2688]{1,0:T(8,128)(2,1)} %copy-done.54, bf16[128,3840]{1,0:T(8,128)(2,1)} %copy-done.51), custom_call_target="tpu_custom_call" | custom-call | flops 48318382080 | bytes 334233600 | tf_op jit(solution)/shard_map/feed_terms/pallas_call | solution.py:474
  287.2 8.4 %attend_back.2 = (bf16[512,192]{1,0:T(8,128)(2,1)}, f32[512,384]{1,0:T(8,128)}, bf16[512,384]{1,0:T(8,128)(2,1)}) custom-call(bf16[128,576]{1,0:T(8,128)(2,1)} %get-tuple-element.187.refs_0_, bf16[128,576]{1,0:T(8,128)(2,1)} %copy-done.74, bf16[128,576]{1,0:T(8,128)(2,1)} %copy-done.75, bf16[128,576]{1,0:T(8,128)(2,1)} %copy-done.76, ...), custom_call_target="tpu_custom_call" | custom-call | flops 4026531840 | bytes 13631488 | tf_op jit(solution)/shard_map/attend_back/pallas_call | solution.py:474
  307.5 11.7 %collective-permute-done.59 = f32[2,3]{1,0:T(2,128)S(1)} collective-permute-done((f32[2,3]{1,0:T(2,128)S(1)}, f32[2,3]{1,0:T(2,128)S(1)}, u32[]{:S(2)}, u32[]{:S(2)}) %collective-permute-start.59) | collective-permute-done | bytes 56 | tf_op jit(solution)/shard_map/ppermute | solution.py:1486
  320.1 6.6 %project_back.1 = (f32[128,768]{1,0:T(8,128)}, bf16[128,2304]{1,0:T(8,128)(2,1)}, f32[16,768]{1,0:T(8,128)}) custom-call(f32[128,768]{1,0:T(8,128)} %get-tuple-element.205.grad_one, bf16[768,768]{1,0:T(8,128)(2,1)} %constant.91.clone.perm, f32[16,768]{1,0:T(8,128)} %get-tuple-element.206.sums, bf16[128,576]{1,0:T(8,128)(2,1)} %get-tuple-element.227.refs_0_, ...), custom_call_target="tpu_custom_call" | custom-call | flops 1811939328 | bytes 31850496 | tf_op jit(solution)/shard_map/project_back/pallas_call | solution.py:474
  327.4 13.2 %feed_back.3 = (f32[128,768]{1,0:T(8,128)}, bf16[128,3840]{1,0:T(8,128)(2,1)}, bf16[128,768]{1,0:T(8,128)(2,1)}, f32[16,768]{1,0:T(8,128)}, bf16[128,192]{1,0:T(...) custom-call(f32[128,768]{1,0:T(8,128)} %get-tuple-element.231.source, ...), custom_call_target="tpu_custom_call" | custom-call | flops 7247757312 | bytes 76365824 | tf_op jit(solution)/shard_map/feed_back/pallas_call | solution.py:474
  345.5 3.0 collective-permute-start.70
  350.0 3.8 attend_terms.2
  355.7 5.6 %feed_terms.3 = bf16[384,6144]{1,0:T(8,128)(2,1)} custom-call(bf16[128,768]{1,0:T(8,128)(2,1)} %get-tuple-element.241.normed, bf16[128,3072]{1,0:T(8,128)(2,1)} %get-tuple-element.242.act, bf16[128,3840]{1,0:T(8,128)(2,1)} %get-tuple-element.243.gave, bf16[128,2688]{1,0:T(8,128)(2,1)} %copy-done.52, bf16[128,3840]{1,0:T(8,128)(2,1)} %copy-done.50), custom_call_target="tpu_custom_call" | custom-call | flops 48318382080 | bytes 334233600 | tf_op jit(solution)/shard_map/feed_terms/pallas_call | solution.py:474
  362.0 8.4 %attend_back.3 = (bf16[512,192]{1,0:T(8,128)(2,1)}, f32[512,384]{1,0:T(8,128)}, bf16[512,384]{1,0:T(8,128)(2,1)}) custom-call(bf16[128,576]{1,0:T(8,128)(2,1)} %get-tuple-element.166.refs_0_, bf16[128,576]{1,0:T(8,128)(2,1)} %copy-done.67, bf16[128,576]{1,0:T(8,128)(2,1)} %copy-done.68, bf16[128,576]{1,0:T(8,128)(2,1)} %copy-done.69, ...), custom_call_target="tpu_custom_call" | custom-call | flops 4026531840 | bytes 13631488 | tf_op jit(solution)/shard_map/attend_back/pallas_call | solution.py:474
  380.4 13.2 %collective-permute-done.73.refs_1_ = bf16[192,1536]{1,0:T(8,128)(2,1)S(1)} collective-permute-done((bf16[192,1536]{1,0:T(8,128)(2,1)S(1)}, bf16[192,1536]{1,0:T(8,128)(2,1)S(1)}, u32[]{:S(2)}, u32[]{:S(2)}) %collective-permute-start.73) | collective-permute-done | bytes 589856 | tf_op jit(solution)/shard_map/ppermute | solution.py:1226
  394.7 2.8 fold.2
  398.3 3.5 collect.1
  405.6 2.9 collective-permute-start.83
  409.5 3.8 attend_terms.3
  413.3 4.9 collective-permute-done.83.refs_3_
  424.1 6.3 %input_back.1 = bf16[128,768]{1,0:T(8,128)(2,1)} custom-call(f32[128,768]{1,0:T(8,128)} %get-tuple-element.273.grad_one, bf16[768,768]{1,0:T(8,128)(2,1)} %constant.91.clone.perm, bf16[128,2304]{1,0:T(8,128)(2,1)} %get-tuple-element.269.project, bf16[192,1536]{1,0:T(8,128)(2,1)} %maximum_select_fusion.3.rest_0_.refs_0_, ...), custom_call_target="tpu_custom_call" | custom-call | flops 18119393280 | bytes 290979840 | tf_op jit(solution)/shard_map/input_back/pallas_call | solution.py:474
  433.7 3.6 collective-permute-done.87
  442.2 7.4 %collective-permute-done.84.refs_1_ = bf16[192,1536]{1,0:T(8,128)(2,1)S(1)} collective-permute-done((bf16[192,1536]{1,0:T(8,128)(2,1)}, bf16[192,1536]{1,0:T(8,128)(2,1)S(1)}, u32[]{:S(2)}, u32[]{:S(2)}) %collective-permute-start.84) | collective-permute-done | bytes 589856 | tf_op jit(solution)/shard_map/ppermute | solution.py:1226
  456.3 10.0 %collective-permute-done.90 = bf16[24,6144]{1,0:T(8,128)(2,1)S(1)} collective-permute-done((bf16[24,6144]{1,0:T(8,128)(2,1)S(1)}, bf16[24,6144]{1,0:T(8,128)(2,1)S(1)}, u32[]{:S(2)}, u32[]{:S(2)}) %collective-permute-start.90) | collective-permute-done | bytes 294944 | tf_op jit(solution)/shard_map/ppermute | solution.py:61
  473.4 3.7 collective-permute-done.96
  477.1 15.6 %collective-permute-done.95 = bf16[24,3200]{1,0:T(8,128)(2,1)S(1)} collective-permute-done((bf16[24,3200]{1,0:T(8,128)(2,1)}, bf16[24,3200]{1,0:T(8,128)(2,1)S(1)}, u32[]{:S(2)}, u32[]{:S(2)}) %collective-permute-start.95) | collective-permute-done | bytes 153632 | tf_op jit(solution)/shard_map/ppermute | solution.py:61
  495.0 10.3 %reduce-scatter.8.cloned.1.call-done = bf16[24,6144]{1,0:T(8,128)(2,1)} async-done(((bf16[96,6144]{1,0:T(8,128)(2,1)}), bf16[24,6144]{1,0:T(8,128)(2,1)}) %reduce-scatter.8.cloned.1.call-update) | async-done | bytes 294928 | tf_op jit(solution)/shard_map/reduce_scatter | solution.py:1491
  (453 shorter events, 146.7 us)
Async XLA Ops:
  7.2 53.3 %all-gather.4.cloned.1.call-start = ((), (), s32[]{:S(2)}) async-start(), calls=%async_computation.3 | async-start | bytes 1474560 | tf_op jit(solution)/shard_map/all_gather | solution.py:1207
  29.4 94.5 %all-gather.6.cloned.1.call-start = ((), (), s32[]{:S(2)}) async-start(), calls=%async_computation.4 | async-start | bytes 1474560 | tf_op jit(solution)/shard_map/all_gather | solution.py:1207
  35.6 15.5 %collective-permute-start.6 = (bf16[192,1664]{1,0:T(8,128)(2,1)S(1)}, bf16[192,1664]{1,0:T(8,128)(2,1)S(1)}, u32[]{:S(2)}, u32[]{:S(2)}) collective-permute-start(bf16[192,1664]{1,0:T(8,128)(2,1)S(1)} %maximum_select_fusion.2.refs_0_.rest_4_.refs_4_), channel_id=1, source_target_pairs={{0,8},{8,0},{16,24},{24,16},{1,9},{9,1},{17,25},{25,17},{2,10},{10... | collective-permute-start | bytes 1916936 | tf_op jit(solution)/shard_map/ppermute | solution.py:1226
  39.1 13.2 %collective-permute-start.7 = (bf16[192,1664]{1,0:T(8,128)(2,1)S(1)}, bf16[192,1664]{1,0:T(8,128)(2,1)S(1)}, u32[]{:S(2)}, u32[]{:S(2)}) collective-permute-start(bf16[192,1664]{1,0:T(8,128)(2,1)S(1)} %maximum_select_fusion.2.refs_0_.rest_4_.refs_4_), channel_id=1, source_target_pairs={{0,1},{1,0},{2,3},{3,2},{4,5},{5,4},{6,7},{7,6},{8,9},{9,8},{10,11... | collective-permute-start | bytes 1916936 | tf_op jit(solution)/shard_map/ppermute | solution.py:54
  61.8 18.5 %collective-permute-start.11 = (bf16[96,3072]{1,0:T(8,128)(2,1)S(1)}, bf16[96,3072]{1,0:T(8,128)(2,1)S(1)}, u32[]{:S(2)}, u32[]{:S(2)}) collective-permute-start(bf16[96,3072]{1,0:T(8,128)(2,1)S(1)} %get-tuple-element.163), channel_id=1, source_target_pairs={{0,8},{8,0},{16,24},{24,16},{1,9},{9,1},{17,25},{25,17},{2,10},{10... | collective-permute-start | bytes 1769480 | tf_op jit(solution)/shard_map/ppermute | solution.py:1226
  63.4 20.3 %collective-permute-start.12 = (bf16[96,3072]{1,0:T(8,128)(2,1)S(1)}, bf16[96,3072]{1,0:T(8,128)(2,1)S(1)}, u32[]{:S(2)}, u32[]{:S(2)}) collective-permute-start(bf16[96,3072]{1,0:T(8,128)(2,1)S(1)} %get-tuple-element.317), channel_id=1, source_target_pairs={{0,16},{8,24},{16,0},{24,8},{1,17},{9,25},{17,1},{25,9},{2,18},{10... | collective-permute-start | bytes 1769480 | tf_op jit(solution)/shard_map/ppermute | solution.py:1226
  64.9 28.3 %collective-permute-start.21 = (bf16[24,3072]{1,0:T(8,128)(2,1)S(1)}, bf16[24,3072]{1,0:T(8,128)(2,1)S(1)}, u32[]{:S(2)}, u32[]{:S(2)}) collective-permute-start(bf16[24,3072]{1,0:T(8,128)(2,1)S(1)} %pad_maximum_fusion.7), channel_id=1, source_target_pairs={{0,4},{1,5},{2,6},{3,7},{4,0},{5,1},{6,2},{7,3},{8,12},{9,13},{10,... | collective-permute-start | bytes 442376 | tf_op jit(solution)/shard_map/ppermute | solution.py:61
  68.3 24.9 %collective-permute-start.20 = (bf16[24,3072]{1,0:T(8,128)(2,1)S(1)}, bf16[24,3072]{1,0:T(8,128)(2,1)S(1)}, u32[]{:S(2)}, u32[]{:S(2)}) collective-permute-start(bf16[24,3072]{1,0:T(8,128)(2,1)S(1)} %pad_maximum_fusion.7), channel_id=1, source_target_pairs={{0,2},{1,3},{2,4},{3,5},{4,6},{5,7},{6,0},{7,1},{8,10},{9,11},{10,... | collective-permute-start | bytes 442376 | tf_op jit(solution)/shard_map/ppermute | solution.py:61
  93.2 145.3 %all-gather.8.cloned.1.call-start = ((), (), s32[]{:S(2)}) async-start(), calls=%async_computation.5 | async-start | bytes 5898240 | tf_op jit(solution)/shard_map/all_gather | solution.py:1455
  123.9 313.6 %reduce-scatter.4.cloned.1.call-start = ((), (), s32[]{:S(2)}) async-start(), calls=%async_computation.6 | async-start | bytes 5898240 | tf_op jit(solution)/shard_map/reduce_scatter | solution.py:1529
  124.1 41.8 %collective-permute-start.28 = (bf16[192,3072]{1,0:T(8,128)(2,1)}, bf16[192,3072]{1,0:T(8,128)(2,1)S(1)}, u32[]{:S(2)}, u32[]{:S(2)}) collective-permute-start(bf16[192,3072]{1,0:T(8,128)(2,1)} %maximum_select_fusion.refs_8_.refs_4_), channel_id=1, source_target_pairs={{0,16},{8,24},{16,0},{24,8},{1,17},{9,25},{17,1},{25,9},{2,18},{10... | collective-permute-start | bytes 3538952 | tf_op jit(solution)/shard_map/ppermute | solution.py:1226
  125.7 41.8 %collective-permute-start.29 = (bf16[192,3072]{1,0:T(8,128)(2,1)S(1)}, bf16[192,3072]{1,0:T(8,128)(2,1)S(1)}, u32[]{:S(2)}, u32[]{:S(2)}) collective-permute-start(bf16[192,3072]{1,0:T(8,128)(2,1)S(1)} %maximum_select_fusion.1.refs_12_.refs_8_), channel_id=1, source_target_pairs={{0,8},{8,0},{16,24},{24,16},{1,9},{9,1},{17,25},{25,17},{2,10},{10... | collective-permute-start | bytes 3538952 | tf_op jit(solution)/shard_map/ppermute | solution.py:1226
  127.1 59.2 %collective-permute-start.34 = (bf16[192,1536]{1,0:T(8,128)(2,1)S(1)}, bf16[192,1536]{1,0:T(8,128)(2,1)S(1)}, u32[]{:S(2)}, u32[]{:S(2)}) collective-permute-start(bf16[192,1536]{1,0:T(8,128)(2,1)S(1)} %maximum_select_fusion.4.rest_0_.refs_4_), channel_id=1, source_target_pairs={{0,16},{8,24},{16,0},{24,8},{1,17},{9,25},{17,1},{25,9},{2,18},{10... | collective-permute-start | bytes 1769480 | tf_op jit(solution)/shard_map/ppermute | solution.py:1226
  127.7 60.9 %collective-permute-start.35 = (bf16[192,1536]{1,0:T(8,128)(2,1)S(1)}, bf16[192,1536]{1,0:T(8,128)(2,1)S(1)}, u32[]{:S(2)}, u32[]{:S(2)}) collective-permute-start(bf16[192,1536]{1,0:T(8,128)(2,1)S(1)} %maximum_select_fusion.5.rest_4_.refs_4_.refs_0_.refs_8_), channel_id=1, source_target_pairs={{0,8},{8,0},{16,24},{24,16},{1,9},{9,1},{17,25},{25,17},{2,10},{10... | collective-permute-start | bytes 1769480 | tf_op jit(solution)/shard_map/ppermute | solution.py:1226
  128.2 39.2 %collective-permute-start.25 = (bf16[128,192]{1,0:T(8,128)(2,1)S(1)}, bf16[128,192]{1,0:T(8,128)(2,1)S(1)}, u32[]{:S(2)}, u32[]{:S(2)}) collective-permute-start(bf16[128,192]{1,0:T(8,128)(2,1)S(1)} %copy-done.85), channel_id=1, source_target_pairs={{0,6},{1,7},{2,0},{3,1},{4,2},{5,3},{6,4},{7,5},{8,14},{9,15},{10,... | collective-permute-start | bytes 147464 | tf_op jit(solution)/shard_map/ppermute | solution.py:61
  167.4 27.2 %collective-permute-start.30 = (bf16[192,3072]{1,0:T(8,128)(2,1)}, bf16[192,3072]{1,0:T(8,128)(2,1)S(1)}, u32[]{:S(2)}, u32[]{:S(2)}) collective-permute-start(bf16[192,3072]{1,0:T(8,128)(2,1)} %maximum_select_fusion.refs_8_.refs_4_), channel_id=1, source_target_pairs={{0,1},{1,0},{2,3},{3,2},{4,5},{5,4},{6,7},{7,6},{8,9},{9,8},{10,11... | collective-permute-start | bytes 3538952 | tf_op jit(solution)/shard_map/ppermute | solution.py:54
  167.5 27.7 %collective-permute-start.32 = (bf16[192,3072]{1,0:T(8,128)(2,1)S(1)}, bf16[192,3072]{1,0:T(8,128)(2,1)S(1)}, u32[]{:S(2)}, u32[]{:S(2)}) collective-permute-start(bf16[192,3072]{1,0:T(8,128)(2,1)S(1)} %maximum_select_fusion.1.refs_12_.refs_8_), channel_id=1, source_target_pairs={{0,1},{1,0},{2,3},{3,2},{4,5},{5,4},{6,7},{7,6},{8,9},{9,8},{10,11... | collective-permute-start | bytes 3538952 | tf_op jit(solution)/shard_map/ppermute | solution.py:54
  171.8 23.5 %collective-permute-start.31 = (bf16[192,3072]{1,0:T(8,128)(2,1)S(1)}, bf16[192,3072]{1,0:T(8,128)(2,1)S(1)}, u32[]{:S(2)}, u32[]{:S(2)}) collective-permute-start(bf16[192,3072]{1,0:T(8,128)(2,1)S(1)} %collective-permute-done.28.refs_9_.refs_5_), channel_id=1, source_target_pairs={{0,1},{1,0},{2,3},{3,2},{4,5},{5,4},{6,7},{7,6},{8,9},{9,8},{10,11... | collective-permute-start | bytes 3538952 | tf_op jit(solution)/shard_map/ppermute | solution.py:54
  194.7 13.7 %collective-permute-start.36 = (bf16[192,1536]{1,0:T(8,128)(2,1)S(1)}, bf16[192,1536]{1,0:T(8,128)(2,1)S(1)}, u32[]{:S(2)}, u32[]{:S(2)}) collective-permute-start(bf16[192,1536]{1,0:T(8,128)(2,1)S(1)} %maximum_select_fusion.4.rest_0_.refs_4_), channel_id=1, source_target_pairs={{0,1},{1,0},{2,3},{3,2},{4,5},{5,4},{6,7},{7,6},{8,9},{9,8},{10,11... | collective-permute-start | bytes 1769480 | tf_op jit(solution)/shard_map/ppermute | solution.py:54
  194.7 13.7 %collective-permute-start.38 = (bf16[192,1536]{1,0:T(8,128)(2,1)S(1)}, bf16[192,1536]{1,0:T(8,128)(2,1)S(1)}, u32[]{:S(2)}, u32[]{:S(2)}) collective-permute-start(bf16[192,1536]{1,0:T(8,128)(2,1)S(1)} %maximum_select_fusion.5.rest_4_.refs_4_.refs_0_.refs_8_), channel_id=1, source_target_pairs={{0,1},{1,0},{2,3},{3,2},{4,5},{5,4},{6,7},{7,6},{8,9},{9,8},{10,11... | collective-permute-start | bytes 1769480 | tf_op jit(solution)/shard_map/ppermute | solution.py:54
  195.2 13.2 %collective-permute-start.37 = (bf16[192,1536]{1,0:T(8,128)(2,1)S(1)}, bf16[192,1536]{1,0:T(8,128)(2,1)S(1)}, u32[]{:S(2)}, u32[]{:S(2)}) collective-permute-start(bf16[192,1536]{1,0:T(8,128)(2,1)S(1)} %collective-permute-done.34.rest_1_.refs_5_), channel_id=1, source_target_pairs={{0,1},{1,0},{2,3},{3,2},{4,5},{5,4},{6,7},{7,6},{8,9},{9,8},{10,11... | collective-permute-start | bytes 1769480 | tf_op jit(solution)/shard_map/ppermute | solution.py:54
  214.9 15.3 %collective-permute-start.41 = (bf16[128,576]{1,0:T(8,128)(2,1)}, bf16[128,576]{1,0:T(8,128)(2,1)S(1)}, u32[]{:S(2)}, u32[]{:S(2)}) collective-permute-start(bf16[128,576]{1,0:T(8,128)(2,1)} %get-tuple-element.189), channel_id=1, source_target_pairs={{0,4},{1,5},{2,6},{3,7},{4,0},{5,1},{6,2},{7,3},{8,12},{9,13},{10,... | collective-permute-start | bytes 442376 | tf_op jit(solution)/shard_map/ppermute | solution.py:61
  215.1 15.1 %collective-permute-start.42 = (bf16[128,576]{1,0:T(8,128)(2,1)}, bf16[128,576]{1,0:T(8,128)(2,1)S(1)}, u32[]{:S(2)}, u32[]{:S(2)}) collective-permute-start(bf16[128,576]{1,0:T(8,128)(2,1)} %get-tuple-element.190), channel_id=1, source_target_pairs={{0,6},{1,7},{2,0},{3,1},{4,2},{5,3},{6,4},{7,5},{8,14},{9,15},{10,... | collective-permute-start | bytes 442376 | tf_op jit(solution)/shard_map/ppermute | solution.py:61
  286.3 187.0 %reduce-scatter.6.cloned.1.call-start = ((), (), s32[]{:S(2)}) async-start(), calls=%async_computation.7 | async-start | bytes 5898240 | tf_op jit(solution)/shard_map/reduce_scatter | solution.py:1490
  302.4 16.9 %collective-permute-start.60 = (bf16[128,576]{1,0:T(8,128)(2,1)}, bf16[128,576]{1,0:T(8,128)(2,1)S(1)}, u32[]{:S(2)}, u32[]{:S(2)}) collective-permute-start(bf16[128,576]{1,0:T(8,128)(2,1)} %get-tuple-element.228), channel_id=1, source_target_pairs={{0,6},{1,7},{2,0},{3,1},{4,2},{5,3},{6,4},{7,5},{8,14},{9,15},{10,... | collective-permute-start | bytes 442376 | tf_op jit(solution)/shard_map/ppermute | solution.py:61
  303.8 15.5 %collective-permute-start.61 = (bf16[128,576]{1,0:T(8,128)(2,1)}, bf16[128,576]{1,0:T(8,128)(2,1)S(1)}, u32[]{:S(2)}, u32[]{:S(2)}) collective-permute-start(bf16[128,576]{1,0:T(8,128)(2,1)} %get-tuple-element.229), channel_id=1, source_target_pairs={{0,4},{1,5},{2,6},{3,7},{4,0},{5,1},{6,2},{7,3},{8,12},{9,13},{10,... | collective-permute-start | bytes 442376 | tf_op jit(solution)/shard_map/ppermute | solution.py:61
  304.7 14.6 %collective-permute-start.62 = (bf16[128,576]{1,0:T(8,128)(2,1)}, bf16[128,576]{1,0:T(8,128)(2,1)S(1)}, u32[]{:S(2)}, u32[]{:S(2)}) collective-permute-start(bf16[128,576]{1,0:T(8,128)(2,1)} %get-tuple-element.230), channel_id=1, source_target_pairs={{0,2},{1,3},{2,4},{3,5},{4,6},{5,7},{6,0},{7,1},{8,10},{9,11},{10,... | collective-permute-start | bytes 442376 | tf_op jit(solution)/shard_map/ppermute | solution.py:61
  306.6 47.3 %collective-permute-start.63 = (bf16[128,2688]{1,0:T(8,128)(2,1)S(1)}, bf16[128,2688]{1,0:T(8,128)(2,1)S(1)}, u32[]{:S(2)}, u32[]{:S(2)}) collective-permute-start(bf16[128,2688]{1,0:T(8,128)(2,1)S(1)} %copy-done.53), channel_id=1, source_target_pairs={{0,1},{1,0},{2,3},{3,2},{4,5},{5,4},{6,7},{7,6},{8,9},{9,8},{10,11... | collective-permute-start | bytes 2064392 | tf_op jit(solution)/shard_map/ppermute | solution.py:54
  319.3 25.4 %collective-permute-start.66 = (bf16[128,768]{1,0:T(8,128)(2,1)S(1)}, bf16[128,768]{1,0:T(8,128)(2,1)S(1)}, u32[]{:S(2)}, u32[]{:S(2)}) collective-permute-start(bf16[128,768]{1,0:T(8,128)(2,1)S(1)} %copy-done.63), channel_id=1, source_target_pairs={{0,1},{1,0},{2,3},{3,2},{4,5},{5,4},{6,7},{7,6},{8,9},{9,8},{10,11... | collective-permute-start | bytes 589832 | tf_op jit(solution)/shard_map/ppermute | solution.py:54
  326.7 21.8 %collective-permute-start.65 = (bf16[128,2304]{1,0:T(8,128)(2,1)}, bf16[128,2304]{1,0:T(8,128)(2,1)S(1)}, u32[]{:S(2)}, u32[]{:S(2)}) collective-permute-start(bf16[128,2304]{1,0:T(8,128)(2,1)} %get-tuple-element.246.project), channel_id=1, source_target_pairs={{0,1},{1,0},{2,3},{3,2},{4,5},{5,4},{6,7},{7,6},{8,9},{9,8},{10,11... | collective-permute-start | bytes 1769480 | tf_op jit(solution)/shard_map/ppermute | solution.py:54
  327.3 18.2 %collective-permute-start.67 = (f32[16,768]{1,0:T(8,128)}, f32[16,768]{1,0:T(8,128)S(1)}, u32[]{:S(2)}, u32[]{:S(2)}) collective-permute-start(f32[16,768]{1,0:T(8,128)} %get-tuple-element.248.vector), channel_id=1, source_target_pairs={{0,1},{1,0},{2,3},{3,2},{4,5},{5,4},{6,7},{7,6},{8,9},{9,8},{10,11... | collective-permute-start | bytes 147464 | tf_op jit(solution)/shard_map/ppermute | solution.py:54
  344.6 16.7 %collective-permute-start.69 = (bf16[128,192]{1,0:T(8,128)(2,1)}, bf16[128,192]{1,0:T(8,128)(2,1)S(1)}, u32[]{:S(2)}, u32[]{:S(2)}) collective-permute-start(bf16[128,192]{1,0:T(8,128)(2,1)} %get-tuple-element.252), channel_id=1, source_target_pairs={{0,2},{1,3},{2,4},{3,5},{4,6},{5,7},{6,0},{7,1},{8,10},{9,11},{10,... | collective-permute-start | bytes 147464 | tf_op jit(solution)/shard_map/ppermute | solution.py:61
  345.5 15.8 %collective-permute-start.70 = (bf16[128,192]{1,0:T(8,128)(2,1)}, bf16[128,192]{1,0:T(8,128)(2,1)S(1)}, u32[]{:S(2)}, u32[]{:S(2)}) collective-permute-start(bf16[128,192]{1,0:T(8,128)(2,1)} %get-tuple-element.253), channel_id=1, source_target_pairs={{0,4},{1,5},{2,6},{3,7},{4,0},{5,1},{6,2},{7,3},{8,12},{9,13},{10,... | collective-permute-start | bytes 147464 | tf_op jit(solution)/shard_map/ppermute | solution.py:61
  353.9 39.8 %collective-permute-start.74 = (bf16[192,1664]{1,0:T(8,128)(2,1)}, bf16[192,1664]{1,0:T(8,128)(2,1)S(1)}, u32[]{:S(2)}, u32[]{:S(2)}) collective-permute-start(bf16[192,1664]{1,0:T(8,128)(2,1)} %get-tuple-element.262), channel_id=1, source_target_pairs={{0,16},{8,24},{16,0},{24,8},{1,17},{9,25},{17,1},{25,9},{2,18},{10... | collective-permute-start | bytes 1916936 | tf_op jit(solution)/shard_map/ppermute | solution.py:1226
  370.4 23.3 %collective-permute-start.73 = (bf16[192,1536]{1,0:T(8,128)(2,1)S(1)}, bf16[192,1536]{1,0:T(8,128)(2,1)S(1)}, u32[]{:S(2)}, u32[]{:S(2)}) collective-permute-start(bf16[192,1536]{1,0:T(8,128)(2,1)S(1)} %copy-done.58), channel_id=1, source_target_pairs={{0,8},{8,0},{16,24},{24,16},{1,9},{9,1},{17,25},{25,17},{2,10},{10... | collective-permute-start | bytes 1769480 | tf_op jit(solution)/shard_map/ppermute | solution.py:1226
  373.7 131.6 %reduce-scatter.8.cloned.1.call-start = ((), (), s32[]{:S(2)}) async-start(), calls=%async_computation.8 | async-start | bytes 1474560 | tf_op jit(solution)/shard_map/reduce_scatter | solution.py:1491
  376.7 20.8 %collective-permute-start.76 = (bf16[128,576]{1,0:T(8,128)(2,1)}, bf16[128,576]{1,0:T(8,128)(2,1)S(1)}, u32[]{:S(2)}, u32[]{:S(2)}) collective-permute-start(bf16[128,576]{1,0:T(8,128)(2,1)} %get-tuple-element.266), channel_id=1, source_target_pairs={{0,6},{1,7},{2,0},{3,1},{4,2},{5,3},{6,4},{7,5},{8,14},{9,15},{10,... | collective-permute-start | bytes 442376 | tf_op jit(solution)/shard_map/ppermute | solution.py:61
  377.3 20.2 %collective-permute-start.77 = (bf16[128,576]{1,0:T(8,128)(2,1)}, bf16[128,576]{1,0:T(8,128)(2,1)S(1)}, u32[]{:S(2)}, u32[]{:S(2)}) collective-permute-start(bf16[128,576]{1,0:T(8,128)(2,1)} %get-tuple-element.267), channel_id=1, source_target_pairs={{0,4},{1,5},{2,6},{3,7},{4,0},{5,1},{6,2},{7,3},{8,12},{9,13},{10,... | collective-permute-start | bytes 442376 | tf_op jit(solution)/shard_map/ppermute | solution.py:61
  379.0 18.6 %collective-permute-start.78 = (bf16[128,576]{1,0:T(8,128)(2,1)}, bf16[128,576]{1,0:T(8,128)(2,1)S(1)}, u32[]{:S(2)}, u32[]{:S(2)}) collective-permute-start(bf16[128,576]{1,0:T(8,128)(2,1)} %get-tuple-element.268), channel_id=1, source_target_pairs={{0,2},{1,3},{2,4},{3,5},{4,6},{5,7},{6,0},{7,1},{8,10},{9,11},{10,... | collective-permute-start | bytes 442376 | tf_op jit(solution)/shard_map/ppermute | solution.py:61
  421.8 15.5 %collective-permute-start.87 = (bf16[24,3200]{1,0:T(8,128)(2,1)}, bf16[24,3200]{1,0:T(8,128)(2,1)S(1)}, u32[]{:S(2)}, u32[]{:S(2)}) collective-permute-start(bf16[24,3200]{1,0:T(8,128)(2,1)} %get-tuple-element.285), channel_id=1, source_target_pairs={{0,4},{1,5},{2,6},{3,7},{4,0},{5,1},{6,2},{7,3},{8,12},{9,13},{10,... | collective-permute-start | bytes 460808 | tf_op jit(solution)/shard_map/ppermute | solution.py:61
  423.4 13.9 %collective-permute-start.86 = (bf16[24,3200]{1,0:T(8,128)(2,1)}, bf16[24,3200]{1,0:T(8,128)(2,1)S(1)}, u32[]{:S(2)}, u32[]{:S(2)}) collective-permute-start(bf16[24,3200]{1,0:T(8,128)(2,1)} %get-tuple-element.284), channel_id=1, source_target_pairs={{0,2},{1,3},{2,4},{3,5},{4,6},{5,7},{6,0},{7,1},{8,10},{9,11},{10,... | collective-permute-start | bytes 460808 | tf_op jit(solution)/shard_map/ppermute | solution.py:61
  430.4 19.2 %collective-permute-start.84 = (bf16[192,1536]{1,0:T(8,128)(2,1)}, bf16[192,1536]{1,0:T(8,128)(2,1)S(1)}, u32[]{:S(2)}, u32[]{:S(2)}) collective-permute-start(bf16[192,1536]{1,0:T(8,128)(2,1)} %get-tuple-element.280), channel_id=1, source_target_pairs={{0,8},{8,0},{16,24},{24,16},{1,9},{9,1},{17,25},{25,17},{2,10},{10... | collective-permute-start | bytes 1769480 | tf_op jit(solution)/shard_map/ppermute | solution.py:1226
  432.0 18.7 %collective-permute-start.85 = (bf16[192,1664]{1,0:T(8,128)(2,1)S(1)}, bf16[192,1664]{1,0:T(8,128)(2,1)S(1)}, u32[]{:S(2)}, u32[]{:S(2)}) collective-permute-start(bf16[192,1664]{1,0:T(8,128)(2,1)S(1)} %copy-done.56), channel_id=1, source_target_pairs={{0,16},{8,24},{16,0},{24,8},{1,17},{9,25},{17,1},{25,9},{2,18},{10... | collective-permute-start | bytes 1916936 | tf_op jit(solution)/shard_map/ppermute | solution.py:1226
  438.7 17.6 %collective-permute-start.91 = (bf16[24,6144]{1,0:T(8,128)(2,1)S(1)}, bf16[24,6144]{1,0:T(8,128)(2,1)S(1)}, u32[]{:S(2)}, u32[]{:S(2)}) collective-permute-start(bf16[24,6144]{1,0:T(8,128)(2,1)S(1)} %get-tuple-element.315), channel_id=1, source_target_pairs={{0,6},{1,7},{2,0},{3,1},{4,2},{5,3},{6,4},{7,5},{8,14},{9,15},{10,... | collective-permute-start | bytes 884744 | tf_op jit(solution)/shard_map/ppermute | solution.py:61
  438.7 27.5 %collective-permute-start.90 = (bf16[24,6144]{1,0:T(8,128)(2,1)S(1)}, bf16[24,6144]{1,0:T(8,128)(2,1)S(1)}, u32[]{:S(2)}, u32[]{:S(2)}) collective-permute-start(bf16[24,6144]{1,0:T(8,128)(2,1)S(1)} %get-tuple-element.316), channel_id=1, source_target_pairs={{0,4},{1,5},{2,6},{3,7},{4,0},{5,1},{6,2},{7,3},{8,12},{9,13},{10,... | collective-permute-start | bytes 884744 | tf_op jit(solution)/shard_map/ppermute | solution.py:61
  440.1 26.1 %collective-permute-start.89 = (bf16[24,6144]{1,0:T(8,128)(2,1)S(1)}, bf16[24,6144]{1,0:T(8,128)(2,1)S(1)}, u32[]{:S(2)}, u32[]{:S(2)}) collective-permute-start(bf16[24,6144]{1,0:T(8,128)(2,1)S(1)} %get-tuple-element.314), channel_id=1, source_target_pairs={{0,2},{1,3},{2,4},{3,5},{4,6},{5,7},{6,0},{7,1},{8,10},{9,11},{10,... | collective-permute-start | bytes 884744 | tf_op jit(solution)/shard_map/ppermute | solution.py:61
  470.5 22.2 %collective-permute-start.95 = (bf16[24,3200]{1,0:T(8,128)(2,1)}, bf16[24,3200]{1,0:T(8,128)(2,1)S(1)}, u32[]{:S(2)}, u32[]{:S(2)}) collective-permute-start(bf16[24,3200]{1,0:T(8,128)(2,1)} %get-tuple-element.294), channel_id=1, source_target_pairs={{0,4},{1,5},{2,6},{3,7},{4,0},{5,1},{6,2},{7,3},{8,12},{9,13},{10,... | collective-permute-start | bytes 460808 | tf_op jit(solution)/shard_map/ppermute | solution.py:61
  471.1 21.5 %collective-permute-start.94 = (bf16[24,3200]{1,0:T(8,128)(2,1)}, bf16[24,3200]{1,0:T(8,128)(2,1)S(1)}, u32[]{:S(2)}, u32[]{:S(2)}) collective-permute-start(bf16[24,3200]{1,0:T(8,128)(2,1)} %get-tuple-element.293), channel_id=1, source_target_pairs={{0,2},{1,3},{2,4},{3,5},{4,6},{5,7},{6,0},{7,1},{8,10},{9,11},{10,... | collective-permute-start | bytes 460808 | tf_op jit(solution)/shard_map/ppermute | solution.py:61
  (153 other events, 1343.3 us)
Sparse Core Ops, SparseCore 0:
  29.5 30.9 all-gather.3
  93.3 30.5 all-gather.5
  125.7 77.6 all-gather.7
  286.4 56.7 reduce-scatter.3
  373.8 68.8 reduce-scatter.5
  473.5 31.7 reduce-scatter.7

commit v3 on v2

--- a/solution.py
+++ b/solution.py
@@ -458,7 +458,7 @@
 VMEM_BYTES = 56 * 1024 * 1024
 HINT = 4
 SIDE_HINT = 40
-SIDE = ("feed_terms", "attend_terms", "fold", "split", "input_back")
+SIDE = ("feed_terms", "attend_terms", "slice_terms", "fold", "split", "input_back")
 
 
 def shape(dims, kind):
@@ -556,20 +556,36 @@
     return jnp.sum(values, 0, keepdims=True)
 
 
-def fetch_project(pieces, weight, left_sems, right_sems, width):
+def fetch_project(layer, pieces, weight, left_sems, right_sems, width):
+    if len(pieces) == 2:
+        every = slice(0, 3 * width)
+        return fetch_whole(pieces, weight, left_sems, every, every)
     first, last = slice(0, 2 * width), slice(2 * width, 3 * width)
     copies = fetch_left(pieces[:4], weight, left_sems, first, first)
     return copies + fetch_right(pieces[4:], weight, right_sems, slice(0, width), last)
 
 
-def project_kernel(first, chips, source, perm, bias, *rest):
-    pieces, low_out, rest = rest[:8], rest[8], rest[9:]
-    outs, (weight, stage, left_sems, right_sems) = rest[:chips], rest[chips:]
+def plain_rows(columns, perm):
+    return lax.dot_general(
+        columns, perm, (((0,), (1,)), ((), ())), preferred_element_type=F32
+    )
+
+
+def project_kernel(layer, chips, many, source, perm, bias, *rest):
+    pieces, low_out, rest = rest[:many], rest[many], rest[many + 1 :]
+    outs, (weight, stage, columns, *sems) = rest[:chips], rest[chips:]
+    left_sems, right_sems, column_sems = sems
     chip, _ = spot_in()
     width = perm.shape[0]
-    copies = fetch_project(pieces, weight, left_sems, right_sems, width)
-    if first:
+    copies = fetch_project(layer, pieces, weight, left_sems, right_sems, width)
+    if layer == 0:
+        start = pieces[4].shape[1] - LANES
+        column_copies = fetch_right(
+            pieces[4:], columns, column_sems, slice(start, start + LANES), slice(0, LANES)
+        )
         low = matmul(source[...], perm[...]).astype(BF)
+        wait_all(column_copies)
+        bias = plain_rows(columns[...], perm[...])
     else:
         low = source[...].astype(BF)
     low_out[...] = low
@@ -590,11 +606,11 @@
         outs[step][...] = stage[lax.rem(chip + step, chips)]
 
 
-def project_fast(first, chips, source, perm, bias, pieces):
+def project_fast(layer, chips, source, perm, bias, pieces):
     rows, width = source.shape
     group = 3 * width // chips
     out = run(
-        functools.partial(project_kernel, first, chips),
+        functools.partial(project_kernel, layer, chips, len(pieces)),
         "project",
         [shape((rows, width), BF)] + [shape((rows, group), BF)] * chips,
         [source, perm, bias],
@@ -602,7 +618,9 @@
         [
             pltpu.VMEM((width, 3 * width), BF),
             pltpu.VMEM((chips, rows, group), BF),
+            pltpu.VMEM((width, LANES), BF),
             pltpu.SemaphoreType.DMA((4,)),
+            pltpu.SemaphoreType.DMA((8,)),
             pltpu.SemaphoreType.DMA((8,)),
         ],
         flops=6 * rows * width * width,
@@ -693,21 +711,14 @@
 def fetch_feed(weights, mixer, expand, shrink, sems):
     width, wide = expand.shape
     every, full = slice(0, width), slice(0, wide)
-    mixer_copies = fetch_right(weights[:4], mixer, sems[0], slice(width, 2 * width), every)
-    if len(weights) == 6:
-        return (
-            mixer_copies,
-            fetch_whole(weights[4:], expand, sems[1], full, full),
-            fetch_whole(weights[4:], shrink, sems[2], slice(wide, 2 * wide), full),
-        )
     return (
-        mixer_copies,
-        fetch_left(weights[4:8], expand, sems[1], full, full),
-        fetch_right(weights[8:], shrink, sems[2], full, full),
-    )
-
-
-def feed_kernel(chips, many, hidden, low, perm, rows_in, wide_bias, *refs):
+        fetch_right(weights[:4], mixer, sems[0], slice(width, 2 * width), every),
+        fetch_whole(weights[4:], expand, sems[1], full, full),
+        fetch_whole(weights[4:], shrink, sems[2], slice(wide, 2 * wide), full),
+    )
+
+
+def feed_kernel(layer, chips, many, hidden, low, perm, rows_in, wide_bias, *refs):
     pieces, refs = refs[:chips], refs[chips:]
     weights, refs = refs[:many], refs[many:]
     (out, attended, normed_low, pre_out, act_out, hat_one, scale_one, hat_two, scale_two,
@@ -764,11 +775,11 @@
     sent[:, 3 * half :] = half_at(act_out, 1 - core)
 
 
-def feed_fast(chips, hidden, low, perm, vectors, wide_bias, pieces, weights):
+def feed_fast(layer, chips, hidden, low, perm, vectors, wide_bias, pieces, weights):
     rows, width = hidden.shape
     wide = wide_bias.shape[1]
     return run(
-        functools.partial(feed_kernel, chips, len(weights)),
+        functools.partial(feed_kernel, layer, chips, len(weights)),
         "feed",
         [
             shape((rows, width), F32),
@@ -805,7 +816,7 @@
 
 
 def feed_back_kernel(
-    first, chips, many, source, perm, perm_wide, vectors, hat_one, scale_one, hat_two, scale_two,
+    layer, chips, many, source, perm, perm_wide, vectors, hat_one, scale_one, hat_two, scale_two,
     pre_in, *refs
 ):
     weights, refs = refs[:many], refs[many:]
@@ -820,7 +831,7 @@
     mixer_copies, expand_copies, shrink_copies = fetch_feed(
         weights, mixer, expand, shrink, sems
     )
-    grad = matmul(source[...], perm[...]) if first else source[...]
+    grad = matmul(source[...], perm[...]) if layer == LAYERS - 1 else source[...]
     hat = hat_two[...]
     sums[...] = jnp.zeros_like(sums)
     sums[10:11, :] = column_sum(grad * hat)
@@ -876,11 +887,11 @@
         outs[step][...] = stage[lax.rem(chip + step, chips)]
 
 
-def feed_back_fast(first, chips, source, perm, perm_wide, vectors, saved, weights):
+def feed_back_fast(layer, chips, source, perm, perm_wide, vectors, saved, weights):
     rows, width = source.shape
     wide = saved[-1].shape[1]
     out = run(
-        functools.partial(feed_back_kernel, first, chips, len(weights)),
+        functools.partial(feed_back_kernel, layer, chips, len(weights)),
         "feed_back",
         [
             shape((rows, width), F32),
@@ -904,6 +915,343 @@
         flops=4 * rows * width * (wide + 2 * width),
     )
     return out[0], out[1], out[2], out[3], out[4:]
+
+
+def fetch_rows(pieces, target, sems, start):
+    _, core = spot_in()
+    rows, width = pieces[0].shape[0], target.shape[1]
+    copies = []
+    for index, piece in enumerate(pieces):
+        part = core if index == 0 else 1 - core
+        for block in range(4):
+            goal = pl.multiple_of((part * 4 + block) * rows, 16)
+            copy = pltpu.make_async_copy(
+                piece.at[:, start + block * width : start + (block + 1) * width],
+                target.at[pl.ds(goal, rows), :],
+                sems.at[4 * index + block],
+            )
+            copy.start()
+            copies.append(copy)
+    return copies
+
+
+def fetch_blocks(pieces, target, sems):
+    _, core = spot_in()
+    spot = lax.axis_index("dp")
+    rows, width = pieces[0].shape[0], target.shape[1]
+    copies = []
+    for index, piece in enumerate(pieces):
+        part = core if index == 0 else 1 - core
+        for bits in range(4):
+            goal = pl.multiple_of((part * 4 + jnp.bitwise_xor(spot, bits)) * rows, 16)
+            copy = pltpu.make_async_copy(
+                piece.at[:, bits * width : (bits + 1) * width],
+                target.at[pl.ds(goal, rows), :],
+                sems.at[4 * index + bits],
+            )
+            copy.start()
+            copies.append(copy)
+    return copies
+
+
+def mix_kernel(chips, hidden, low, perm, rows_in, *refs):
+    pieces, refs = refs[:chips], refs[chips:]
+    weights, refs = refs[:4], refs[4:]
+    attended, normed_out, normed_low, hat_one, scale_one, sent, squares = refs[:7]
+    stage, mixer, sems = refs[7:]
+    chip, core = spot_in()
+    width = perm.shape[0]
+    group = width // chips
+    half = width // 2
+    copies = fetch_right(weights, mixer, sems, slice(width, 2 * width), slice(0, width))
+    for step in range(chips):
+        stage[lax.rem(chip + step, chips)] = pieces[step][...]
+    moved = matmul(stage[0], perm[:group, :])
+    for index in range(1, chips):
+        moved += matmul(stage[index], perm[index * group : (index + 1) * group, :])
+    moved = moved.astype(BF)
+    attended[...] = moved
+    wait_all(copies)
+    attn_out = matmul(moved, mixer[...]) + rows_in[2:3]
+    start = hidden[...].astype(F32)
+    hat, scale = norm_in(start + attn_out)
+    hat_one[...] = hat
+    scale_one[...] = jnp.broadcast_to(scale, scale_one.shape)
+    normed = hat * rows_in[3:4] + rows_in[4:5]
+    normed_out[...] = normed
+    normed_low[...] = normed.astype(BF)
+    squares[...] = jnp.zeros_like(squares)
+    squares[0:1, :] = column_sum(start * start)
+    squares[1:2, :] = column_sum(attn_out * attn_out)
+    sent[:, :half] = half_at(low, 1 - core)
+    sent[:, half:] = half_at(attended, 1 - core)
+
+
+def mix_fast(chips, hidden, low, perm, vectors, pieces, weights):
+    rows, width = hidden.shape
+    return run(
+        functools.partial(mix_kernel, chips),
+        "mix",
+        [
+            shape((rows, width), BF),
+            shape((rows, width), F32),
+            shape((rows, width), BF),
+            shape((rows, width), F32),
+            shape((rows, LANES), F32),
+            shape((rows, width), BF),
+            shape((8, width), F32),
+        ],
+        [hidden, low, perm, vectors, *pieces],
+        weights,
+        [
+            pltpu.VMEM((chips, rows, width // chips), BF),
+            pltpu.VMEM((width, width), BF),
+            pltpu.SemaphoreType.DMA((8,)),
+        ],
+        flops=4 * rows * width * width,
+    )
+
+
+def slice_row(wide_bias):
+    spot = lax.axis_index("dp")
+    line = lax.broadcasted_iota(jnp.int32, wide_bias.shape, 0)
+    return jnp.sum(jnp.where(line == spot, wide_bias[...], 0.0), 0, keepdims=True)
+
+
+def slice_feed_kernel(wide_bias, *refs):
+    peers = 4
+    blocks, weights, refs = refs[:peers], refs[peers : peers + 2], refs[peers + 2 :]
+    near, sends, refs = refs[0], refs[1:peers], refs[peers:]
+    pre_out, act_out, expand, shrink, expand_sems, shrink_sems = refs
+    rows, width = blocks[0].shape
+    expand_copies = fetch_blocks(weights, expand, expand_sems)
+    shrink_copies = fetch_rows(weights, shrink, shrink_sems, 4 * width)
+    bias = slice_row(wide_bias)
+    wait_all(expand_copies)
+    tokens = jnp.concatenate([block[...] for block in blocks], 0)
+    pre = matmul(tokens, expand[...]) + bias
+    pre_out[...] = pre
+    act = (0.5 * pre * (1.0 + lax.erf(pre * ROOT_HALF))).astype(BF)
+    act_out[...] = act
+    wait_all(shrink_copies)
+    part = matmul(act, shrink[...])
+    near[...] = part[:rows]
+    for index, out in enumerate(sends):
+        out[...] = part[(index + 1) * rows : (index + 2) * rows].astype(BF)
+
+
+def slice_scratch(width):
+    return [
+        pltpu.VMEM((width, width), BF),
+        pltpu.VMEM((width, width), BF),
+        pltpu.SemaphoreType.DMA((8,)),
+        pltpu.SemaphoreType.DMA((8,)),
+    ]
+
+
+def slice_feed_fast(wide_bias, blocks, weights):
+    rows, width = blocks[0].shape
+    out = run(
+        slice_feed_kernel,
+        "slice_feed",
+        [shape((rows, width), F32)]
+        + [shape((rows, width), BF)] * 3
+        + [shape((4 * rows, width), F32), shape((4 * rows, width), BF)],
+        [wide_bias, *blocks],
+        weights,
+        slice_scratch(width),
+        flops=16 * rows * width * width,
+    )
+    return out[:4], out[4], out[5]
+
+
+def peer_sum(parts):
+    total = parts[0][...]
+    for part in parts[1:]:
+        total = total + part[...].astype(F32)
+    return total
+
+
+def finish_kernel(normed, rows_in, squares_in, *refs):
+    parts, (out, hat_two, scale_two, squares) = refs[:4], refs[4:]
+    ffn_out = peer_sum(parts) + rows_in[9:10]
+    squares[...] = squares_in[...]
+    squares[2:3, :] = column_sum(ffn_out * ffn_out)
+    hat, scale = norm_in(normed[...] + ffn_out)
+    hat_two[...] = hat
+    scale_two[...] = jnp.broadcast_to(scale, scale_two.shape)
+    out[...] = hat * rows_in[10:11] + rows_in[11:12]
+
+
+def finish_fast(normed, vectors, squares, parts):
+    rows, width = normed.shape
+    return run(
+        finish_kernel,
+        "finish",
+        [
+            shape((rows, width), F32),
+            shape((rows, width), F32),
+            shape((rows, LANES), F32),
+            shape(squares.shape, F32),
+        ],
+        [normed, vectors, squares, *parts],
+    )
+
+
+def finish_back_kernel(first, source, perm, vectors, hat_two, scale_two, grad_out, low_out, sums):
+    grad = matmul(source[...], perm[...]) if first else source[...]
+    hat = hat_two[...]
+    sums[...] = jnp.zeros_like(sums)
+    sums[10:11, :] = column_sum(grad * hat)
+    sums[11:12, :] = column_sum(grad)
+    grad_two = norm_back(grad * vectors[10:11], hat, scale_two[:, 0:1])
+    grad_out[...] = grad_two
+    low = grad_two.astype(BF)
+    low_out[...] = low
+    sums[9:10, :] = column_sum(low.astype(F32))
+
+
+def finish_back_fast(first, source, perm, vectors, hat_two, scale_two):
+    rows, width = source.shape
+    return run(
+        functools.partial(finish_back_kernel, first),
+        "finish_back",
+        [shape((rows, width), F32), shape((rows, width), BF), shape((16, width), F32)],
+        [source, perm, vectors, hat_two, scale_two],
+    )
+
+
+def slice_back_kernel(*refs):
+    peers = 4
+    blocks, refs = refs[:peers], refs[peers:]
+    inputs, refs = refs[:peers], refs[peers:]
+    pre_in, act_in, weights, refs = refs[0], refs[1], refs[2:4], refs[4:]
+    near, sends, refs = refs[0], refs[1:peers], refs[peers:]
+    slope_out, gave, sums, expand, shrink, expand_sems, shrink_sems = refs
+    _, core = spot_in()
+    rows, width = blocks[0].shape
+    half = width // 2
+    shrink_copies = fetch_rows(weights, shrink, shrink_sems, 4 * width)
+    expand_copies = fetch_blocks(weights, expand, expand_sems)
+    for index in range(peers):
+        span = slice(index * rows, (index + 1) * rows)
+        gave[span, :half] = half_at(inputs[index], 1 - core)
+        gave[span, width : 2 * width] = blocks[index][...]
+    gave[:, half:width] = half_at(act_in, 1 - core)
+    tokens = jnp.concatenate([block[...] for block in blocks], 0)
+    pre = pre_in[...]
+    slope = 0.5 * (1.0 + lax.erf(pre * ROOT_HALF)) + pre * (
+        jnp.exp(-0.5 * pre * pre) * ROOT_TAU
+    )
+    wait_all(shrink_copies)
+    grad_pre = (matmul_t(tokens, shrink[...]) * slope).astype(BF)
+    slope_out[...] = grad_pre
+    gave[:, 2 * width :] = grad_pre
+    sums[...] = jnp.broadcast_to(column_sum(grad_pre.astype(F32)), sums.shape)
+    wait_all(expand_copies)
+    part = matmul_t(grad_pre, expand[...])
+    near[...] = part[:rows]
+    for index, out in enumerate(sends):
+        out[...] = part[(index + 1) * rows : (index + 2) * rows].astype(BF)
+
+
+def slice_back_fast(blocks, inputs, pre, act, weights):
+    rows, width = blocks[0].shape
+    out = run(
+        slice_back_kernel,
+        "slice_back",
+        [shape((rows, width), F32)]
+        + [shape((rows, width), BF)] * 3
+        + [
+            shape((4 * rows, width), BF),
+            shape((4 * rows, 3 * width), BF),
+            shape((8, width), F32),
+        ],
+        [*blocks, *inputs, pre, act],
+        weights,
+        slice_scratch(width),
+        flops=16 * rows * width * width,
+    )
+    return out[:4], out[4], out[5], out[6]
+
+
+def slice_terms_kernel(peers, perm_rows, perm_units, *refs):
+    blocks, inputs, refs = refs[:peers], refs[peers : 2 * peers], refs[2 * peers :]
+    act_in, slope, theirs, out = refs
+    _, core = spot_in()
+    width = slope.shape[1]
+    half = width // 2
+    left = jnp.concatenate(
+        [half_at(member, core) for member in inputs] + [theirs[:, :half]], 0
+    )
+    left = matmul(left, perm_rows[...]).astype(BF)
+    right = jnp.concatenate([slope[...], theirs[:, 2 * width :]], 0)
+    out[:, :width] = grad_matmul(left, right).astype(BF)
+    left = jnp.concatenate([half_at(act_in, core), theirs[:, half:width]], 0)
+    left = matmul(left, perm_units[...]).astype(BF)
+    right = jnp.concatenate(
+        [block[...] for block in blocks] + [theirs[:, width : 2 * width]], 0
+    )
+    out[:, width:] = grad_matmul(left, right).astype(BF)
+
+
+def slice_terms_fast(perm_rows, perm_units, blocks, inputs, act, slope, theirs):
+    rows, width = blocks[0].shape
+    return run(
+        functools.partial(slice_terms_kernel, 4),
+        "slice_terms",
+        [shape((width // 2, 2 * width), BF)],
+        [perm_rows, perm_units, *blocks, *inputs, act, slope, theirs],
+        flops=16 * rows * width * width,
+    )[0]
+
+
+def mix_back_kernel(chips, grad_two, perm, vectors, hat_one, scale_one, sums_in, *refs):
+    parts, weights, refs = refs[:4], refs[4:8], refs[8:]
+    grad_one_out, attn_nat, sums = refs[:3]
+    outs = refs[3 : 3 + chips]
+    stage, mixer, sems = refs[3 + chips :]
+    chip, _ = spot_in()
+    width = perm.shape[0]
+    group = width // chips
+    copies = fetch_right(weights, mixer, sems, slice(width, 2 * width), slice(0, width))
+    grad_normed = grad_two[...] + peer_sum(parts)
+    hat = hat_one[...]
+    sums[...] = sums_in[...]
+    sums[3:4, :] = column_sum(grad_normed * hat)
+    sums[4:5, :] = column_sum(grad_normed)
+    grad_one = norm_back(grad_normed * vectors[3:4], hat, scale_one[:, 0:1])
+    grad_one_out[...] = grad_one
+    grad_attn = grad_one.astype(BF)
+    sums[2:3, :] = column_sum(grad_attn.astype(F32))
+    attn_nat[...] = matmul_t(grad_attn, perm[...]).astype(BF)
+    wait_all(copies)
+    grad_mixed = matmul_t(grad_attn, mixer[...]).astype(BF)
+    for index in range(chips):
+        stage[index] = matmul_t(
+            grad_mixed, perm[index * group : (index + 1) * group, :]
+        ).astype(BF)
+    for step in range(chips):
+        outs[step][...] = stage[lax.rem(chip + step, chips)]
+
+
+def mix_back_fast(chips, grad_two, perm, vectors, hat_one, scale_one, sums, parts, weights):
+    rows, width = grad_two.shape
+    out = run(
+        functools.partial(mix_back_kernel, chips),
+        "mix_back",
+        [shape((rows, width), F32), shape((rows, width), BF), shape((16, width), F32)]
+        + [shape((rows, width // chips), BF)] * chips,
+        [grad_two, perm, vectors, hat_one, scale_one, sums, *parts],
+        weights,
+        [
+            pltpu.VMEM((chips, rows, width // chips), BF),
+            pltpu.VMEM((width, width), BF),
+            pltpu.SemaphoreType.DMA((8,)),
+        ],
+        flops=6 * rows * width * width,
+    )
+    return out[0], out[1], out[2], out[3:]
 
 
 def attend_back_kernel(chips, *refs):
@@ -1016,31 +1364,31 @@
     return grad
 
 
-def project_back_kernel(chips, grad_one, perm, sums, *refs):
+def project_back_kernel(layer, chips, many, grad_one, perm, sums, *refs):
     pieces, refs = refs[:chips], refs[chips:]
-    weights, refs = refs[:8], refs[8:]
+    weights, refs = refs[:many], refs[many:]
     out, project, vector_out, stage, weight, left_sems, right_sems = refs
-    copies = fetch_project(weights, weight, left_sems, right_sems, perm.shape[0])
+    copies = fetch_project(layer, weights, weight, left_sems, right_sems, perm.shape[0])
     collect(chips, stage, pieces, project)
     wait_all(copies)
     out[...] = through_project(grad_one[...], project, weight)
     vector_rows(project, sums, perm, vector_out)
 
 
-def collect_kernel(chips, perm, sums, *refs):
+def collect_kernel(chips, perm, perm_wide, feed_sums, sums, *refs):
     pieces, refs = refs[:chips], refs[chips:]
     project, vector_out, stage = refs
     collect(chips, stage, pieces, project)
-    vector_rows(project, sums, perm, vector_out)
-
-
-def collect_fast(chips, perm, sums, pieces):
+    slice_vector_rows(project, sums, feed_sums, perm, perm_wide, vector_out)
+
+
+def collect_fast(chips, perm, perm_wide, feed_sums, sums, pieces):
     rows, group = pieces[0].shape
     return run(
         functools.partial(collect_kernel, chips),
         "collect",
         [shape((rows, chips * group), BF), shape(sums.shape, F32)],
-        [perm, sums, *pieces],
+        [perm, perm_wide, feed_sums, sums, *pieces],
         (),
         [pltpu.VMEM((chips, rows, group), BF)],
     )
@@ -1049,7 +1397,7 @@
 def input_back_kernel(grad_one, perm, project, *refs):
     weights, refs = refs[:8], refs[8:]
     out, weight, left_sems, right_sems = refs
-    wait_all(fetch_project(weights, weight, left_sems, right_sems, perm.shape[0]))
+    wait_all(fetch_project(0, weights, weight, left_sems, right_sems, perm.shape[0]))
     grad = through_project(grad_one[...], project, weight)
     out[...] = matmul_t(grad.astype(BF), perm[...]).astype(BF)
 
@@ -1069,6 +1417,29 @@
         ],
         flops=6 * rows * width * width,
     )[0]
+
+
+def exact_back(values, perm):
+    high = values.astype(BF)
+    rest = values - high.astype(F32)
+    middle = rest.astype(BF)
+    low = (rest - middle.astype(F32)).astype(BF)
+    return matmul_t(high, perm) + matmul_t(middle, perm) + matmul_t(low, perm)
+
+
+def slice_vector_rows(project, sums, feed_sums, perm, perm_wide, vector_out):
+    width = perm.shape[0]
+    spot = lax.axis_index("dp")
+    vector_out[...] = sums[...]
+    line = lax.broadcasted_iota(jnp.int32, (8, width), 0)
+    rows = exact_back(feed_sums[...], perm_wide[...])
+    first = column_sum(project[:, :width].astype(F32))
+    second = column_sum(project[:, 2 * width :].astype(F32))
+    rows = jnp.where(line == 0, first, jnp.where(line == 1, second, rows))
+    moved = exact_move(rows, perm[...])
+    vector_out[0:2, :] = moved[0:2, :]
+    wide_line = lax.broadcasted_iota(jnp.int32, (16, width), 0)
+    vector_out[...] = jnp.where(wide_line == 5 + spot, moved[2:3, :], vector_out[...])
 
 
 def vector_rows(project, sums, perm, vector_out):
@@ -1083,10 +1454,10 @@
     vector_out[8:9, :] = moved[0:1, :]
 
 
-def project_back_fast(chips, grad_one, perm, sums, pieces, weights):
+def project_back_fast(layer, chips, grad_one, perm, sums, pieces, weights):
     rows, width = grad_one.shape
     return run(
-        functools.partial(project_back_kernel, chips),
+        functools.partial(project_back_kernel, layer, chips, len(weights)),
         "project_back",
         [
             shape((rows, width), F32),
@@ -1209,6 +1580,12 @@
     )
 
 
+def chips_scatter(array):
+    return lax.psum_scatter(
+        array, "seq", scatter_dimension=0, tiled=True, axis_index_groups=core_groups()
+    )
+
+
 def chips_join(parts):
     chips = chips_of()
     chip, _ = place()
@@ -1261,7 +1638,7 @@
 
 def vectors_kernel(groups, perm, perm_wide, *refs):
     pieces, refs = refs[:4], refs[4:]
-    moved_out, plain_out, wide_out, stage, sems = refs
+    outs, (stage, sems) = refs[:-2], refs[-2:]
     width = perm.shape[0]
     start = pieces[0].shape[1] - LANES
     wait_all(
@@ -1270,33 +1647,43 @@
     columns = stage[...]
     line = lax.broadcasted_iota(jnp.int32, (width, width), 0)
     spot = lax.broadcasted_iota(jnp.int32, (width, width), 1)
-    moved_out[...] = grad_matmul(columns, (line == spot).astype(BF))
-    plain = lax.dot_general(
-        columns, perm[...], (((0,), (1,)), ((), ())), preferred_element_type=F32
-    )
-    plain_out[...] = plain
+    moved = grad_matmul(columns, (line == spot).astype(BF))
+    plain = plain_rows(columns, perm[...])
     wide = matmul(plain.astype(BF), perm_wide[...])
     piece = width // (2 * groups)
     for layer in range(LAYERS):
+        base = layer * VECS
+        moved_out, plain_out, wide_out = outs[3 * layer : 3 * layer + 3]
+        moved_out[:VECS, :] = moved[base : base + VECS]
+        plain_out[:VECS, :] = plain[base : base + VECS]
+        if layer == 0:
+            wide_out[...] = wide[base + 5 : base + 5 + groups]
+            continue
         for index in range(groups):
-            row = layer * VECS + 5 + index
+            row = base + 5 + index
             for part in range(2 * groups):
                 goal = part * groups * piece + index * piece
-                wide_out[layer : layer + 1, goal : goal + piece] = wide[
+                wide_out[:, goal : goal + piece] = wide[
                     row : row + 1, part * piece : (part + 1) * piece
                 ]
 
 
 def vectors_fast(groups, perm, perm_wide, pieces):
     width = perm.shape[0]
-    return run(
+    out = run(
         functools.partial(vectors_kernel, groups),
         "vectors",
-        [shape((LANES, width), F32)] * 2 + [shape((8, groups * width), F32)],
+        [
+            *[shape((16, width), F32)] * 2,
+            shape((groups, width), F32),
+            *[shape((16, width), F32)] * 2,
+            shape((1, groups * width), F32),
+        ],
         [perm, perm_wide],
         pieces,
         [pltpu.VMEM((width, LANES), BF), pltpu.SemaphoreType.DMA((8,))],
     )
+    return [out[:3], out[3:]]
 
 
 def fold_kernel(*refs):
@@ -1365,6 +1752,38 @@
         + (inner % count) * (width // (2 * count))
         + (spot // (2 * block)) * (block // count)
         + inner // count
+    )
+
+
+def peer_shift(array, bits):
+    size = lax.axis_size("dp")
+    return lax.ppermute(array, "dp", [(i, i ^ bits) for i in range(size)])
+
+
+def peer_gather(array):
+    return [array] + [peer_shift(array, bits) for bits in range(1, 4)]
+
+
+def peer_trade(parts):
+    return [parts[0]] + [peer_shift(parts[bits], bits) for bits in range(1, 4)]
+
+
+def units_matrix(width, block, count):
+    half = width // 2
+    spot = np.arange(half)
+    inner = spot % block
+    chips = half // (block * count)
+    return one_hot(
+        (spot // block) % chips * (block * count) + inner * count + spot // (block * chips)
+    )
+
+
+def rows_matrix(width, block):
+    half = width // 2
+    spot = np.arange(half)
+    chips = half // (4 * block)
+    return one_hot(
+        (spot // block) % chips * (4 * block) + spot // (block * chips) * block + spot % block
     )
 
 
@@ -1389,37 +1808,50 @@
     mixer_moved = move(mixer_weight.reshape(-1, width), perm).reshape(mixer_weight.shape)
     shrink_moved = move(shrink_weight.reshape(-1, width), perm).reshape(shrink_weight.shape)
     pieces = 2 * groups
-    expand_moved = (
-        move(expand_weight.reshape(-1, width), perm_wide)
-        .reshape(LAYERS * share, groups, pieces, width // pieces)
+    spot = lax.axis_index("dp")
+    perm_rows = rows_matrix(width, share)
+    perm_units = units_matrix(width, share, groups)
+    expand_zero = move(expand_weight[0].reshape(-1, width), perm_wide).reshape(share, wide)
+    expand_one = (
+        move(expand_weight[1].reshape(-1, width), perm_wide)
+        .reshape(share, groups, pieces, width // pieces)
         .transpose(0, 2, 1, 3)
-        .reshape(expand_weight.shape)
+        .reshape(share, wide)
     )
     shrink_moved = shrink_moved.reshape(LAYERS, share, groups * width)
     vector_columns = vector_params.reshape(LAYERS * VECS, share).T
     vector_columns = jnp.pad(vector_columns, ((0, 0), (0, LANES - LAYERS * VECS)))
 
+    parts = chips_parts(
+        jnp.concatenate([triple_weight[0], mixer_moved[0], vector_columns], 1)
+    )
+    expand_zero = after(expand_zero, parts[1])
+    expand_zero = jnp.concatenate(
+        peer_trade(
+            [
+                lax.dynamic_slice(
+                    expand_zero, (0, jnp.bitwise_xor(spot, bits) * width), (share, width)
+                )
+                for bits in range(4)
+            ]
+        ),
+        1,
+    )
     feed_parts = [
-        jnp.concatenate([expand_moved[layer], shrink_moved[layer]], 1) for layer in range(LAYERS)
+        jnp.concatenate([expand_zero, shrink_moved[0]], 1),
+        jnp.concatenate([expand_one, shrink_moved[1]], 1),
     ]
-    attn_one = jnp.concatenate([triple_weight[1], mixer_moved[1]], 1)
-    parts = chips_parts(jnp.concatenate([triple_weight[0], mixer_moved[0], vector_columns], 1))
-    parts[-1] = after(parts[-1], feed_parts[0])
-    attn_zero = chips_join(parts)
-    attn_zero = square_pieces(*square_second(*square_first(attn_zero, 2 * width)))
-    feed_zero = chips_gather(feed_parts[0])
-    attn_one = chips_parts(after(attn_one, attn_zero[0], attn_zero[4]))
-    feed_zero = square_first(after(feed_zero, *attn_zero), wide)
-    moved_rows, plain_rows, wide_rows = vectors_fast(groups, perm, perm_wide, attn_zero[4:])
-    rows_of = []
-    for layer in range(LAYERS):
-        cut = slice(layer * VECS, (layer + 1) * VECS)
-        rows_of.append(
-            (moved_rows[cut], plain_rows[cut], wide_rows[layer : layer + 1])
-        )
+    early = jnp.concatenate([feed_parts[0], triple_weight[1], mixer_moved[1]], 1)
+    parts[-1] = after(parts[-1], early, feed_parts[1])
+    attn = chips_join(parts)
+    early = chips_gather(after(early, attn))
+    feed_zero, attn_one = early[:, : 2 * wide], early[:, 2 * wide :]
+    attn = square_second(*square_first(attn, 2 * width))
+    attn = square_pieces(*attn)
 
     def project(layer, hidden, pieces):
-        low, blocks = project_fast(layer == 0, chips, hidden, perm, rows_of[layer][1], pieces)
+        bias = perm[:8].astype(F32) if layer == 0 else rows_of[layer][1]
+        low, blocks = project_fast(layer, chips, hidden, perm, bias, pieces)
         blocks = [blocks[0]] + [chip_shift(blocks[step], step) for step in range(1, chips)]
         return low, blocks
 
@@ -1434,7 +1866,7 @@
         (
             hidden, attended, normed, pre_act, act, hat_one, scale_one, hat_two, scale_two,
             sent, squares,
-        ) = feed_fast(chips, hidden, low, perm, rows, ffn_bias, pieces, weights)
+        ) = feed_fast(layer, chips, hidden, low, perm, rows, ffn_bias, pieces, weights)
         return (
             hidden,
             (hat_one, scale_one, hat_two, scale_two, pre_act),
@@ -1442,25 +1874,33 @@
             jnp.sum(squares[:3], -1),
         )
 
-    low, blocks = project(0, hidden_input[0], attn_zero)
-    feed_zero = [after(feed_zero[0], low), *feed_zero[1:]]
-    feed_zero = square_second(*feed_zero)
-    blocks[0] = after(blocks[0], feed_zero[0], feed_zero[2])
+    low_zero, blocks = project(0, hidden_input[0], attn)
+    feed_zero = after(feed_zero, *blocks)
+    attn_one = square_second(*square_first(after(attn_one, *blocks), 2 * width))
     feed_one = chips_gather(after(feed_parts[1], *blocks))
-    attn_one[-1] = after(attn_one[-1], low)
-    attn_one = chips_join(attn_one)
+    blocks[0] = after(blocks[0], attn_one[0], attn_one[2])
     attend_zero, pieces = attend_blocks(blocks)
-    attn_one = square_first(after(attn_one, attend_zero[2]), 2 * width)
-    attn_one = square_second(*attn_one)
-    feed_one = lax.all_gather(
-        after(feed_one, attn_one[0], attn_one[2]), "dp", axis=0, tiled=True
-    )
-    feed_zero = square_pieces(*feed_zero)
-    pieces[0] = after(pieces[0], attn_one[0], attn_one[2])
-    hidden, feed_saved_zero, acts_zero, squares_zero = feed(
-        0, low, low, pieces, attn_zero[4:] + feed_zero
-    )
+    attn_one = [
+        attn_one[0], after(attn_one[1], attend_zero[2]),
+        attn_one[2], after(attn_one[3], attend_zero[2]),
+    ]
+    vector_pieces = [after(attn[4], attend_zero[2], attn_one[1], attn_one[3]), *attn[5:]]
+    rows_of = vectors_fast(groups, perm, perm_wide, vector_pieces)
     attn_one = square_pieces(*attn_one)
+    slice_pieces = [feed_zero, core_swap(feed_zero)]
+    pieces[0] = after(pieces[0], slice_pieces[1], *attn_one)
+
+    attended, normed, normed_low, hat, scale, sent, squares = mix_fast(
+        chips, low_zero, low_zero, perm, rows_of[0][0], pieces, attn[4:]
+    )
+    norms_zero, acts_zero = (hat, scale), (low_zero, attended, None, None, core_swap(sent))
+    inputs = peer_gather(normed_low)
+    terms, pre, act = slice_feed_fast(rows_of[0][2], inputs, slice_pieces)
+    feed_one = lax.all_gather(after(feed_one, normed), "dp", axis=0, tiled=True)
+    slice_saved = (inputs, pre, act)
+    hidden, hat, scale, squares = finish_fast(normed, rows_of[0][0], squares, peer_trade(terms))
+    ends_zero, squares_zero = (hat, scale), jnp.sum(squares[:3], -1)
+
     low, blocks = project(1, hidden, attn_one)
     attend_one, pieces = attend_blocks(blocks)
     feed_one = after(feed_one, attend_one[2])
@@ -1468,8 +1908,8 @@
     hidden, feed_saved_one, acts_one, squares_one = feed(
         1, hidden, low, pieces, attn_one[4:] + feed_one
     )
-    packs = [attn_zero + feed_zero, attn_one + feed_one]
-    kept = [(attend_zero, feed_saved_zero, acts_zero), (attend_one, feed_saved_one, acts_one)]
+    packs = [attn, attn_one + feed_one]
+    kept = [(attend_zero, None, acts_zero), (attend_one, feed_saved_one, acts_one)]
     collected = [squares_zero, squares_one]
     elements = count * width * lax.axis_size("dp") * lax.axis_size("seq")
     hidden_output = move_back(hidden.astype(BF), perm)
@@ -1496,7 +1936,7 @@
     def back_feed(layer, grad):
         (_, feed_saved, acts), weights = kept[layer], packs[layer]
         grad_one, gave, attn_nat, sums, grads = feed_back_fast(
-            layer == LAYERS - 1, chips, grad, perm, perm_wide, rows_of[layer][0], feed_saved,
+            layer, chips, grad, perm, perm_wide, rows_of[layer][0], feed_saved,
             weights[4:],
         )
         grads = [grads[0]] + [chip_shift(grads[step], step) for step in range(1, chips)]
@@ -1513,7 +1953,7 @@
         return [pieces[0]] + [chip_shift(pieces[step], -step) for step in range(1, chips)]
 
     def back_project(layer, grad_one, sums, pieces):
-        return project_back_fast(chips, grad_one, perm, sums, pieces, packs[layer][:8])
+        return project_back_fast(layer, chips, grad_one, perm, sums, pieces, packs[layer][:8])
 
     def back_terms(layer, project_grad, attn_nat, vector, far):
         low, attended, _, _, theirs = kept[layer][2]
@@ -1527,7 +1967,7 @@
     grad_one, attn_nat, sums, grads, feed_term = back_feed(1, output_grad[0])
     totals = sum_more(totals, grad_one)
     feed_sum_one = lax.psum_scatter(feed_term, "dp", scatter_dimension=0, tiled=True)
-    grads[0] = after(grads[0], feed_term, totals)
+    grads[0] = after(grads[0], feed_term, totals, hidden_output)
     grad_q, near, far = back_attend(1, grads)
     totals = sum_more(totals, grad_q)
     pieces = back_combine(after(grad_q, totals), near, core_swap(far))
@@ -1537,33 +1977,68 @@
     far_one = swap_all(project_grad, attn_nat, vector)
     terms_args = (project_grad, attn_nat, vector)
 
-    grad_one, attn_nat, sums, grads, feed_term = back_feed(0, grad)
     attn_terms = back_terms(1, *terms_args, far_one)
-    totals = sum_more(totals, grad_one)
-    grads[0] = after(grads[0], feed_term, attn_terms[0], totals)
+    rows = rows_of[0][0]
+    totals = sum_more(totals, grad)
+    grad_two, grad_low, sums = finish_back_fast(False, grad, perm, rows, *ends_zero)
+    blocks = peer_gather(grad_low)
+    blocks[2] = after(blocks[2], totals)
+    blocks[1] = after(blocks[1], feed_sum_one, attn_terms[0])
+    feed_sum_one = chips_scatter(feed_sum_one).astype(F32)
+    inputs, pre, act = slice_saved
+    terms, slope, gave, feed_sums = slice_back_fast(blocks, inputs, pre, act, slice_pieces)
+    totals = sum_more(totals, slope)
+    terms = peer_trade(terms)
+    terms[0] = after(terms[0], totals)
+    grad_one, attn_nat, sums, grads = mix_back_fast(
+        chips, grad_two, perm, rows, *norms_zero, sums, terms, attn[4:]
+    )
+    grads = [grads[0]] + [chip_shift(grads[step], step) for step in range(1, chips)]
+    attn_terms = [
+        attn_terms[0], after(attn_terms[1], grad_one), attn_terms[2], after(attn_terms[3], grad_one)
+    ]
+    grads[0] = after(grads[0], feed_sum_one)
     grad_q, near, far = back_attend(0, grads)
-    feed_sum_zero = scatter_feed(feed_term)
-    totals = sum_more(totals, grad_q)
-    pieces = back_combine(grad_q, near, core_swap(far))
+    feed_term = slice_terms_fast(
+        perm_rows, perm_units, blocks, inputs, act, after(slope, grad_q), core_swap(gave)
+    )
+    feed_sum_zero = chips_scatter(feed_term)
+    attn_terms[0] = after(attn_terms[0], grad_q)
     folded = square_fold(attn_terms)
-    pieces[0] = after(pieces[0], folded[0], totals)
-    project_grad, vector = collect_fast(chips, perm, sums, pieces)
+    pieces = back_combine(after(grad_q, folded[0]), near, core_swap(far))
+    split_one = square_split(folded)
+    pieces[0] = after(pieces[0], split_one[0], feed_term)
+    project_grad, vector = collect_fast(chips, perm, perm_wide, feed_sums, sums, pieces)
     far_zero = swap_all(project_grad, attn_nat, vector)
-    attn_terms = back_terms(0, project_grad, attn_nat, vector, far_zero)
-    input_grad = input_back_fast(
-        after(grad_one, attn_terms[0]), perm, project_grad, packs[0][:8]
-    )
-    split_one = square_split([after(folded[0], attn_terms[0]), *folded[1:]])
-    feed_sum_one = after(feed_sum_one, attn_terms[0])
-    feed_sum_one = scatter_chips(feed_sum_one)
-    attn_terms = [
-        attn_terms[0], after(attn_terms[1], split_one[0], input_grad), *attn_terms[2:]
-    ]
+    attn_terms = list(back_terms(0, project_grad, attn_nat, vector, far_zero))
     folded = square_fold(attn_terms)
+    input_grad = input_back_fast(after(grad_one, folded[0]), perm, project_grad, attn)
+    split_one = [after(split_one[0], folded[0]), *split_one[1:]]
     attn_sum_one = square_total(split_one)
-    folded = [after(folded[0], attn_sum_one, feed_sum_one), *folded[1:]]
+    feed_sum_zero = after(feed_sum_zero, folded[0])
+    expand_sums = peer_trade(
+        [
+            lax.dynamic_slice(
+                feed_sum_zero, (jnp.bitwise_xor(spot, bits) * share, 0), (share, width)
+            )
+            for bits in range(4)
+        ]
+    )
+    expand_zero = jnp.concatenate(
+        [
+            matmul_t(
+                lax.select_n(spot, *[expand_sums[index ^ other] for other in range(4)]), perm_wide
+            )
+            for index in range(groups)
+        ],
+        1,
+    )
+    shrink_zero = matmul_t(feed_sum_zero[:, width:], perm)
+    folded = [after(folded[0], input_grad, *expand_sums, shrink_zero), *folded[1:]]
     attn_sum_zero = square_total(square_split(folded))
-    terms = [(attn_sum_zero, feed_sum_zero), (attn_sum_one, feed_sum_one)]
+    terms = [(attn_sum_zero, None), (attn_sum_one, None)]
+    expand_grads = [expand_zero, feed_sum_one[:, :wide]]
+    shrink_grads = [shrink_zero, feed_sum_one[:, wide:].reshape(wide_share, width)]
     grad = input_grad
     root_squares = jnp.sqrt(totals / elements)
     vector_grad = jnp.stack(
@@ -1580,10 +2055,8 @@
         grad[None],
         jnp.stack([terms[layer][0][:, : 3 * width] for layer in range(LAYERS)]),
         jnp.stack([terms[layer][0][:, 3 * width : 4 * width] for layer in range(LAYERS)]),
-        jnp.stack([terms[layer][1][:, :wide] for layer in range(LAYERS)]),
-        jnp.stack(
-            [terms[layer][1][:, wide:].reshape(wide_share, width) for layer in range(LAYERS)]
-        ),
+        jnp.stack(expand_grads),
+        jnp.stack(shrink_grads),
         vector_grad,
         root_squares,
     )

time: 525 us -> 480 us (0.914)
  waiting for transfers between devices: 228 us -> 152 us
  starting transfers between devices: 90 us -> 107 us
  Pallas kernels: 138 us -> 149 us
    ppermute x20 -> x16, waiting for transfers between devices: 105 us -> 46.9 us  [dp_swap(): return lax.ppermute(array, 'dp', [(i, i ^ bit) for i in range(size)])]
    ppermute x39 -> x33, waiting for transfers between devices: 72.9 us -> 35 us  [chip_shift(): return lax.ppermute(array, 'seq', pairs)]
    ppermute x0 -> x18, waiting for transfers between devices: none -> 33.4 us  [peer_shift(): return lax.ppermute(array, 'dp', [(i, i ^ bits) for i in range(size)])]
    ppermute x0 -> x18, starting transfers between devices: none -> 21.3 us  [peer_shift(): return lax.ppermute(array, 'dp', [(i, i ^ bits) for i in range(size)])]
    pallas_call x24 -> x28, Pallas kernels: 138 us -> 149 us  [run(): pl.pallas_call(kernel, name=name, out_shape=list(outs), in_specs=[VMEM] *...]
    reduce_scatter x2, waiting for transfers between devices: 10.3 us -> 0.02 us  [chips_scatter(): lax.psum_scatter(array, 'seq', scatter_dimension=0, tiled=True, axis_inde...]
    ppermute x20 -> x16, starting transfers between devices: 26.2 us -> 17.3 us  [dp_swap(): return lax.ppermute(array, 'dp', [(i, i ^ bit) for i in range(size)])]
    all_gather x2, waiting for transfers between devices: 18 us -> 9.69 us  [chips_gather(): lax.all_gather(array, 'seq', axis=0, tiled=True, axis_index_groups=core_g...]
  transfers between devices with their start and end apart: 103 -> 108, of which waited for: 40 -> 48; matrix products, arithmetic and copies ran while one was open for 3% -> 3% of each run, Pallas kernels for 22% -> 24%
where the time goes in v3:
time: 480 us; the launch traced here: 471 us
  waiting for transfers between devices  152 us (32%)
  Pallas kernels  149 us (31%)
  starting transfers between devices  107 us (22%)
  local copies, waits for them, and re-layouts  29 us (6%)
  between operations  15.9 us (3%)
  other arithmetic  10.2 us (2%)
  matrix products  7.24 us (2%)
    pallas_call x28, Pallas kernels, run(): pl.pallas_call(kernel, name=name, out_shape=list(outs), in_specs=[VMEM] *...  149 us
    ppermute x33, starting transfers between devices, chip_shift(): return lax.ppermute(array, 'seq', pairs)  57.4 us
    ppermute x16, waiting for transfers between devices, dp_swap(): return lax.ppermute(array, 'dp', [(i, i ^ bit) for i in range(size)])  46.9 us
    ppermute x33, waiting for transfers between devices, chip_shift(): return lax.ppermute(array, 'seq', pairs)  35 us
    ppermute x18, waiting for transfers between devices, peer_shift(): return lax.ppermute(array, 'dp', [(i, i ^ bits) for i in range(size)])  33.4 us
    unnamed x245, local copies, waits for them, and re-layouts  24.8 us
    ppermute x18, starting transfers between devices, peer_shift(): return lax.ppermute(array, 'dp', [(i, i ^ bits) for i in range(size)])  21.3 us
    ppermute x5, waiting for transfers between devices, sum_more(): totals = totals + lax.ppermute(after(totals, token), axis, pairs)  17.9 us
  transfers between devices with their start and end apart: 108, of which 48 were waited for; matrix products, arithmetic and copies ran while one was open for 3% of the time, Pallas kernels for 24%

profile of v3, /device:TPU:0, one launch (start us, length us, event | category | flops | bytes accessed | tf_op | source)
XLA Modules:
  0.0 470.9 jit_solution(13745727286257963700)
XLA Ops:
  10.7 4.0 collective-permute-start.1
  19.6 7.1 %collective-permute-done = bf16[24,3200]{1,0:T(8,128)(2,1)} collective-permute-done((bf16[24,3200]{1,0:T(8,128)(2,1)}, bf16[24,3200]{1,0:T(8,128)(2,1)}, u32[]{:S(2)}, u32[]{:S(2)}) %collective-permute-start) | collective-permute-done | bytes 153632 | tf_op jit(solution)/shard_map/ppermute | solution.py:61
  37.8 7.5 %collective-permute-done.6 = bf16[96,1536]{1,0:T(8,128)(2,1)S(1)} collective-permute-done((bf16[96,1536]{1,0:T(8,128)(2,1)S(1)}, bf16[96,1536]{1,0:T(8,128)(2,1)S(1)}, u32[]{:S(2)}, u32[]{:S(2)}) %collective-permute-start.6) | collective-permute-done | bytes 294944 | tf_op jit(solution)/shard_map/ppermute | solution.py:1603
  47.4 8.9 %collective-permute-done.8.rest_1_.refs_1_ = bf16[192,1536]{1,0:T(8,128)(2,1)S(1)} collective-permute-done((bf16[192,1536]{1,0:T(8,128)(2,1)S(1)}, bf16[192,1536]{1,0:T(8,128)(2,1)S(1)}, u32[]{:S(2)}, u32[]{:S(2)}) %collective-permute-start.8) | collective-permute-done | bytes 589856 | tf_op jit(solution)/shard_map/ppermute | solution.py:1603
  62.5 5.7 %project.2 = (bf16[128,768]{1,0:T(8,128)(2,1)}, bf16[128,576]{1,0:T(8,128)(2,1)}, bf16[128,576]{1,0:T(8,128)(2,1)}, bf16[128,576]{1,0:T(8,128)(2,1)}, bf16[128,576]{1,0:T(8,128)(2,1)}) custom-call(bf16[128,768]{1,0:T(8,128)(2,1)} %bitcast.74, bf16[768,768]{1,0:T(8,128)(2,1)} %constant.70.clone.perm, f32[8,768]{1,0:T(8,128)} %constant.83.bias, ...), custom_call_target="tpu_custom_call" | custom-call | flops 1811939328 | bytes 28409856 | tf_op jit(solution)/shard_map/project/pallas_call | solution.py:474
  68.2 3.5 collective-permute-start.14
  73.7 2.8 collective-permute-start.16
  76.6 9.7 %all-gather.4.cloned.1.call-done = bf16[96,9216]{1,0:T(8,128)(2,1)} async-done(((bf16[24,9216]{1,0:T(8,128)(2,1)}), bf16[96,9216]{1,0:T(8,128)(2,1)}) %all-gather.4.cloned.1.call-update) | async-done | bytes 1769488 | tf_op jit(solution)/shard_map/all_gather | solution.py:1578
  91.9 5.8 %collective-permute-done.17 = bf16[96,1536]{1,0:T(8,128)(2,1)S(1)} collective-permute-done((bf16[96,1536]{1,0:T(8,128)(2,1)}, bf16[96,1536]{1,0:T(8,128)(2,1)S(1)}, u32[]{:S(2)}, u32[]{:S(2)}) %collective-permute-start.17) | collective-permute-done | bytes 294944 | tf_op jit(solution)/shard_map/ppermute | solution.py:1603
  108.1 5.6 %attend.2 = (f32[512,192]{1,0:T(8,128)}, f32[512,128]{1,0:T(8,128)}, bf16[128,192]{1,0:T(8,128)(2,1)}, bf16[128,192]{1,0:T(8,128)(2,1)}, bf16[128,192]{1,0:T(8,128)(2,1)}, /*index=5*/bf16[128,192]{1,0:T(8,128)(2,1)}) custom-call(bf16[128,576]{1,0:T(8,128)(2,1)} %get-tuple-element.189.refs_0_, bf16[128,576]{1,0:T(8,128)(2,1)} %copy-done.84, ...), custom_call_target="tpu_custom_call" | custom-call | flops 1610612736 | bytes 8126464 | tf_op jit(solution)/shard_map/attend/pallas_call | solution.py:474
  118.3 4.5 collective-permute-start.30
  124.0 4.3 vectors.1
  131.1 4.6 mix.1
  140.2 4.3 collective-permute-done.33.refs_1_.refs_5_
  144.5 3.2 collective-permute-done.34.refs_2_.refs_6_
  148.6 6.6 %slice_feed.1 = (f32[128,768]{1,0:T(8,128)}, bf16[128,768]{1,0:T(8,128)(2,1)}, bf16[128,768]{1,0:T(8,128)(2,1)}, bf16[128,768]{1,0:T(8,128)(2,1)}, f32[512,768]{1,0:T(8,128)}, /*index=5*/bf16[512,768]{1,0:T(8,128)(2,1)}) custom-call(f32[4,768]{1,0:T(4,128)} %get-tuple-element.205.wide_bias, bf16[128,768]{1,0:T(8,128)(2,1)} %get-tuple-element.206.refs_0_.refs_4_, ...), custom_call_target="tpu_custom_call" | custom-call | flops 4831838208 | bytes 26001408 | tf_op jit(solution)/shard_map/slice_feed/pallas_call | solution.py:474
  159.6 5.5 %collective-permute-done.36.refs_1_ = bf16[128,768]{1,0:T(8,128)(2,1)S(1)} collective-permute-done((bf16[128,768]{1,0:T(8,128)(2,1)}, bf16[128,768]{1,0:T(8,128)(2,1)S(1)}, u32[]{:S(2)}, u32[]{:S(2)}) %collective-permute-start.36) | collective-permute-done | bytes 196640 | tf_op jit(solution)/shard_map/ppermute | solution.py:1760
  165.1 3.2 collective-permute-done.37.refs_2_
  169.1 3.1 finish.1
  172.1 5.1 %project.3 = (bf16[128,768]{1,0:T(8,128)(2,1)}, bf16[128,576]{1,0:T(8,128)(2,1)}, bf16[128,576]{1,0:T(8,128)(2,1)}, bf16[128,576]{1,0:T(8,128)(2,1)}, bf16[128,576]{1,0:T(8,128)(2,1)}) custom-call(f32[128,768]{1,0:T(8,128)} %get-tuple-element.211.source.hidden, bf16[768,768]{1,0:T(8,128)(2,1)} %constant.70.clone.perm, f32[16,768]{1,0:T(8,128)} %get-tuple-element.212.bias, ...), custom_call_target="tpu_custom_call" | custom-call | flops 1811939328 | bytes 28508160 | tf_op jit(solution)/shard_map/project/pallas_call | solution.py:474
  181.6 4.8 %collective-permute-done.39.refs_1_ = bf16[128,576]{1,0:T(8,128)(2,1)S(1)} collective-permute-done((bf16[128,576]{1,0:T(8,128)(2,1)}, bf16[128,576]{1,0:T(8,128)(2,1)S(1)}, u32[]{:S(2)}, u32[]{:S(2)}) %collective-permute-start.39) | collective-permute-done | bytes 147488 | tf_op jit(solution)/shard_map/ppermute | solution.py:61
  186.5 3.9 collective-permute-done.40.refs_2_
  193.1 5.6 %attend.3 = (f32[512,192]{1,0:T(8,128)}, f32[512,128]{1,0:T(8,128)}, bf16[128,192]{1,0:T(8,128)(2,1)}, bf16[128,192]{1,0:T(8,128)(2,1)}, bf16[128,192]{1,0:T(8,128)(2,1)}, /*index=5*/bf16[128,192]{1,0:T(8,128)(2,1)}) custom-call(bf16[128,576]{1,0:T(8,128)(2,1)} %get-tuple-element.216.refs_0_, bf16[128,576]{1,0:T(8,128)(2,1)} %copy-done.94, ...), custom_call_target="tpu_custom_call" | custom-call | flops 1610612736 | bytes 8126464 | tf_op jit(solution)/shard_map/attend/pallas_call | solution.py:474
  198.9 5.2 %collective-permute-start.46 = (bf16[128,192]{1,0:T(8,128)(2,1)}, bf16[128,192]{1,0:T(8,128)(2,1)S(1)}, u32[]{:S(2)}, u32[]{:S(2)}) collective-permute-start(bf16[128,192]{1,0:T(8,128)(2,1)} %get-tuple-element.221), channel_id=1, source_target_pairs={{0,6},{1,7},{2,0},{3,1},{4,2},{5,3},{6,4},{7,5},{8,14},{9,15},{10,... | collective-permute-start | bytes 147464 | tf_op jit(solution)/shard_map/ppermute | solution.py:61
  206.9 4.2 collective-permute-done.47.refs_2_
  213.4 9.9 %feed.1 = (f32[128,768]{1,0:T(8,128)}, bf16[128,768]{1,0:T(8,128)(2,1)}, bf16[128,768]{1,0:T(8,128)(2,1)}, f32[128,3072]{1,0:T(8,128)}, bf16[128,3072]{1,0:T(8,1...) custom-call(f32[128,768]{1,0:T(8,128)} %get-tuple-element.211.source, ...), custom_call_target="tpu_custom_call" | custom-call | flops 6039797760 | bytes 74399744 | tf_op jit(solution)/shard_map/feed/pallas_call | solution.py:474
  223.4 13.2 %feed_back.1 = (f32[128,768]{1,0:T(8,128)}, bf16[128,3840]{1,0:T(8,128)(2,1)}, bf16[128,768]{1,0:T(8,128)(2,1)}, f32[16,768]{1,0:T(8,128)}, bf16[128,192]{1,0:T(...) custom-call(bf16[128,768]{1,0:T(8,128)(2,1)} %bitcast.75, ...), custom_call_target="tpu_custom_call" | custom-call | flops 7247757312 | bytes 74842112 | tf_op jit(solution)/shard_map/feed_back/pallas_call | solution.py:474
  237.1 3.0 collective-permute-done.50.theirs
  241.4 5.6 %feed_terms.1 = bf16[384,6144]{1,0:T(8,128)(2,1)} custom-call(bf16[128,768]{1,0:T(8,128)(2,1)} %get-tuple-element.237.normed, bf16[128,3072]{1,0:T(8,128)(2,1)} %get-tuple-element.238.act, bf16[128,3840]{1,0:T(8,128)(2,1)} %get-tuple-element.239.gave, bf16[128,2688]{1,0:T(8,128)(2,1)} %copy-done.56, bf16[128,3840]{1,0:T(8,128)(2,1)} %copy-done.55), custom_call_target="tpu_custom_call" | custom-call | flops 48318382080 | bytes 334233600 | tf_op jit(solution)/shard_map/feed_terms/pallas_call | solution.py:474
  257.7 8.5 %attend_back.2 = (bf16[512,192]{1,0:T(8,128)(2,1)}, f32[512,384]{1,0:T(8,128)}, bf16[512,384]{1,0:T(8,128)(2,1)}) custom-call(bf16[128,576]{1,0:T(8,128)(2,1)} %get-tuple-element.216.refs_0_, bf16[128,576]{1,0:T(8,128)(2,1)} %copy-done.94, bf16[128,576]{1,0:T(8,128)(2,1)} %copy-done.95, bf16[128,576]{1,0:T(8,128)(2,1)} %copy-done.96, ...), custom_call_target="tpu_custom_call" | custom-call | flops 4026531840 | bytes 13631488 | tf_op jit(solution)/shard_map/attend_back/pallas_call | solution.py:474
  278.0 12.3 %collective-permute-done.58 = f32[2,3]{1,0:T(2,128)S(1)} collective-permute-done((f32[2,3]{1,0:T(2,128)S(1)}, f32[2,3]{1,0:T(2,128)S(1)}, u32[]{:S(2)}, u32[]{:S(2)}) %collective-permute-start.58) | collective-permute-done | bytes 56 | tf_op jit(solution)/shard_map/ppermute | solution.py:1926
  291.0 6.6 %project_back.1 = (f32[128,768]{1,0:T(8,128)}, bf16[128,2304]{1,0:T(8,128)(2,1)}, f32[16,768]{1,0:T(8,128)}) custom-call(f32[128,768]{1,0:T(8,128)} %get-tuple-element.234.grad_one, bf16[768,768]{1,0:T(8,128)(2,1)} %constant.70.clone.perm, f32[16,768]{1,0:T(8,128)} %get-tuple-element.235.sums, bf16[128,576]{1,0:T(8,128)(2,1)} %get-tuple-element.256.refs_0_, ...), custom_call_target="tpu_custom_call" | custom-call | flops 1811939328 | bytes 31850496 | tf_op jit(solution)/shard_map/project_back/pallas_call | solution.py:474
  302.5 3.3 collective-permute-done.67
  310.0 3.8 attend_terms.2
  317.2 7.7 %slice_back.1 = (f32[128,768]{1,0:T(8,128)}, bf16[128,768]{1,0:T(8,128)(2,1)}, bf16[128,768]{1,0:T(8,128)(2,1)}, bf16[128,768]{1,0:T(8,128)(2,1)}, bf16[512,768]...) custom-call(bf16[128,768]{1,0:T(8,128)(2,1)} %get-tuple-element.267.refs_0_, ...), custom_call_target="tpu_custom_call" | custom-call | flops 4831838208 | bytes 41779200 | tf_op jit(solution)/shard_map/slice_back/pallas_call | solution.py:474
  330.5 3.9 collective-permute-done.70.refs_1_
  334.4 3.5 collective-permute-done.72.refs_3_
  338.6 5.0 %mix_back.1 = (f32[128,768]{1,0:T(8,128)}, bf16[128,768]{1,0:T(8,128)(2,1)}, f32[16,768]{1,0:T(8,128)}, bf16[128,192]{1,0:T(8,128)(2,1)}, bf16[128,192]{1,0:T(8,...) custom-call(f32[128,768]{1,0:T(8,128)} %get-tuple-element.263.grad_two, ...), custom_call_target="tpu_custom_call" | custom-call | flops 1811939328 | bytes 26017792 | tf_op jit(solution)/shard_map/mix_back/pallas_call | solution.py:474
  352.5 8.3 %attend_back.3 = (bf16[512,192]{1,0:T(8,128)(2,1)}, f32[512,384]{1,0:T(8,128)}, bf16[512,384]{1,0:T(8,128)(2,1)}) custom-call(bf16[128,576]{1,0:T(8,128)(2,1)} %get-tuple-element.189.refs_0_, bf16[128,576]{1,0:T(8,128)(2,1)} %copy-done.84, bf16[128,576]{1,0:T(8,128)(2,1)} %copy-done.86, bf16[128,576]{1,0:T(8,128)(2,1)} %copy-done.88, ...), custom_call_target="tpu_custom_call" | custom-call | flops 4026531840 | bytes 13631488 | tf_op jit(solution)/shard_map/attend_back/pallas_call | solution.py:474
  361.8 3.3 collective-permute-done.77.refs_3_
  377.5 6.7 %slice_terms.1 = bf16[384,1536]{1,0:T(8,128)(2,1)} custom-call(bf16[384,384]{1,0:T(8,128)(2,1)} %constant.72.clone.perm_rows, bf16[384,384]{1,0:T(8,128)(2,1)} %constant.73.clone.perm_units, bf16[128,768]{1,0:T(8,128)(2,1)} %get-tuple-element.267.refs_0_, bf16[128,768]{1,0:T(8,128)(2,1)} %copy-done.75, bf16[128,768]{1,0:T(8,128)(2,1)} %copy-done.73, ...), custom_call_target="tpu_custom_call" | custom-call | flops 48318382080 | bytes 290979840 | tf_op jit(solution)/shard_map/slice_terms/pallas_call | solution.py:474
  389.0 5.1 %collect.1 = (bf16[128,2304]{1,0:T(8,128)(2,1)}, f32[16,768]{1,0:T(8,128)}) custom-call(bf16[768,768]{1,0:T(8,128)(2,1)} %constant.70.clone.perm, bf16[768,768]{1,0:T(8,128)(2,1)} %constant.71.clone.perm_wide, f32[8,768]{1,0:T(8,128)} %get-tuple-element.287.feed_sums, f32[16,768]{1,0:T(8,128)} %get-tuple-element.288.sums, ...), custom_call_target="tpu_custom_call" | custom-call | bytes 14647296 | tf_op jit(solution)/shard_map/collect/pallas_call | solution.py:474
  400.0 3.9 attend_terms.3
  406.3 12.4 %collective-permute-done.89.refs_1_ = bf16[192,1536]{1,0:T(8,128)(2,1)S(1)} collective-permute-done((bf16[192,1536]{1,0:T(8,128)(2,1)}, bf16[192,1536]{1,0:T(8,128)(2,1)S(1)}, u32[]{:S(2)}, u32[]{:S(2)}) %collective-permute-start.89) | collective-permute-done | bytes 589856 | tf_op jit(solution)/shard_map/ppermute | solution.py:1603
  420.8 2.8 fold.3
  427.1 6.4 %input_back.1 = bf16[128,768]{1,0:T(8,128)(2,1)} custom-call(f32[128,768]{1,0:T(8,128)} %get-tuple-element.326.grad_one, bf16[768,768]{1,0:T(8,128)(2,1)} %constant.70.clone.perm, bf16[128,2304]{1,0:T(8,128)(2,1)} %get-tuple-element.317.project, bf16[192,1536]{1,0:T(8,128)(2,1)} %copy-done.19, bf16[192,1536]{1,0:T(8,128)(2,1)} %copy-done.59, ...), custom_call_target="tpu_custom_call" | custom-call | flops 18119393280 | bytes 290979840 | tf_op jit(solution)/shard_map/input_back/pallas_call | solution.py:474
  444.1 3.4 collective-permute-start.98
  454.0 7.3 %collective-permute-done.97 = bf16[24,3200]{1,0:T(8,128)(2,1)S(1)} collective-permute-done((bf16[24,3200]{1,0:T(8,128)(2,1)}, bf16[24,3200]{1,0:T(8,128)(2,1)S(1)}, u32[]{:S(2)}, u32[]{:S(2)}) %collective-permute-start.97) | collective-permute-done | bytes 153632 | tf_op jit(solution)/shard_map/ppermute | solution.py:61
  (514 shorter events, 180.0 us)
Async XLA Ops:
  7.2 79.0 %all-gather.4.cloned.1.call-start = ((), (), s32[]{:S(2)}) async-start(), calls=%async_computation.3 | async-start | bytes 2211840 | tf_op jit(solution)/shard_map/all_gather | solution.py:1578
  10.7 24.4 %collective-permute-start.1 = (bf16[24,3200]{1,0:T(8,128)(2,1)}, bf16[24,3200]{1,0:T(8,128)(2,1)}, u32[]{:S(2)}, u32[]{:S(2)}) collective-permute-start(bf16[24,3200]{1,0:T(8,128)(2,1)} %fusion.6), channel_id=1, source_target_pairs={{0,4},{1,5},{2,6},{3,7},{4,0},{5,1},{6,2},{7,3},{8,12},{9,13},{10,... | collective-permute-start | bytes 460808 | tf_op jit(solution)/shard_map/ppermute | solution.py:61
  14.7 20.3 %collective-permute-start.2 = (bf16[24,3200]{1,0:T(8,128)(2,1)}, bf16[24,3200]{1,0:T(8,128)(2,1)}, u32[]{:S(2)}, u32[]{:S(2)}) collective-permute-start(bf16[24,3200]{1,0:T(8,128)(2,1)} %fusion.6), channel_id=1, source_target_pairs={{0,6},{1,7},{2,0},{3,1},{4,2},{5,3},{6,4},{7,5},{8,14},{9,15},{10,... | collective-permute-start | bytes 460808 | tf_op jit(solution)/shard_map/ppermute | solution.py:61
  16.0 10.7 %collective-permute-start = (bf16[24,3200]{1,0:T(8,128)(2,1)}, bf16[24,3200]{1,0:T(8,128)(2,1)}, u32[]{:S(2)}, u32[]{:S(2)}) collective-permute-start(bf16[24,3200]{1,0:T(8,128)(2,1)} %fusion.6), channel_id=1, source_target_pairs={{0,2},{1,3},{2,4},{3,5},{4,6},{5,7},{6,0},{7,1},{8,10},{9,11},{10,... | collective-permute-start | bytes 460808 | tf_op jit(solution)/shard_map/ppermute | solution.py:61
  36.5 99.3 %all-gather.6.cloned.1.call-start = ((), (), s32[]{:S(2)}) async-start(), calls=%async_computation.4 | async-start | bytes 1474560 | tf_op jit(solution)/shard_map/all_gather | solution.py:1578
  45.5 12.2 %collective-permute-start.9 = (bf16[192,1664]{1,0:T(8,128)(2,1)S(1)}, bf16[192,1664]{1,0:T(8,128)(2,1)S(1)}, u32[]{:S(2)}, u32[]{:S(2)}) collective-permute-start(bf16[192,1664]{1,0:T(8,128)(2,1)S(1)} %maximum_select_fusion.rest_4_.refs_0_.refs_4_), channel_id=1, source_target_pairs={{0,8},{8,0},{16,24},{24,16},{1,9},{9,1},{17,25},{25,17},{2,10},{10... | collective-permute-start | bytes 1916936 | tf_op jit(solution)/shard_map/ppermute | solution.py:1603
  47.4 13.3 %collective-permute-start.12 = (bf16[192,1664]{1,0:T(8,128)(2,1)S(1)}, bf16[192,1664]{1,0:T(8,128)(2,1)S(1)}, u32[]{:S(2)}, u32[]{:S(2)}) collective-permute-start(bf16[192,1664]{1,0:T(8,128)(2,1)S(1)} %maximum_select_fusion.rest_4_.refs_0_.refs_4_), channel_id=1, source_target_pairs={{0,1},{1,0},{2,3},{3,2},{4,5},{5,4},{6,7},{7,6},{8,9},{9,8},{10,11... | collective-permute-start | bytes 1916936 | tf_op jit(solution)/shard_map/ppermute | solution.py:54
  68.2 18.0 %collective-permute-start.14 = (bf16[128,576]{1,0:T(8,128)(2,1)}, bf16[128,576]{1,0:T(8,128)(2,1)S(1)}, u32[]{:S(2)}, u32[]{:S(2)}) collective-permute-start(bf16[128,576]{1,0:T(8,128)(2,1)} %get-tuple-element.183), channel_id=1, source_target_pairs={{0,2},{1,3},{2,4},{3,5},{4,6},{5,7},{6,0},{7,1},{8,10},{9,11},{10,... | collective-permute-start | bytes 442376 | tf_op jit(solution)/shard_map/ppermute | solution.py:61
  71.7 16.1 %collective-permute-start.15 = (bf16[128,576]{1,0:T(8,128)(2,1)}, bf16[128,576]{1,0:T(8,128)(2,1)S(1)}, u32[]{:S(2)}, u32[]{:S(2)}) collective-permute-start(bf16[128,576]{1,0:T(8,128)(2,1)} %get-tuple-element.184), channel_id=1, source_target_pairs={{0,4},{1,5},{2,6},{3,7},{4,0},{5,1},{6,2},{7,3},{8,12},{9,13},{10,... | collective-permute-start | bytes 442376 | tf_op jit(solution)/shard_map/ppermute | solution.py:61
  73.7 14.1 %collective-permute-start.16 = (bf16[128,576]{1,0:T(8,128)(2,1)}, bf16[128,576]{1,0:T(8,128)(2,1)S(1)}, u32[]{:S(2)}, u32[]{:S(2)}) collective-permute-start(bf16[128,576]{1,0:T(8,128)(2,1)} %get-tuple-element.185), channel_id=1, source_target_pairs={{0,6},{1,7},{2,0},{3,1},{4,2},{5,3},{6,4},{7,5},{8,14},{9,15},{10,... | collective-permute-start | bytes 442376 | tf_op jit(solution)/shard_map/ppermute | solution.py:61
  91.7 107.1 %all-gather.8.cloned.1.call-start = ((), (), s32[]{:S(2)}) async-start(), calls=%async_computation.5 | async-start | bytes 5898240 | tf_op jit(solution)/shard_map/all_gather | solution.py:1899
  91.9 32.0 %collective-permute-start.25 = (bf16[96,6144]{1,0:T(8,128)(2,1)S(1)}, bf16[96,6144]{1,0:T(8,128)(2,1)S(1)}, u32[]{:S(2)}, u32[]{:S(2)}) collective-permute-start(bf16[96,6144]{1,0:T(8,128)(2,1)S(1)} %slice.123.refs_4_.refs_10_), channel_id=1, source_target_pairs={{0,1},{1,0},{2,3},{3,2},{4,5},{5,4},{6,7},{7,6},{8,9},{9,8},{10,11... | collective-permute-start | bytes 3538952 | tf_op jit(solution)/shard_map/ppermute | solution.py:54
  100.9 14.1 %collective-permute-start.23 = (bf16[192,1536]{1,0:T(8,128)(2,1)S(1)}, bf16[192,1536]{1,0:T(8,128)(2,1)S(1)}, u32[]{:S(2)}, u32[]{:S(2)}) collective-permute-start(bf16[192,1536]{1,0:T(8,128)(2,1)S(1)} %maximum_select_fusion.2.rest_0_.refs_4_), channel_id=1, source_target_pairs={{0,16},{8,24},{16,0},{24,8},{1,17},{9,25},{17,1},{25,9},{2,18},{10... | collective-permute-start | bytes 1769480 | tf_op jit(solution)/shard_map/ppermute | solution.py:1603
  103.9 13.9 %collective-permute-start.24 = (bf16[192,1536]{1,0:T(8,128)(2,1)S(1)}, bf16[192,1536]{1,0:T(8,128)(2,1)S(1)}, u32[]{:S(2)}, u32[]{:S(2)}) collective-permute-start(bf16[192,1536]{1,0:T(8,128)(2,1)S(1)} %maximum_select_fusion.3.rest_4_.refs_4_.refs_0_.refs_8_), channel_id=1, source_target_pairs={{0,8},{8,0},{16,24},{24,16},{1,9},{9,1},{17,25},{25,17},{2,10},{10... | collective-permute-start | bytes 1769480 | tf_op jit(solution)/shard_map/ppermute | solution.py:1603
  107.2 11.1 %collective-permute-start.26 = (bf16[192,1536]{1,0:T(8,128)(2,1)S(1)}, bf16[192,1536]{1,0:T(8,128)(2,1)S(1)}, u32[]{:S(2)}, u32[]{:S(2)}) collective-permute-start(bf16[192,1536]{1,0:T(8,128)(2,1)S(1)} %maximum_select_fusion.2.rest_0_.refs_4_), channel_id=1, source_target_pairs={{0,1},{1,0},{2,3},{3,2},{4,5},{5,4},{6,7},{7,6},{8,9},{9,8},{10,11... | collective-permute-start | bytes 1769480 | tf_op jit(solution)/shard_map/ppermute | solution.py:54
  107.5 15.3 %collective-permute-start.28 = (bf16[192,1536]{1,0:T(8,128)(2,1)S(1)}, bf16[192,1536]{1,0:T(8,128)(2,1)S(1)}, u32[]{:S(2)}, u32[]{:S(2)}) collective-permute-start(bf16[192,1536]{1,0:T(8,128)(2,1)S(1)} %maximum_select_fusion.3.rest_4_.refs_4_.refs_0_.refs_8_), channel_id=1, source_target_pairs={{0,1},{1,0},{2,3},{3,2},{4,5},{5,4},{6,7},{7,6},{8,9},{9,8},{10,11... | collective-permute-start | bytes 1769480 | tf_op jit(solution)/shard_map/ppermute | solution.py:54
  117.8 10.6 %collective-permute-start.27 = (bf16[192,1536]{1,0:T(8,128)(2,1)S(1)}, bf16[192,1536]{1,0:T(8,128)(2,1)S(1)}, u32[]{:S(2)}, u32[]{:S(2)}) collective-permute-start(bf16[192,1536]{1,0:T(8,128)(2,1)S(1)} %collective-permute-done.23.rest_1_.refs_5_), channel_id=1, source_target_pairs={{0,1},{1,0},{2,3},{3,2},{4,5},{5,4},{6,7},{7,6},{8,9},{9,8},{10,11... | collective-permute-start | bytes 1769480 | tf_op jit(solution)/shard_map/ppermute | solution.py:54
  117.8 10.6 %collective-permute-start.29 = (bf16[192,1536]{1,0:T(8,128)(2,1)S(1)}, bf16[192,1536]{1,0:T(8,128)(2,1)S(1)}, u32[]{:S(2)}, u32[]{:S(2)}) collective-permute-start(bf16[192,1536]{1,0:T(8,128)(2,1)S(1)} %collective-permute-done.24.rest_5_.refs_5_.refs_1_.refs_9_), channel_id=1, source_target_pairs={{0,1},{1,0},{2,3},{3,2},{4,5},{5,4},{6,7},{7,6},{8,9},{9,8},{10,11... | collective-permute-start | bytes 1769480 | tf_op jit(solution)/shard_map/ppermute | solution.py:54
  118.3 11.8 %collective-permute-start.30 = (bf16[128,192]{1,0:T(8,128)(2,1)}, bf16[128,192]{1,0:T(8,128)(2,1)S(1)}, u32[]{:S(2)}, u32[]{:S(2)}) collective-permute-start(bf16[128,192]{1,0:T(8,128)(2,1)} %get-tuple-element.200), channel_id=1, source_target_pairs={{0,6},{1,7},{2,0},{3,1},{4,2},{5,3},{6,4},{7,5},{8,14},{9,15},{10,... | collective-permute-start | bytes 147464 | tf_op jit(solution)/shard_map/ppermute | solution.py:61
  135.8 173.2 %reduce-scatter.4.cloned.1.call-start = ((), (), s32[]{:S(2)}) async-start(), calls=%async_computation.6 | async-start | bytes 5898240 | tf_op jit(solution)/shard_map/reduce_scatter | solution.py:1969
  137.3 10.4 %collective-permute-start.34 = (bf16[128,768]{1,0:T(8,128)(2,1)S(1)}, bf16[128,768]{1,0:T(8,128)(2,1)S(1)}, u32[]{:S(2)}, u32[]{:S(2)}) collective-permute-start(bf16[128,768]{1,0:T(8,128)(2,1)S(1)} %copy-done.68), channel_id=1, source_target_pairs={{0,16},{8,24},{16,0},{24,8},{1,17},{9,25},{17,1},{25,9},{2,18},{10... | collective-permute-start | bytes 589832 | tf_op jit(solution)/shard_map/ppermute | solution.py:1760
  179.2 11.2 %collective-permute-start.40 = (bf16[128,576]{1,0:T(8,128)(2,1)}, bf16[128,576]{1,0:T(8,128)(2,1)S(1)}, u32[]{:S(2)}, u32[]{:S(2)}) collective-permute-start(bf16[128,576]{1,0:T(8,128)(2,1)} %get-tuple-element.218), channel_id=1, source_target_pairs={{0,4},{1,5},{2,6},{3,7},{4,0},{5,1},{6,2},{7,3},{8,12},{9,13},{10,... | collective-permute-start | bytes 442376 | tf_op jit(solution)/shard_map/ppermute | solution.py:61
  198.7 12.5 %collective-permute-start.49 = (bf16[384,6144]{1,0:T(8,128)(2,1)}, bf16[384,6144]{1,0:T(8,128)(2,1)S(1)}, u32[]{:S(2)}, u32[]{:S(2)}) collective-permute-start(bf16[384,6144]{1,0:T(8,128)(2,1)} %all-gather.8.cloned.1.call-done.refs_8_.refs_4_), channel_id=1, source_target_pairs={{0,1},{1,0},{2,3},{3,2},{4,5},{5,4},{6,7},{7,6},{8,9},{9,8},{10,11... | collective-permute-start | bytes 14155784 | tf_op jit(solution)/shard_map/ppermute | solution.py:54
  247.1 102.7 %reduce-scatter.6.cloned.1.call-start = ((), (), s32[]{:S(2)}) async-start(), calls=%async_computation.7 | async-start | bytes 1474560 | tf_op jit(solution)/shard_map/reduce_scatter | solution.py:1584
  273.0 17.3 %collective-permute-start.59 = (bf16[128,576]{1,0:T(8,128)(2,1)}, bf16[128,576]{1,0:T(8,128)(2,1)S(1)}, u32[]{:S(2)}, u32[]{:S(2)}) collective-permute-start(bf16[128,576]{1,0:T(8,128)(2,1)} %get-tuple-element.257), channel_id=1, source_target_pairs={{0,6},{1,7},{2,0},{3,1},{4,2},{5,3},{6,4},{7,5},{8,14},{9,15},{10,... | collective-permute-start | bytes 442376 | tf_op jit(solution)/shard_map/ppermute | solution.py:61
  275.0 15.2 %collective-permute-start.60 = (bf16[128,576]{1,0:T(8,128)(2,1)}, bf16[128,576]{1,0:T(8,128)(2,1)S(1)}, u32[]{:S(2)}, u32[]{:S(2)}) collective-permute-start(bf16[128,576]{1,0:T(8,128)(2,1)} %get-tuple-element.258), channel_id=1, source_target_pairs={{0,4},{1,5},{2,6},{3,7},{4,0},{5,1},{6,2},{7,3},{8,12},{9,13},{10,... | collective-permute-start | bytes 442376 | tf_op jit(solution)/shard_map/ppermute | solution.py:61
  275.6 14.6 %collective-permute-start.61 = (bf16[128,576]{1,0:T(8,128)(2,1)}, bf16[128,576]{1,0:T(8,128)(2,1)S(1)}, u32[]{:S(2)}, u32[]{:S(2)}) collective-permute-start(bf16[128,576]{1,0:T(8,128)(2,1)} %get-tuple-element.259), channel_id=1, source_target_pairs={{0,2},{1,3},{2,4},{3,5},{4,6},{5,7},{6,0},{7,1},{8,10},{9,11},{10,... | collective-permute-start | bytes 442376 | tf_op jit(solution)/shard_map/ppermute | solution.py:61
  275.6 14.6 %collective-permute-start.58 = (f32[2,3]{1,0:T(2,128)S(1)}, f32[2,3]{1,0:T(2,128)S(1)}, u32[]{:S(2)}, u32[]{:S(2)}) collective-permute-start(f32[2,3]{1,0:T(2,128)S(1)} %fusion.33), channel_id=1, source_target_pairs={{0,4},{1,5},{2,6},{3,7},{4,0},{5,1},{6,2},{7,3},{8,12},{9,13},{10,... | collective-permute-start | bytes 80 | tf_op jit(solution)/shard_map/ppermute | solution.py:1926
  297.6 11.5 %collective-permute-start.63 = (bf16[128,2304]{1,0:T(8,128)(2,1)}, bf16[128,2304]{1,0:T(8,128)(2,1)S(1)}, u32[]{:S(2)}, u32[]{:S(2)}) collective-permute-start(bf16[128,2304]{1,0:T(8,128)(2,1)} %get-tuple-element.269.project), channel_id=1, source_target_pairs={{0,1},{1,0},{2,3},{3,2},{4,5},{5,4},{6,7},{7,6},{8,9},{9,8},{10,11... | collective-permute-start | bytes 1769480 | tf_op jit(solution)/shard_map/ppermute | solution.py:54
  309.0 124.5 %reduce-scatter.8.cloned.1.call-start = ((), (), s32[]{:S(2)}) async-start(), calls=%async_computation.8 | async-start | bytes 1474560 | tf_op jit(solution)/shard_map/reduce_scatter | solution.py:1584
  324.9 51.0 %collective-permute-start.81 = (bf16[512,2304]{1,0:T(8,128)(2,1)}, bf16[512,2304]{1,0:T(8,128)(2,1)}, u32[]{:S(2)}, u32[]{:S(2)}) collective-permute-start(bf16[512,2304]{1,0:T(8,128)(2,1)} %get-tuple-element.312), channel_id=1, source_target_pairs={{0,1},{1,0},{2,3},{3,2},{4,5},{5,4},{6,7},{7,6},{8,9},{9,8},{10,11... | collective-permute-start | bytes 7077896 | tf_op jit(solution)/shard_map/ppermute | solution.py:54
  327.4 10.5 %collective-permute-start.72 = (bf16[128,768]{1,0:T(8,128)(2,1)}, bf16[128,768]{1,0:T(8,128)(2,1)S(1)}, u32[]{:S(2)}, u32[]{:S(2)}) collective-permute-start(bf16[128,768]{1,0:T(8,128)(2,1)} %get-tuple-element.284), channel_id=1, source_target_pairs={{0,24},{8,16},{16,8},{24,0},{1,25},{9,17},{17,9},{25,1},{2,26},{10... | collective-permute-start | bytes 589832 | tf_op jit(solution)/shard_map/ppermute | solution.py:1760
  348.0 13.7 %collective-permute-start.76 = (bf16[192,1536]{1,0:T(8,128)(2,1)S(1)}, bf16[192,1536]{1,0:T(8,128)(2,1)S(1)}, u32[]{:S(2)}, u32[]{:S(2)}) collective-permute-start(bf16[192,1536]{1,0:T(8,128)(2,1)S(1)} %copy-done.62), channel_id=1, source_target_pairs={{0,8},{8,0},{16,24},{24,16},{1,9},{9,1},{17,25},{25,17},{2,10},{10... | collective-permute-start | bytes 1769480 | tf_op jit(solution)/shard_map/ppermute | solution.py:1603
  350.8 14.2 %collective-permute-start.77 = (bf16[192,1664]{1,0:T(8,128)(2,1)S(1)}, bf16[192,1664]{1,0:T(8,128)(2,1)S(1)}, u32[]{:S(2)}, u32[]{:S(2)}) collective-permute-start(bf16[192,1664]{1,0:T(8,128)(2,1)S(1)} %copy-done.58), channel_id=1, source_target_pairs={{0,16},{8,24},{16,0},{24,8},{1,17},{9,25},{17,1},{25,9},{2,18},{10... | collective-permute-start | bytes 1916936 | tf_op jit(solution)/shard_map/ppermute | solution.py:1603
  368.7 15.5 %collective-permute-start.79 = (bf16[96,1536]{1,0:T(8,128)(2,1)}, bf16[96,1536]{1,0:T(8,128)(2,1)S(1)}, u32[]{:S(2)}, u32[]{:S(2)}) collective-permute-start(bf16[96,1536]{1,0:T(8,128)(2,1)} %get-tuple-element.307), channel_id=1, source_target_pairs={{0,16},{8,24},{16,0},{24,8},{1,17},{9,25},{17,1},{25,9},{2,18},{10... | collective-permute-start | bytes 884744 | tf_op jit(solution)/shard_map/ppermute | solution.py:1603
  369.5 14.7 %collective-permute-start.80 = (bf16[96,1664]{1,0:T(8,128)(2,1)}, bf16[96,1664]{1,0:T(8,128)(2,1)S(1)}, u32[]{:S(2)}, u32[]{:S(2)}) collective-permute-start(bf16[96,1664]{1,0:T(8,128)(2,1)} %get-tuple-element.309), channel_id=1, source_target_pairs={{0,8},{8,0},{16,24},{24,16},{1,9},{9,1},{17,25},{25,17},{2,10},{10... | collective-permute-start | bytes 958472 | tf_op jit(solution)/shard_map/ppermute | solution.py:1603
  373.8 13.6 %collective-permute-start.82 = (bf16[128,576]{1,0:T(8,128)(2,1)}, bf16[128,576]{1,0:T(8,128)(2,1)S(1)}, u32[]{:S(2)}, u32[]{:S(2)}) collective-permute-start(bf16[128,576]{1,0:T(8,128)(2,1)} %get-tuple-element.314), channel_id=1, source_target_pairs={{0,6},{1,7},{2,0},{3,1},{4,2},{5,3},{6,4},{7,5},{8,14},{9,15},{10,... | collective-permute-start | bytes 442376 | tf_op jit(solution)/shard_map/ppermute | solution.py:61
  374.4 13.9 %collective-permute-start.83 = (bf16[128,576]{1,0:T(8,128)(2,1)}, bf16[128,576]{1,0:T(8,128)(2,1)S(1)}, u32[]{:S(2)}, u32[]{:S(2)}) collective-permute-start(bf16[128,576]{1,0:T(8,128)(2,1)} %get-tuple-element.315), channel_id=1, source_target_pairs={{0,4},{1,5},{2,6},{3,7},{4,0},{5,1},{6,2},{7,3},{8,12},{9,13},{10,... | collective-permute-start | bytes 442376 | tf_op jit(solution)/shard_map/ppermute | solution.py:61
  375.9 12.3 %collective-permute-start.84 = (bf16[128,576]{1,0:T(8,128)(2,1)}, bf16[128,576]{1,0:T(8,128)(2,1)S(1)}, u32[]{:S(2)}, u32[]{:S(2)}) collective-permute-start(bf16[128,576]{1,0:T(8,128)(2,1)} %get-tuple-element.316), channel_id=1, source_target_pairs={{0,2},{1,3},{2,4},{3,5},{4,6},{5,7},{6,0},{7,1},{8,10},{9,11},{10,... | collective-permute-start | bytes 442376 | tf_op jit(solution)/shard_map/ppermute | solution.py:61
  395.2 28.5 %collective-permute-start.101 = (bf16[24,3200]{1,0:T(8,128)(2,1)}, bf16[24,3200]{1,0:T(8,128)(2,1)S(1)}, u32[]{:S(2)}, u32[]{:S(2)}) collective-permute-start(bf16[24,3200]{1,0:T(8,128)(2,1)} %get-tuple-element.339), channel_id=1, source_target_pairs={{0,6},{1,7},{2,0},{3,1},{4,2},{5,3},{6,4},{7,5},{8,14},{9,15},{10,... | collective-permute-start | bytes 460808 | tf_op jit(solution)/shard_map/ppermute | solution.py:61
  396.6 27.1 %collective-permute-start.100 = (bf16[24,3200]{1,0:T(8,128)(2,1)}, bf16[24,3200]{1,0:T(8,128)(2,1)S(1)}, u32[]{:S(2)}, u32[]{:S(2)}) collective-permute-start(bf16[24,3200]{1,0:T(8,128)(2,1)} %get-tuple-element.338), channel_id=1, source_target_pairs={{0,4},{1,5},{2,6},{3,7},{4,0},{5,1},{6,2},{7,3},{8,12},{9,13},{10,... | collective-permute-start | bytes 460808 | tf_op jit(solution)/shard_map/ppermute | solution.py:61
  398.1 25.6 %collective-permute-start.99 = (bf16[24,3200]{1,0:T(8,128)(2,1)}, bf16[24,3200]{1,0:T(8,128)(2,1)S(1)}, u32[]{:S(2)}, u32[]{:S(2)}) collective-permute-start(bf16[24,3200]{1,0:T(8,128)(2,1)} %get-tuple-element.337), channel_id=1, source_target_pairs={{0,2},{1,3},{2,4},{3,5},{4,6},{5,7},{6,0},{7,1},{8,10},{9,11},{10,... | collective-permute-start | bytes 460808 | tf_op jit(solution)/shard_map/ppermute | solution.py:61
  403.9 14.8 %collective-permute-start.89 = (bf16[192,1536]{1,0:T(8,128)(2,1)}, bf16[192,1536]{1,0:T(8,128)(2,1)S(1)}, u32[]{:S(2)}, u32[]{:S(2)}) collective-permute-start(bf16[192,1536]{1,0:T(8,128)(2,1)} %get-tuple-element.322), channel_id=1, source_target_pairs={{0,8},{8,0},{16,24},{24,16},{1,9},{9,1},{17,25},{25,17},{2,10},{10... | collective-permute-start | bytes 1769480 | tf_op jit(solution)/shard_map/ppermute | solution.py:1603
  404.7 15.3 %collective-permute-start.90 = (bf16[192,1664]{1,0:T(8,128)(2,1)}, bf16[192,1664]{1,0:T(8,128)(2,1)S(1)}, u32[]{:S(2)}, u32[]{:S(2)}) collective-permute-start(bf16[192,1664]{1,0:T(8,128)(2,1)} %get-tuple-element.324), channel_id=1, source_target_pairs={{0,16},{8,24},{16,0},{24,8},{1,17},{9,25},{17,1},{25,9},{2,18},{10... | collective-permute-start | bytes 1916936 | tf_op jit(solution)/shard_map/ppermute | solution.py:1603
  424.6 16.4 %collective-permute-start.94 = (bf16[96,1536]{1,0:T(8,128)(2,1)S(1)}, bf16[96,1536]{1,0:T(8,128)(2,1)S(1)}, u32[]{:S(2)}, u32[]{:S(2)}) collective-permute-start(bf16[96,1536]{1,0:T(8,128)(2,1)S(1)} %copy-done.66), channel_id=1, source_target_pairs={{0,16},{8,24},{16,0},{24,8},{1,17},{9,25},{17,1},{25,9},{2,18},{10... | collective-permute-start | bytes 884744 | tf_op jit(solution)/shard_map/ppermute | solution.py:1603
  426.1 14.9 %collective-permute-start.95 = (bf16[96,1664]{1,0:T(8,128)(2,1)S(1)}, bf16[96,1664]{1,0:T(8,128)(2,1)S(1)}, u32[]{:S(2)}, u32[]{:S(2)}) collective-permute-start(bf16[96,1664]{1,0:T(8,128)(2,1)S(1)} %copy-done.65), channel_id=1, source_target_pairs={{0,8},{8,0},{16,24},{24,16},{1,9},{9,1},{17,25},{25,17},{2,10},{10... | collective-permute-start | bytes 958472 | tf_op jit(solution)/shard_map/ppermute | solution.py:1603
  447.5 13.8 %collective-permute-start.97 = (bf16[24,3200]{1,0:T(8,128)(2,1)}, bf16[24,3200]{1,0:T(8,128)(2,1)S(1)}, u32[]{:S(2)}, u32[]{:S(2)}) collective-permute-start(bf16[24,3200]{1,0:T(8,128)(2,1)} %get-tuple-element.334), channel_id=1, source_target_pairs={{0,4},{1,5},{2,6},{3,7},{4,0},{5,1},{6,2},{7,3},{8,12},{9,13},{10,... | collective-permute-start | bytes 460808 | tf_op jit(solution)/shard_map/ppermute | solution.py:61
  449.2 12.1 %collective-permute-start.96 = (bf16[24,3200]{1,0:T(8,128)(2,1)}, bf16[24,3200]{1,0:T(8,128)(2,1)S(1)}, u32[]{:S(2)}, u32[]{:S(2)}) collective-permute-start(bf16[24,3200]{1,0:T(8,128)(2,1)} %get-tuple-element.333), channel_id=1, source_target_pairs={{0,2},{1,3},{2,4},{3,5},{4,6},{5,7},{6,0},{7,1},{8,10},{9,11},{10,... | collective-permute-start | bytes 460808 | tf_op jit(solution)/shard_map/ppermute | solution.py:61
  (180 other events, 830.4 us)
Sparse Core Ops, SparseCore 0:
  36.7 49.5 all-gather.3
  91.7 31.0 all-gather.5
  136.0 61.3 all-gather.7
  247.2 55.4 reduce-scatter.3
  309.1 28.4 reduce-scatter.5
  395.3 34.4 reduce-scatter.7

commit v4 on v3

--- a/solution.py
+++ b/solution.py
@@ -456,7 +456,7 @@
 ANY = pl.BlockSpec(memory_space=pl.ANY)
 VMEM = pl.BlockSpec(memory_space=pltpu.VMEM)
 VMEM_BYTES = 56 * 1024 * 1024
-HINT = 4
+HINT = 2
 SIDE_HINT = 40
 SIDE = ("feed_terms", "attend_terms", "slice_terms", "fold", "split", "input_back")
 

time: 480 us -> 475 us (0.990)
    ppermute x33, starting transfers between devices: 57.4 us -> 52.4 us  [chip_shift(): return lax.ppermute(array, 'seq', pairs)]
    unnamed x245 -> x237, local copies, waits for them, and re-layouts: 24.8 us -> 23.5 us
  transfers between devices with their start and end apart: 108 -> 108, of which waited for: 48 -> 50; matrix products, arithmetic and copies ran while one was open for 3% -> 3% of each run, Pallas kernels for 24% -> 24%
where the time goes in v4:
time: 475 us; the launch traced here: 466 us
  waiting for transfers between devices  156 us (33%)
  Pallas kernels  148 us (31%)
  starting transfers between devices  104 us (22%)
  local copies, waits for them, and re-layouts  26.8 us (6%)
  between operations  15.9 us (3%)
  other arithmetic  7.88 us (2%)
  matrix products  7.23 us (2%)
    pallas_call x28, Pallas kernels, run(): pl.pallas_call(kernel, name=name, out_shape=list(outs), in_specs=[VMEM] *...  148 us
    ppermute x33, starting transfers between devices, chip_shift(): return lax.ppermute(array, 'seq', pairs)  52.4 us
    ppermute x16, waiting for transfers between devices, dp_swap(): return lax.ppermute(array, 'dp', [(i, i ^ bit) for i in range(size)])  43.4 us
    ppermute x33, waiting for transfers between devices, chip_shift(): return lax.ppermute(array, 'seq', pairs)  38.5 us
    ppermute x18, waiting for transfers between devices, peer_shift(): return lax.ppermute(array, 'dp', [(i, i ^ bits) for i in range(size)])  37.7 us
    unnamed x237, local copies, waits for them, and re-layouts  23.5 us
    ppermute x18, starting transfers between devices, peer_shift(): return lax.ppermute(array, 'dp', [(i, i ^ bits) for i in range(size)])  22 us
    ppermute x16, starting transfers between devices, dp_swap(): return lax.ppermute(array, 'dp', [(i, i ^ bit) for i in range(size)])  18.2 us
  transfers between devices with their start and end apart: 108, of which 50 were waited for; matrix products, arithmetic and copies ran while one was open for 3% of the time, Pallas kernels for 24%

profile of v4, /device:TPU:0, one launch (start us, length us, event | category | flops | bytes accessed | tf_op | source)
XLA Modules:
  0.0 466.3 jit_solution(3488773325754817748)
XLA Ops:
  10.7 4.0 collective-permute-start.1
  19.6 7.1 %collective-permute-done = bf16[24,3200]{1,0:T(8,128)(2,1)} collective-permute-done((bf16[24,3200]{1,0:T(8,128)(2,1)}, bf16[24,3200]{1,0:T(8,128)(2,1)}, u32[]{:S(2)}, u32[]{:S(2)}) %collective-permute-start) | collective-permute-done | bytes 153632 | tf_op jit(solution)/shard_map/ppermute | solution.py:61
  37.8 7.5 %collective-permute-done.6 = bf16[96,1536]{1,0:T(8,128)(2,1)S(1)} collective-permute-done((bf16[96,1536]{1,0:T(8,128)(2,1)S(1)}, bf16[96,1536]{1,0:T(8,128)(2,1)S(1)}, u32[]{:S(2)}, u32[]{:S(2)}) %collective-permute-start.6) | collective-permute-done | bytes 294944 | tf_op jit(solution)/shard_map/ppermute | solution.py:1603
  47.4 8.9 %collective-permute-done.8.rest_1_.refs_1_ = bf16[192,1536]{1,0:T(8,128)(2,1)S(1)} collective-permute-done((bf16[192,1536]{1,0:T(8,128)(2,1)S(1)}, bf16[192,1536]{1,0:T(8,128)(2,1)S(1)}, u32[]{:S(2)}, u32[]{:S(2)}) %collective-permute-start.8) | collective-permute-done | bytes 589856 | tf_op jit(solution)/shard_map/ppermute | solution.py:1603
  62.5 5.7 %project.2 = (bf16[128,768]{1,0:T(8,128)(2,1)}, bf16[128,576]{1,0:T(8,128)(2,1)}, bf16[128,576]{1,0:T(8,128)(2,1)}, bf16[128,576]{1,0:T(8,128)(2,1)}, bf16[128,576]{1,0:T(8,128)(2,1)}) custom-call(bf16[128,768]{1,0:T(8,128)(2,1)} %bitcast.65, bf16[768,768]{1,0:T(8,128)(2,1)} %constant.70.clone.perm, f32[8,768]{1,0:T(8,128)} %constant.83.bias, ...), custom_call_target="tpu_custom_call" | custom-call | flops 905969664 | bytes 14204928 | tf_op jit(solution)/shard_map/project/pallas_call | solution.py:474
  68.3 3.5 collective-permute-start.14
  73.8 2.8 collective-permute-start.16
  76.6 9.6 %all-gather.4.cloned.1.call-done = bf16[96,9216]{1,0:T(8,128)(2,1)} async-done(((bf16[24,9216]{1,0:T(8,128)(2,1)}), bf16[96,9216]{1,0:T(8,128)(2,1)}) %all-gather.4.cloned.1.call-update) | async-done | bytes 1769488 | tf_op jit(solution)/shard_map/all_gather | solution.py:1578
  91.8 5.6 %collective-permute-done.17 = bf16[96,1536]{1,0:T(8,128)(2,1)S(1)} collective-permute-done((bf16[96,1536]{1,0:T(8,128)(2,1)S(1)}, bf16[96,1536]{1,0:T(8,128)(2,1)S(1)}, u32[]{:S(2)}, u32[]{:S(2)}) %collective-permute-start.17) | collective-permute-done | bytes 294944 | tf_op jit(solution)/shard_map/ppermute | solution.py:1603
  104.7 5.6 %attend.2 = (f32[512,192]{1,0:T(8,128)}, f32[512,128]{1,0:T(8,128)}, bf16[128,192]{1,0:T(8,128)(2,1)}, bf16[128,192]{1,0:T(8,128)(2,1)}, bf16[128,192]{1,0:T(8,128)(2,1)}, /*index=5*/bf16[128,192]{1,0:T(8,128)(2,1)}) custom-call(bf16[128,576]{1,0:T(8,128)(2,1)} %get-tuple-element.189.refs_0_, bf16[128,576]{1,0:T(8,128)(2,1)} %copy-done.88, ...), custom_call_target="tpu_custom_call" | custom-call | flops 805306368 | bytes 4063232 | tf_op jit(solution)/shard_map/attend/pallas_call | solution.py:474
  114.9 4.5 collective-permute-start.30
  120.6 4.3 vectors.1
  128.9 4.6 mix.1
  137.9 4.3 collective-permute-done.33.refs_1_.refs_5_
  142.3 5.6 %collective-permute-done.34.refs_2_.refs_6_ = bf16[128,768]{1,0:T(8,128)(2,1)S(1)} collective-permute-done((bf16[128,768]{1,0:T(8,128)(2,1)S(1)}, bf16[128,768]{1,0:T(8,128)(2,1)S(1)}, u32[]{:S(2)}, u32[]{:S(2)}) %collective-permute-start.34) | collective-permute-done | bytes 196640 | tf_op jit(solution)/shard_map/ppermute | solution.py:1760
  150.7 6.6 %slice_feed.1 = (f32[128,768]{1,0:T(8,128)}, bf16[128,768]{1,0:T(8,128)(2,1)}, bf16[128,768]{1,0:T(8,128)(2,1)}, bf16[128,768]{1,0:T(8,128)(2,1)}, f32[512,768]{1,0:T(8,128)}, /*index=5*/bf16[512,768]{1,0:T(8,128)(2,1)}) custom-call(f32[4,768]{1,0:T(4,128)} %get-tuple-element.205.wide_bias, bf16[128,768]{1,0:T(8,128)(2,1)} %get-tuple-element.206.refs_0_.refs_4_, ...), custom_call_target="tpu_custom_call" | custom-call | flops 2415919104 | bytes 13000704 | tf_op jit(solution)/shard_map/slice_feed/pallas_call | solution.py:474
  161.4 3.2 collective-permute-done.36.refs_1_
  164.6 4.7 %collective-permute-done.37.refs_2_ = bf16[128,768]{1,0:T(8,128)(2,1)S(1)} collective-permute-done((bf16[128,768]{1,0:T(8,128)(2,1)}, bf16[128,768]{1,0:T(8,128)(2,1)S(1)}, u32[]{:S(2)}, u32[]{:S(2)}) %collective-permute-start.37) | collective-permute-done | bytes 196640 | tf_op jit(solution)/shard_map/ppermute | solution.py:1760
  172.7 5.1 %project.3 = (bf16[128,768]{1,0:T(8,128)(2,1)}, bf16[128,576]{1,0:T(8,128)(2,1)}, bf16[128,576]{1,0:T(8,128)(2,1)}, bf16[128,576]{1,0:T(8,128)(2,1)}, bf16[128,576]{1,0:T(8,128)(2,1)}) custom-call(f32[128,768]{1,0:T(8,128)} %get-tuple-element.211.source.hidden, bf16[768,768]{1,0:T(8,128)(2,1)} %constant.70.clone.perm, f32[16,768]{1,0:T(8,128)} %get-tuple-element.212.bias, ...), custom_call_target="tpu_custom_call" | custom-call | flops 905969664 | bytes 14254080 | tf_op jit(solution)/shard_map/project/pallas_call | solution.py:474
  177.9 3.7 collective-permute-start.41
  181.6 3.7 collective-permute-done.39.refs_1_
  185.3 3.9 collective-permute-done.40.refs_2_
  192.0 5.6 %attend.3 = (f32[512,192]{1,0:T(8,128)}, f32[512,128]{1,0:T(8,128)}, bf16[128,192]{1,0:T(8,128)(2,1)}, bf16[128,192]{1,0:T(8,128)(2,1)}, bf16[128,192]{1,0:T(8,128)(2,1)}, /*index=5*/bf16[128,192]{1,0:T(8,128)(2,1)}) custom-call(bf16[128,576]{1,0:T(8,128)(2,1)} %get-tuple-element.216.refs_0_, bf16[128,576]{1,0:T(8,128)(2,1)} %copy-done.96, ...), custom_call_target="tpu_custom_call" | custom-call | flops 805306368 | bytes 4063232 | tf_op jit(solution)/shard_map/attend/pallas_call | solution.py:474
  197.8 3.4 collective-permute-start.46
  203.9 4.2 collective-permute-done.47.refs_2_
  210.4 9.9 %feed.1 = (f32[128,768]{1,0:T(8,128)}, bf16[128,768]{1,0:T(8,128)(2,1)}, bf16[128,768]{1,0:T(8,128)(2,1)}, f32[128,3072]{1,0:T(8,128)}, bf16[128,3072]{1,0:T(8,1...) custom-call(f32[128,768]{1,0:T(8,128)} %get-tuple-element.211.source, ...), custom_call_target="tpu_custom_call" | custom-call | flops 3019898880 | bytes 37199872 | tf_op jit(solution)/shard_map/feed/pallas_call | solution.py:474
  220.3 13.2 %feed_back.1 = (f32[128,768]{1,0:T(8,128)}, bf16[128,3840]{1,0:T(8,128)(2,1)}, bf16[128,768]{1,0:T(8,128)(2,1)}, f32[16,768]{1,0:T(8,128)}, bf16[128,192]{1,0:T(...) custom-call(bf16[128,768]{1,0:T(8,128)(2,1)} %bitcast.64, ...), custom_call_target="tpu_custom_call" | custom-call | flops 3623878656 | bytes 37421056 | tf_op jit(solution)/shard_map/feed_back/pallas_call | solution.py:474
  234.1 3.0 collective-permute-done.50.theirs
  238.3 5.6 %feed_terms.1 = bf16[384,6144]{1,0:T(8,128)(2,1)} custom-call(bf16[128,768]{1,0:T(8,128)(2,1)} %get-tuple-element.237.normed, bf16[128,3072]{1,0:T(8,128)(2,1)} %get-tuple-element.238.act, bf16[128,3840]{1,0:T(8,128)(2,1)} %get-tuple-element.239.gave, bf16[128,2688]{1,0:T(8,128)(2,1)} %copy-done.67, bf16[128,3840]{1,0:T(8,128)(2,1)} %copy-done.66), custom_call_target="tpu_custom_call" | custom-call | flops 48318382080 | bytes 334233600 | tf_op jit(solution)/shard_map/feed_terms/pallas_call | solution.py:474
  254.7 8.3 %attend_back.2 = (bf16[512,192]{1,0:T(8,128)(2,1)}, f32[512,384]{1,0:T(8,128)}, bf16[512,384]{1,0:T(8,128)(2,1)}) custom-call(bf16[128,576]{1,0:T(8,128)(2,1)} %get-tuple-element.216.refs_0_, bf16[128,576]{1,0:T(8,128)(2,1)} %copy-done.96, bf16[128,576]{1,0:T(8,128)(2,1)} %copy-done.97, bf16[128,576]{1,0:T(8,128)(2,1)} %copy-done.98, ...), custom_call_target="tpu_custom_call" | custom-call | flops 2013265920 | bytes 6815744 | tf_op jit(solution)/shard_map/attend_back/pallas_call | solution.py:474
  274.9 12.1 %collective-permute-done.58 = f32[2,3]{1,0:T(2,128)S(1)} collective-permute-done((f32[2,3]{1,0:T(2,128)S(1)}, f32[2,3]{1,0:T(2,128)S(1)}, u32[]{:S(2)}, u32[]{:S(2)}) %collective-permute-start.58) | collective-permute-done | bytes 56 | tf_op jit(solution)/shard_map/ppermute | solution.py:1926
  287.9 6.7 %project_back.1 = (f32[128,768]{1,0:T(8,128)}, bf16[128,2304]{1,0:T(8,128)(2,1)}, f32[16,768]{1,0:T(8,128)}) custom-call(f32[128,768]{1,0:T(8,128)} %get-tuple-element.234.grad_one, bf16[768,768]{1,0:T(8,128)(2,1)} %constant.70.clone.perm, f32[16,768]{1,0:T(8,128)} %get-tuple-element.235.sums, bf16[128,576]{1,0:T(8,128)(2,1)} %get-tuple-element.256.refs_0_, ...), custom_call_target="tpu_custom_call" | custom-call | flops 905969664 | bytes 15925248 | tf_op jit(solution)/shard_map/project_back/pallas_call | solution.py:474
  307.5 3.8 attend_terms.2
  314.3 7.7 %slice_back.1 = (f32[128,768]{1,0:T(8,128)}, bf16[128,768]{1,0:T(8,128)(2,1)}, bf16[128,768]{1,0:T(8,128)(2,1)}, bf16[128,768]{1,0:T(8,128)(2,1)}, bf16[512,768]...) custom-call(bf16[128,768]{1,0:T(8,128)(2,1)} %get-tuple-element.267.refs_0_, ...), custom_call_target="tpu_custom_call" | custom-call | flops 2415919104 | bytes 20889600 | tf_op jit(solution)/shard_map/slice_back/pallas_call | solution.py:474
  327.0 3.9 collective-permute-done.70.refs_1_
  330.9 4.4 collective-permute-done.71.refs_2_
  336.1 5.0 %mix_back.1 = (f32[128,768]{1,0:T(8,128)}, bf16[128,768]{1,0:T(8,128)(2,1)}, f32[16,768]{1,0:T(8,128)}, bf16[128,192]{1,0:T(8,128)(2,1)}, bf16[128,192]{1,0:T(8,...) custom-call(f32[128,768]{1,0:T(8,128)} %get-tuple-element.263.grad_two, ...), custom_call_target="tpu_custom_call" | custom-call | flops 905969664 | bytes 13008896 | tf_op jit(solution)/shard_map/mix_back/pallas_call | solution.py:474
  351.1 8.3 %attend_back.3 = (bf16[512,192]{1,0:T(8,128)(2,1)}, f32[512,384]{1,0:T(8,128)}, bf16[512,384]{1,0:T(8,128)(2,1)}) custom-call(bf16[128,576]{1,0:T(8,128)(2,1)} %get-tuple-element.189.refs_0_, bf16[128,576]{1,0:T(8,128)(2,1)} %copy-done.88, bf16[128,576]{1,0:T(8,128)(2,1)} %copy-done.89, bf16[128,576]{1,0:T(8,128)(2,1)} %copy-done.90, ...), custom_call_target="tpu_custom_call" | custom-call | flops 2013265920 | bytes 6815744 | tf_op jit(solution)/shard_map/attend_back/pallas_call | solution.py:474
  361.6 2.8 fold.2
  373.0 6.7 %slice_terms.1 = bf16[384,1536]{1,0:T(8,128)(2,1)} custom-call(bf16[384,384]{1,0:T(8,128)(2,1)} %constant.72.clone.perm_rows, bf16[384,384]{1,0:T(8,128)(2,1)} %constant.73.clone.perm_units, bf16[128,768]{1,0:T(8,128)(2,1)} %get-tuple-element.267.refs_0_, bf16[128,768]{1,0:T(8,128)(2,1)} %copy-done.82, bf16[128,768]{1,0:T(8,128)(2,1)} %copy-done.80, ...), custom_call_target="tpu_custom_call" | custom-call | flops 48318382080 | bytes 290979840 | tf_op jit(solution)/shard_map/slice_terms/pallas_call | solution.py:474
  382.9 2.8 collective-permute-done.83.refs_2_
  386.5 5.1 %collect.1 = (bf16[128,2304]{1,0:T(8,128)(2,1)}, f32[16,768]{1,0:T(8,128)}) custom-call(bf16[768,768]{1,0:T(8,128)(2,1)} %constant.70.clone.perm, bf16[768,768]{1,0:T(8,128)(2,1)} %constant.71.clone.perm_wide, f32[8,768]{1,0:T(8,128)} %get-tuple-element.287.feed_sums, f32[16,768]{1,0:T(8,128)} %get-tuple-element.288.sums, ...), custom_call_target="tpu_custom_call" | custom-call | bytes 7323648 | tf_op jit(solution)/shard_map/collect/pallas_call | solution.py:474
  397.9 3.9 attend_terms.3
  404.5 12.1 %collective-permute-done.89.refs_1_ = bf16[192,1536]{1,0:T(8,128)(2,1)S(1)} collective-permute-done((bf16[192,1536]{1,0:T(8,128)(2,1)}, bf16[192,1536]{1,0:T(8,128)(2,1)S(1)}, u32[]{:S(2)}, u32[]{:S(2)}) %collective-permute-start.89) | collective-permute-done | bytes 589856 | tf_op jit(solution)/shard_map/ppermute | solution.py:1603
  418.7 2.9 fold.3
  424.2 6.5 %input_back.1 = bf16[128,768]{1,0:T(8,128)(2,1)} custom-call(f32[128,768]{1,0:T(8,128)} %get-tuple-element.326.grad_one, bf16[768,768]{1,0:T(8,128)(2,1)} %constant.70.clone.perm, bf16[128,2304]{1,0:T(8,128)(2,1)} %get-tuple-element.317.project, bf16[192,1536]{1,0:T(8,128)(2,1)} %copy-done.17, bf16[192,1536]{1,0:T(8,128)(2,1)} %copy-done.27, ...), custom_call_target="tpu_custom_call" | custom-call | flops 18119393280 | bytes 290979840 | tf_op jit(solution)/shard_map/input_back/pallas_call | solution.py:474
  441.8 3.4 collective-permute-start.98
  449.6 7.1 %collective-permute-done.97 = bf16[24,3200]{1,0:T(8,128)(2,1)S(1)} collective-permute-done((bf16[24,3200]{1,0:T(8,128)(2,1)}, bf16[24,3200]{1,0:T(8,128)(2,1)S(1)}, u32[]{:S(2)}, u32[]{:S(2)}) %collective-permute-start.97) | collective-permute-done | bytes 153632 | tf_op jit(solution)/shard_map/ppermute | solution.py:61
  (506 shorter events, 177.0 us)
Async XLA Ops:
  7.2 79.0 %all-gather.4.cloned.1.call-start = ((), (), s32[]{:S(2)}) async-start(), calls=%async_computation.3 | async-start | bytes 2211840 | tf_op jit(solution)/shard_map/all_gather | solution.py:1578
  10.7 24.4 %collective-permute-start.1 = (bf16[24,3200]{1,0:T(8,128)(2,1)}, bf16[24,3200]{1,0:T(8,128)(2,1)}, u32[]{:S(2)}, u32[]{:S(2)}) collective-permute-start(bf16[24,3200]{1,0:T(8,128)(2,1)} %fusion.6), channel_id=1, source_target_pairs={{0,4},{1,5},{2,6},{3,7},{4,0},{5,1},{6,2},{7,3},{8,12},{9,13},{10,... | collective-permute-start | bytes 460808 | tf_op jit(solution)/shard_map/ppermute | solution.py:61
  14.7 20.3 %collective-permute-start.2 = (bf16[24,3200]{1,0:T(8,128)(2,1)}, bf16[24,3200]{1,0:T(8,128)(2,1)}, u32[]{:S(2)}, u32[]{:S(2)}) collective-permute-start(bf16[24,3200]{1,0:T(8,128)(2,1)} %fusion.6), channel_id=1, source_target_pairs={{0,6},{1,7},{2,0},{3,1},{4,2},{5,3},{6,4},{7,5},{8,14},{9,15},{10,... | collective-permute-start | bytes 460808 | tf_op jit(solution)/shard_map/ppermute | solution.py:61
  16.0 10.7 %collective-permute-start = (bf16[24,3200]{1,0:T(8,128)(2,1)}, bf16[24,3200]{1,0:T(8,128)(2,1)}, u32[]{:S(2)}, u32[]{:S(2)}) collective-permute-start(bf16[24,3200]{1,0:T(8,128)(2,1)} %fusion.6), channel_id=1, source_target_pairs={{0,2},{1,3},{2,4},{3,5},{4,6},{5,7},{6,0},{7,1},{8,10},{9,11},{10,... | collective-permute-start | bytes 460808 | tf_op jit(solution)/shard_map/ppermute | solution.py:61
  36.5 97.0 %all-gather.6.cloned.1.call-start = ((), (), s32[]{:S(2)}) async-start(), calls=%async_computation.4 | async-start | bytes 1474560 | tf_op jit(solution)/shard_map/all_gather | solution.py:1578
  45.5 12.2 %collective-permute-start.9 = (bf16[192,1664]{1,0:T(8,128)(2,1)S(1)}, bf16[192,1664]{1,0:T(8,128)(2,1)S(1)}, u32[]{:S(2)}, u32[]{:S(2)}) collective-permute-start(bf16[192,1664]{1,0:T(8,128)(2,1)S(1)} %maximum_select_fusion.rest_4_.refs_0_.refs_4_), channel_id=1, source_target_pairs={{0,8},{8,0},{16,24},{24,16},{1,9},{9,1},{17,25},{25,17},{2,10},{10... | collective-permute-start | bytes 1916936 | tf_op jit(solution)/shard_map/ppermute | solution.py:1603
  47.4 13.3 %collective-permute-start.12 = (bf16[192,1664]{1,0:T(8,128)(2,1)S(1)}, bf16[192,1664]{1,0:T(8,128)(2,1)S(1)}, u32[]{:S(2)}, u32[]{:S(2)}) collective-permute-start(bf16[192,1664]{1,0:T(8,128)(2,1)S(1)} %maximum_select_fusion.rest_4_.refs_0_.refs_4_), channel_id=1, source_target_pairs={{0,1},{1,0},{2,3},{3,2},{4,5},{5,4},{6,7},{7,6},{8,9},{9,8},{10,11... | collective-permute-start | bytes 1916936 | tf_op jit(solution)/shard_map/ppermute | solution.py:54
  68.3 17.9 %collective-permute-start.14 = (bf16[128,576]{1,0:T(8,128)(2,1)}, bf16[128,576]{1,0:T(8,128)(2,1)S(1)}, u32[]{:S(2)}, u32[]{:S(2)}) collective-permute-start(bf16[128,576]{1,0:T(8,128)(2,1)} %get-tuple-element.183), channel_id=1, source_target_pairs={{0,2},{1,3},{2,4},{3,5},{4,6},{5,7},{6,0},{7,1},{8,10},{9,11},{10,... | collective-permute-start | bytes 442376 | tf_op jit(solution)/shard_map/ppermute | solution.py:61
  71.8 16.1 %collective-permute-start.15 = (bf16[128,576]{1,0:T(8,128)(2,1)}, bf16[128,576]{1,0:T(8,128)(2,1)S(1)}, u32[]{:S(2)}, u32[]{:S(2)}) collective-permute-start(bf16[128,576]{1,0:T(8,128)(2,1)} %get-tuple-element.184), channel_id=1, source_target_pairs={{0,4},{1,5},{2,6},{3,7},{4,0},{5,1},{6,2},{7,3},{8,12},{9,13},{10,... | collective-permute-start | bytes 442376 | tf_op jit(solution)/shard_map/ppermute | solution.py:61
  73.8 14.1 %collective-permute-start.16 = (bf16[128,576]{1,0:T(8,128)(2,1)}, bf16[128,576]{1,0:T(8,128)(2,1)S(1)}, u32[]{:S(2)}, u32[]{:S(2)}) collective-permute-start(bf16[128,576]{1,0:T(8,128)(2,1)} %get-tuple-element.185), channel_id=1, source_target_pairs={{0,6},{1,7},{2,0},{3,1},{4,2},{5,3},{6,4},{7,5},{8,14},{9,15},{10,... | collective-permute-start | bytes 442376 | tf_op jit(solution)/shard_map/ppermute | solution.py:61
  91.5 106.0 %all-gather.8.cloned.1.call-start = ((), (), s32[]{:S(2)}) async-start(), calls=%async_computation.5 | async-start | bytes 5898240 | tf_op jit(solution)/shard_map/all_gather | solution.py:1899
  91.7 28.7 %collective-permute-start.25 = (bf16[96,6144]{1,0:T(8,128)(2,1)S(1)}, bf16[96,6144]{1,0:T(8,128)(2,1)S(1)}, u32[]{:S(2)}, u32[]{:S(2)}) collective-permute-start(bf16[96,6144]{1,0:T(8,128)(2,1)S(1)} %slice.123.refs_4_.refs_10_), channel_id=1, source_target_pairs={{0,1},{1,0},{2,3},{3,2},{4,5},{5,4},{6,7},{7,6},{8,9},{9,8},{10,11... | collective-permute-start | bytes 3538952 | tf_op jit(solution)/shard_map/ppermute | solution.py:54
  98.8 14.1 %collective-permute-start.23 = (bf16[192,1536]{1,0:T(8,128)(2,1)S(1)}, bf16[192,1536]{1,0:T(8,128)(2,1)S(1)}, u32[]{:S(2)}, u32[]{:S(2)}) collective-permute-start(bf16[192,1536]{1,0:T(8,128)(2,1)S(1)} %maximum_select_fusion.2.rest_0_.refs_4_), channel_id=1, source_target_pairs={{0,16},{8,24},{16,0},{24,8},{1,17},{9,25},{17,1},{25,9},{2,18},{10... | collective-permute-start | bytes 1769480 | tf_op jit(solution)/shard_map/ppermute | solution.py:1603
  100.5 13.9 %collective-permute-start.24 = (bf16[192,1536]{1,0:T(8,128)(2,1)S(1)}, bf16[192,1536]{1,0:T(8,128)(2,1)S(1)}, u32[]{:S(2)}, u32[]{:S(2)}) collective-permute-start(bf16[192,1536]{1,0:T(8,128)(2,1)S(1)} %maximum_select_fusion.3.rest_4_.refs_4_.refs_0_.refs_8_), channel_id=1, source_target_pairs={{0,8},{8,0},{16,24},{24,16},{1,9},{9,1},{17,25},{25,17},{2,10},{10... | collective-permute-start | bytes 1769480 | tf_op jit(solution)/shard_map/ppermute | solution.py:1603
  103.8 11.1 %collective-permute-start.26 = (bf16[192,1536]{1,0:T(8,128)(2,1)S(1)}, bf16[192,1536]{1,0:T(8,128)(2,1)S(1)}, u32[]{:S(2)}, u32[]{:S(2)}) collective-permute-start(bf16[192,1536]{1,0:T(8,128)(2,1)S(1)} %maximum_select_fusion.2.rest_0_.refs_4_), channel_id=1, source_target_pairs={{0,1},{1,0},{2,3},{3,2},{4,5},{5,4},{6,7},{7,6},{8,9},{9,8},{10,11... | collective-permute-start | bytes 1769480 | tf_op jit(solution)/shard_map/ppermute | solution.py:54
  104.1 15.4 %collective-permute-start.28 = (bf16[192,1536]{1,0:T(8,128)(2,1)S(1)}, bf16[192,1536]{1,0:T(8,128)(2,1)S(1)}, u32[]{:S(2)}, u32[]{:S(2)}) collective-permute-start(bf16[192,1536]{1,0:T(8,128)(2,1)S(1)} %maximum_select_fusion.3.rest_4_.refs_4_.refs_0_.refs_8_), channel_id=1, source_target_pairs={{0,1},{1,0},{2,3},{3,2},{4,5},{5,4},{6,7},{7,6},{8,9},{9,8},{10,11... | collective-permute-start | bytes 1769480 | tf_op jit(solution)/shard_map/ppermute | solution.py:54
  114.4 10.7 %collective-permute-start.29 = (bf16[192,1536]{1,0:T(8,128)(2,1)S(1)}, bf16[192,1536]{1,0:T(8,128)(2,1)S(1)}, u32[]{:S(2)}, u32[]{:S(2)}) collective-permute-start(bf16[192,1536]{1,0:T(8,128)(2,1)S(1)} %collective-permute-done.24.rest_5_.refs_5_.refs_1_.refs_9_), channel_id=1, source_target_pairs={{0,1},{1,0},{2,3},{3,2},{4,5},{5,4},{6,7},{7,6},{8,9},{9,8},{10,11... | collective-permute-start | bytes 1769480 | tf_op jit(solution)/shard_map/ppermute | solution.py:54
  114.9 11.0 %collective-permute-start.30 = (bf16[128,192]{1,0:T(8,128)(2,1)}, bf16[128,192]{1,0:T(8,128)(2,1)S(1)}, u32[]{:S(2)}, u32[]{:S(2)}) collective-permute-start(bf16[128,192]{1,0:T(8,128)(2,1)} %get-tuple-element.200), channel_id=1, source_target_pairs={{0,6},{1,7},{2,0},{3,1},{4,2},{5,3},{6,4},{7,5},{8,14},{9,15},{10,... | collective-permute-start | bytes 147464 | tf_op jit(solution)/shard_map/ppermute | solution.py:61
  133.6 172.9 %reduce-scatter.4.cloned.1.call-start = ((), (), s32[]{:S(2)}) async-start(), calls=%async_computation.6 | async-start | bytes 5898240 | tf_op jit(solution)/shard_map/reduce_scatter | solution.py:1969
  135.9 11.9 %collective-permute-start.34 = (bf16[128,768]{1,0:T(8,128)(2,1)S(1)}, bf16[128,768]{1,0:T(8,128)(2,1)S(1)}, u32[]{:S(2)}, u32[]{:S(2)}) collective-permute-start(bf16[128,768]{1,0:T(8,128)(2,1)S(1)} %copy-done.75), channel_id=1, source_target_pairs={{0,16},{8,24},{16,0},{24,8},{1,17},{9,25},{17,1},{25,9},{2,18},{10... | collective-permute-start | bytes 589832 | tf_op jit(solution)/shard_map/ppermute | solution.py:1760
  137.4 12.7 %collective-permute-start.35 = (bf16[128,768]{1,0:T(8,128)(2,1)S(1)}, bf16[128,768]{1,0:T(8,128)(2,1)S(1)}, u32[]{:S(2)}, u32[]{:S(2)}) collective-permute-start(bf16[128,768]{1,0:T(8,128)(2,1)S(1)} %copy-done.75), channel_id=1, source_target_pairs={{0,24},{8,16},{16,8},{24,0},{1,25},{9,17},{17,9},{25,1},{2,26},{10... | collective-permute-start | bytes 589832 | tf_op jit(solution)/shard_map/ppermute | solution.py:1760
  177.8 11.4 %collective-permute-start.40 = (bf16[128,576]{1,0:T(8,128)(2,1)}, bf16[128,576]{1,0:T(8,128)(2,1)S(1)}, u32[]{:S(2)}, u32[]{:S(2)}) collective-permute-start(bf16[128,576]{1,0:T(8,128)(2,1)} %get-tuple-element.218), channel_id=1, source_target_pairs={{0,4},{1,5},{2,6},{3,7},{4,0},{5,1},{6,2},{7,3},{8,12},{9,13},{10,... | collective-permute-start | bytes 442376 | tf_op jit(solution)/shard_map/ppermute | solution.py:61
  177.9 11.4 %collective-permute-start.41 = (bf16[128,576]{1,0:T(8,128)(2,1)}, bf16[128,576]{1,0:T(8,128)(2,1)S(1)}, u32[]{:S(2)}, u32[]{:S(2)}) collective-permute-start(bf16[128,576]{1,0:T(8,128)(2,1)} %get-tuple-element.219), channel_id=1, source_target_pairs={{0,6},{1,7},{2,0},{3,1},{4,2},{5,3},{6,4},{7,5},{8,14},{9,15},{10,... | collective-permute-start | bytes 442376 | tf_op jit(solution)/shard_map/ppermute | solution.py:61
  244.0 105.3 %reduce-scatter.6.cloned.1.call-start = ((), (), s32[]{:S(2)}) async-start(), calls=%async_computation.7 | async-start | bytes 1474560 | tf_op jit(solution)/shard_map/reduce_scatter | solution.py:1584
  269.7 17.4 %collective-permute-start.59 = (bf16[128,576]{1,0:T(8,128)(2,1)}, bf16[128,576]{1,0:T(8,128)(2,1)S(1)}, u32[]{:S(2)}, u32[]{:S(2)}) collective-permute-start(bf16[128,576]{1,0:T(8,128)(2,1)} %get-tuple-element.257), channel_id=1, source_target_pairs={{0,6},{1,7},{2,0},{3,1},{4,2},{5,3},{6,4},{7,5},{8,14},{9,15},{10,... | collective-permute-start | bytes 442376 | tf_op jit(solution)/shard_map/ppermute | solution.py:61
  272.0 15.1 %collective-permute-start.60 = (bf16[128,576]{1,0:T(8,128)(2,1)}, bf16[128,576]{1,0:T(8,128)(2,1)S(1)}, u32[]{:S(2)}, u32[]{:S(2)}) collective-permute-start(bf16[128,576]{1,0:T(8,128)(2,1)} %get-tuple-element.258), channel_id=1, source_target_pairs={{0,4},{1,5},{2,6},{3,7},{4,0},{5,1},{6,2},{7,3},{8,12},{9,13},{10,... | collective-permute-start | bytes 442376 | tf_op jit(solution)/shard_map/ppermute | solution.py:61
  272.5 14.6 %collective-permute-start.61 = (bf16[128,576]{1,0:T(8,128)(2,1)}, bf16[128,576]{1,0:T(8,128)(2,1)S(1)}, u32[]{:S(2)}, u32[]{:S(2)}) collective-permute-start(bf16[128,576]{1,0:T(8,128)(2,1)} %get-tuple-element.259), channel_id=1, source_target_pairs={{0,2},{1,3},{2,4},{3,5},{4,6},{5,7},{6,0},{7,1},{8,10},{9,11},{10,... | collective-permute-start | bytes 442376 | tf_op jit(solution)/shard_map/ppermute | solution.py:61
  272.6 14.4 %collective-permute-start.58 = (f32[2,3]{1,0:T(2,128)S(1)}, f32[2,3]{1,0:T(2,128)S(1)}, u32[]{:S(2)}, u32[]{:S(2)}) collective-permute-start(f32[2,3]{1,0:T(2,128)S(1)} %fusion.33), channel_id=1, source_target_pairs={{0,4},{1,5},{2,6},{3,7},{4,0},{5,1},{6,2},{7,3},{8,12},{9,13},{10,... | collective-permute-start | bytes 80 | tf_op jit(solution)/shard_map/ppermute | solution.py:1926
  294.6 12.0 %collective-permute-start.63 = (bf16[128,2304]{1,0:T(8,128)(2,1)}, bf16[128,2304]{1,0:T(8,128)(2,1)S(1)}, u32[]{:S(2)}, u32[]{:S(2)}) collective-permute-start(bf16[128,2304]{1,0:T(8,128)(2,1)} %get-tuple-element.269.project), channel_id=1, source_target_pairs={{0,1},{1,0},{2,3},{3,2},{4,5},{5,4},{6,7},{7,6},{8,9},{9,8},{10,11... | collective-permute-start | bytes 1769480 | tf_op jit(solution)/shard_map/ppermute | solution.py:54
  306.5 124.2 %reduce-scatter.8.cloned.1.call-start = ((), (), s32[]{:S(2)}) async-start(), calls=%async_computation.8 | async-start | bytes 1474560 | tf_op jit(solution)/shard_map/reduce_scatter | solution.py:1584
  322.0 49.5 %collective-permute-start.81 = (bf16[512,2304]{1,0:T(8,128)(2,1)}, bf16[512,2304]{1,0:T(8,128)(2,1)}, u32[]{:S(2)}, u32[]{:S(2)}) collective-permute-start(bf16[512,2304]{1,0:T(8,128)(2,1)} %get-tuple-element.312), channel_id=1, source_target_pairs={{0,1},{1,0},{2,3},{3,2},{4,5},{5,4},{6,7},{7,6},{8,9},{9,8},{10,11... | collective-permute-start | bytes 7077896 | tf_op jit(solution)/shard_map/ppermute | solution.py:54
  324.0 11.3 %collective-permute-start.71 = (bf16[128,768]{1,0:T(8,128)(2,1)}, bf16[128,768]{1,0:T(8,128)(2,1)S(1)}, u32[]{:S(2)}, u32[]{:S(2)}) collective-permute-start(bf16[128,768]{1,0:T(8,128)(2,1)} %get-tuple-element.283), channel_id=1, source_target_pairs={{0,16},{8,24},{16,0},{24,8},{1,17},{9,25},{17,1},{25,9},{2,18},{10... | collective-permute-start | bytes 589832 | tf_op jit(solution)/shard_map/ppermute | solution.py:1760
  341.2 19.4 %collective-permute-start.77 = (bf16[192,1664]{1,0:T(8,128)(2,1)S(1)}, bf16[192,1664]{1,0:T(8,128)(2,1)S(1)}, u32[]{:S(2)}, u32[]{:S(2)}) collective-permute-start(bf16[192,1664]{1,0:T(8,128)(2,1)S(1)} %copy-done.69), channel_id=1, source_target_pairs={{0,16},{8,24},{16,0},{24,8},{1,17},{9,25},{17,1},{25,9},{2,18},{10... | collective-permute-start | bytes 1916936 | tf_op jit(solution)/shard_map/ppermute | solution.py:1603
  348.0 12.5 %collective-permute-start.76 = (bf16[192,1536]{1,0:T(8,128)(2,1)S(1)}, bf16[192,1536]{1,0:T(8,128)(2,1)S(1)}, u32[]{:S(2)}, u32[]{:S(2)}) collective-permute-start(bf16[192,1536]{1,0:T(8,128)(2,1)S(1)} %copy-done.70), channel_id=1, source_target_pairs={{0,8},{8,0},{16,24},{24,16},{1,9},{9,1},{17,25},{25,17},{2,10},{10... | collective-permute-start | bytes 1769480 | tf_op jit(solution)/shard_map/ppermute | solution.py:1603
  364.4 15.3 %collective-permute-start.79 = (bf16[96,1536]{1,0:T(8,128)(2,1)}, bf16[96,1536]{1,0:T(8,128)(2,1)S(1)}, u32[]{:S(2)}, u32[]{:S(2)}) collective-permute-start(bf16[96,1536]{1,0:T(8,128)(2,1)} %get-tuple-element.307), channel_id=1, source_target_pairs={{0,16},{8,24},{16,0},{24,8},{1,17},{9,25},{17,1},{25,9},{2,18},{10... | collective-permute-start | bytes 884744 | tf_op jit(solution)/shard_map/ppermute | solution.py:1603
  366.1 13.6 %collective-permute-start.80 = (bf16[96,1664]{1,0:T(8,128)(2,1)}, bf16[96,1664]{1,0:T(8,128)(2,1)S(1)}, u32[]{:S(2)}, u32[]{:S(2)}) collective-permute-start(bf16[96,1664]{1,0:T(8,128)(2,1)} %get-tuple-element.309), channel_id=1, source_target_pairs={{0,8},{8,0},{16,24},{24,16},{1,9},{9,1},{17,25},{25,17},{2,10},{10... | collective-permute-start | bytes 958472 | tf_op jit(solution)/shard_map/ppermute | solution.py:1603
  369.8 13.1 %collective-permute-start.82 = (bf16[128,576]{1,0:T(8,128)(2,1)}, bf16[128,576]{1,0:T(8,128)(2,1)S(1)}, u32[]{:S(2)}, u32[]{:S(2)}) collective-permute-start(bf16[128,576]{1,0:T(8,128)(2,1)} %get-tuple-element.314), channel_id=1, source_target_pairs={{0,6},{1,7},{2,0},{3,1},{4,2},{5,3},{6,4},{7,5},{8,14},{9,15},{10,... | collective-permute-start | bytes 442376 | tf_op jit(solution)/shard_map/ppermute | solution.py:61
  371.0 14.7 %collective-permute-start.83 = (bf16[128,576]{1,0:T(8,128)(2,1)}, bf16[128,576]{1,0:T(8,128)(2,1)S(1)}, u32[]{:S(2)}, u32[]{:S(2)}) collective-permute-start(bf16[128,576]{1,0:T(8,128)(2,1)} %get-tuple-element.315), channel_id=1, source_target_pairs={{0,4},{1,5},{2,6},{3,7},{4,0},{5,1},{6,2},{7,3},{8,12},{9,13},{10,... | collective-permute-start | bytes 442376 | tf_op jit(solution)/shard_map/ppermute | solution.py:61
  371.5 14.2 %collective-permute-start.84 = (bf16[128,576]{1,0:T(8,128)(2,1)}, bf16[128,576]{1,0:T(8,128)(2,1)S(1)}, u32[]{:S(2)}, u32[]{:S(2)}) collective-permute-start(bf16[128,576]{1,0:T(8,128)(2,1)} %get-tuple-element.316), channel_id=1, source_target_pairs={{0,2},{1,3},{2,4},{3,5},{4,6},{5,7},{6,0},{7,1},{8,10},{9,11},{10,... | collective-permute-start | bytes 442376 | tf_op jit(solution)/shard_map/ppermute | solution.py:61
  392.6 29.0 %collective-permute-start.101 = (bf16[24,3200]{1,0:T(8,128)(2,1)}, bf16[24,3200]{1,0:T(8,128)(2,1)S(1)}, u32[]{:S(2)}, u32[]{:S(2)}) collective-permute-start(bf16[24,3200]{1,0:T(8,128)(2,1)} %get-tuple-element.339), channel_id=1, source_target_pairs={{0,6},{1,7},{2,0},{3,1},{4,2},{5,3},{6,4},{7,5},{8,14},{9,15},{10,... | collective-permute-start | bytes 460808 | tf_op jit(solution)/shard_map/ppermute | solution.py:61
  393.9 27.7 %collective-permute-start.100 = (bf16[24,3200]{1,0:T(8,128)(2,1)}, bf16[24,3200]{1,0:T(8,128)(2,1)S(1)}, u32[]{:S(2)}, u32[]{:S(2)}) collective-permute-start(bf16[24,3200]{1,0:T(8,128)(2,1)} %get-tuple-element.338), channel_id=1, source_target_pairs={{0,4},{1,5},{2,6},{3,7},{4,0},{5,1},{6,2},{7,3},{8,12},{9,13},{10,... | collective-permute-start | bytes 460808 | tf_op jit(solution)/shard_map/ppermute | solution.py:61
  396.0 25.6 %collective-permute-start.99 = (bf16[24,3200]{1,0:T(8,128)(2,1)}, bf16[24,3200]{1,0:T(8,128)(2,1)S(1)}, u32[]{:S(2)}, u32[]{:S(2)}) collective-permute-start(bf16[24,3200]{1,0:T(8,128)(2,1)} %get-tuple-element.337), channel_id=1, source_target_pairs={{0,2},{1,3},{2,4},{3,5},{4,6},{5,7},{6,0},{7,1},{8,10},{9,11},{10,... | collective-permute-start | bytes 460808 | tf_op jit(solution)/shard_map/ppermute | solution.py:61
  401.8 14.8 %collective-permute-start.89 = (bf16[192,1536]{1,0:T(8,128)(2,1)}, bf16[192,1536]{1,0:T(8,128)(2,1)S(1)}, u32[]{:S(2)}, u32[]{:S(2)}) collective-permute-start(bf16[192,1536]{1,0:T(8,128)(2,1)} %get-tuple-element.322), channel_id=1, source_target_pairs={{0,8},{8,0},{16,24},{24,16},{1,9},{9,1},{17,25},{25,17},{2,10},{10... | collective-permute-start | bytes 1769480 | tf_op jit(solution)/shard_map/ppermute | solution.py:1603
  402.6 15.3 %collective-permute-start.90 = (bf16[192,1664]{1,0:T(8,128)(2,1)}, bf16[192,1664]{1,0:T(8,128)(2,1)S(1)}, u32[]{:S(2)}, u32[]{:S(2)}) collective-permute-start(bf16[192,1664]{1,0:T(8,128)(2,1)} %get-tuple-element.324), channel_id=1, source_target_pairs={{0,16},{8,24},{16,0},{24,8},{1,17},{9,25},{17,1},{25,9},{2,18},{10... | collective-permute-start | bytes 1916936 | tf_op jit(solution)/shard_map/ppermute | solution.py:1603
  421.8 16.9 %collective-permute-start.94 = (bf16[96,1536]{1,0:T(8,128)(2,1)}, bf16[96,1536]{1,0:T(8,128)(2,1)S(1)}, u32[]{:S(2)}, u32[]{:S(2)}) collective-permute-start(bf16[96,1536]{1,0:T(8,128)(2,1)} %get-tuple-element.329), channel_id=1, source_target_pairs={{0,16},{8,24},{16,0},{24,8},{1,17},{9,25},{17,1},{25,9},{2,18},{10... | collective-permute-start | bytes 884744 | tf_op jit(solution)/shard_map/ppermute | solution.py:1603
  423.6 15.1 %collective-permute-start.95 = (bf16[96,1664]{1,0:T(8,128)(2,1)S(1)}, bf16[96,1664]{1,0:T(8,128)(2,1)S(1)}, u32[]{:S(2)}, u32[]{:S(2)}) collective-permute-start(bf16[96,1664]{1,0:T(8,128)(2,1)S(1)} %copy-done.73), channel_id=1, source_target_pairs={{0,8},{8,0},{16,24},{24,16},{1,9},{9,1},{17,25},{25,17},{2,10},{10... | collective-permute-start | bytes 958472 | tf_op jit(solution)/shard_map/ppermute | solution.py:1603
  445.2 11.5 %collective-permute-start.97 = (bf16[24,3200]{1,0:T(8,128)(2,1)}, bf16[24,3200]{1,0:T(8,128)(2,1)S(1)}, u32[]{:S(2)}, u32[]{:S(2)}) collective-permute-start(bf16[24,3200]{1,0:T(8,128)(2,1)} %get-tuple-element.334), channel_id=1, source_target_pairs={{0,4},{1,5},{2,6},{3,7},{4,0},{5,1},{6,2},{7,3},{8,12},{9,13},{10,... | collective-permute-start | bytes 460808 | tf_op jit(solution)/shard_map/ppermute | solution.py:61
  445.2 11.5 %collective-permute-start.96 = (bf16[24,3200]{1,0:T(8,128)(2,1)}, bf16[24,3200]{1,0:T(8,128)(2,1)S(1)}, u32[]{:S(2)}, u32[]{:S(2)}) collective-permute-start(bf16[24,3200]{1,0:T(8,128)(2,1)} %get-tuple-element.333), channel_id=1, source_target_pairs={{0,2},{1,3},{2,4},{3,5},{4,6},{5,7},{6,0},{7,1},{8,10},{9,11},{10,... | collective-permute-start | bytes 460808 | tf_op jit(solution)/shard_map/ppermute | solution.py:61
  (176 other events, 810.0 us)
Sparse Core Ops, SparseCore 0:
  36.7 49.4 all-gather.3
  91.6 30.8 all-gather.5
  133.7 60.0 all-gather.7
  244.2 55.8 reduce-scatter.3
  306.6 28.3 reduce-scatter.5
  392.7 34.8 reduce-scatter.7

commit v5 on v4

--- a/solution.py
+++ b/solution.py
@@ -1969,9 +1969,9 @@
     feed_sum_one = lax.psum_scatter(feed_term, "dp", scatter_dimension=0, tiled=True)
     grads[0] = after(grads[0], feed_term, totals, hidden_output)
     grad_q, near, far = back_attend(1, grads)
-    totals = sum_more(totals, grad_q)
-    pieces = back_combine(after(grad_q, totals), near, core_swap(far))
-    totals = sum_more(totals, pieces[0])
+    pieces = back_combine(grad_q, near, core_swap(far))
+    for _ in range(2):
+        totals = sum_more(totals, pieces[0])
     pieces[0] = after(pieces[0], totals)
     grad, project_grad, vector = back_project(1, grad_one, sums, pieces)
     far_one = swap_all(project_grad, attn_nat, vector)
@@ -1979,10 +1979,8 @@
 
     attn_terms = back_terms(1, *terms_args, far_one)
     rows = rows_of[0][0]
-    totals = sum_more(totals, grad)
     grad_two, grad_low, sums = finish_back_fast(False, grad, perm, rows, *ends_zero)
     blocks = peer_gather(grad_low)
-    blocks[2] = after(blocks[2], totals)
     blocks[1] = after(blocks[1], feed_sum_one, attn_terms[0])
     feed_sum_one = chips_scatter(feed_sum_one).astype(F32)
     inputs, pre, act = slice_saved
@@ -1997,7 +1995,8 @@
     attn_terms = [
         attn_terms[0], after(attn_terms[1], grad_one), attn_terms[2], after(attn_terms[3], grad_one)
     ]
-    grads[0] = after(grads[0], feed_sum_one)
+    totals = sum_more(totals, grad_one)
+    grads[0] = after(grads[0], feed_sum_one, totals)
     grad_q, near, far = back_attend(0, grads)
     feed_term = slice_terms_fast(
         perm_rows, perm_units, blocks, inputs, act, after(slope, grad_q), core_swap(gave)

time: 475 us -> 472 us (level)
    ppermute x18, waiting for transfers between devices: 37.7 us -> 29.7 us  [peer_shift(): return lax.ppermute(array, 'dp', [(i, i ^ bits) for i in range(size)])]
  transfers between devices with their start and end apart: 108 -> 108, of which waited for: 50 -> 48; matrix products, arithmetic and copies ran while one was open for 3% -> 3% of each run, Pallas kernels for 24% -> 24%
where the time goes in v5:
time: 472 us; the launch traced here: 463 us
  waiting for transfers between devices  154 us (33%)
  Pallas kernels  148 us (31%)
  starting transfers between devices  103 us (22%)
  local copies, waits for them, and re-layouts  26.6 us (6%)
  between operations  15.9 us (3%)
  other arithmetic  7.88 us (2%)
  matrix products  7.24 us (2%)
    pallas_call x28, Pallas kernels, run(): pl.pallas_call(kernel, name=name, out_shape=list(outs), in_specs=[VMEM] *...  148 us
    ppermute x33, starting transfers between devices, chip_shift(): return lax.ppermute(array, 'seq', pairs)  54 us
    ppermute x16, waiting for transfers between devices, dp_swap(): return lax.ppermute(array, 'dp', [(i, i ^ bit) for i in range(size)])  45 us
    ppermute x33, waiting for transfers between devices, chip_shift(): return lax.ppermute(array, 'seq', pairs)  37.1 us
    ppermute x18, waiting for transfers between devices, peer_shift(): return lax.ppermute(array, 'dp', [(i, i ^ bits) for i in range(size)])  29.7 us
    unnamed x237, local copies, waits for them, and re-layouts  23.3 us
    ppermute x18, starting transfers between devices, peer_shift(): return lax.ppermute(array, 'dp', [(i, i ^ bits) for i in range(size)])  21.8 us
    ppermute x5, waiting for transfers between devices, sum_more(): totals = totals + lax.ppermute(after(totals, token), axis, pairs)  19.6 us
  transfers between devices with their start and end apart: 108, of which 48 were waited for; matrix products, arithmetic and copies ran while one was open for 3% of the time, Pallas kernels for 24%

profile of v5, /device:TPU:0, one launch (start us, length us, event | category | flops | bytes accessed | tf_op | source)
XLA Modules:
  0.0 463.3 jit_solution(8848045673638637738)
XLA Ops:
  10.7 4.0 collective-permute-start.1
  19.6 7.1 %collective-permute-done = bf16[24,3200]{1,0:T(8,128)(2,1)} collective-permute-done((bf16[24,3200]{1,0:T(8,128)(2,1)}, bf16[24,3200]{1,0:T(8,128)(2,1)}, u32[]{:S(2)}, u32[]{:S(2)}) %collective-permute-start) | collective-permute-done | bytes 153632 | tf_op jit(solution)/shard_map/ppermute | solution.py:61
  37.8 7.5 %collective-permute-done.6 = bf16[96,1536]{1,0:T(8,128)(2,1)S(1)} collective-permute-done((bf16[96,1536]{1,0:T(8,128)(2,1)S(1)}, bf16[96,1536]{1,0:T(8,128)(2,1)S(1)}, u32[]{:S(2)}, u32[]{:S(2)}) %collective-permute-start.6) | collective-permute-done | bytes 294944 | tf_op jit(solution)/shard_map/ppermute | solution.py:1603
  47.4 8.9 %collective-permute-done.8.rest_1_.refs_1_ = bf16[192,1536]{1,0:T(8,128)(2,1)S(1)} collective-permute-done((bf16[192,1536]{1,0:T(8,128)(2,1)S(1)}, bf16[192,1536]{1,0:T(8,128)(2,1)S(1)}, u32[]{:S(2)}, u32[]{:S(2)}) %collective-permute-start.8) | collective-permute-done | bytes 589856 | tf_op jit(solution)/shard_map/ppermute | solution.py:1603
  62.5 5.7 %project.2 = (bf16[128,768]{1,0:T(8,128)(2,1)}, bf16[128,576]{1,0:T(8,128)(2,1)}, bf16[128,576]{1,0:T(8,128)(2,1)}, bf16[128,576]{1,0:T(8,128)(2,1)}, bf16[128,576]{1,0:T(8,128)(2,1)}) custom-call(bf16[128,768]{1,0:T(8,128)(2,1)} %bitcast.65, bf16[768,768]{1,0:T(8,128)(2,1)} %constant.70.clone.perm, f32[8,768]{1,0:T(8,128)} %constant.83.bias, ...), custom_call_target="tpu_custom_call" | custom-call | flops 905969664 | bytes 14204928 | tf_op jit(solution)/shard_map/project/pallas_call | solution.py:474
  68.3 3.5 collective-permute-start.14
  73.8 2.8 collective-permute-start.16
  76.6 9.6 %all-gather.4.cloned.1.call-done = bf16[96,9216]{1,0:T(8,128)(2,1)} async-done(((bf16[24,9216]{1,0:T(8,128)(2,1)}), bf16[96,9216]{1,0:T(8,128)(2,1)}) %all-gather.4.cloned.1.call-update) | async-done | bytes 1769488 | tf_op jit(solution)/shard_map/all_gather | solution.py:1578
  91.8 5.6 %collective-permute-done.17 = bf16[96,1536]{1,0:T(8,128)(2,1)S(1)} collective-permute-done((bf16[96,1536]{1,0:T(8,128)(2,1)S(1)}, bf16[96,1536]{1,0:T(8,128)(2,1)S(1)}, u32[]{:S(2)}, u32[]{:S(2)}) %collective-permute-start.17) | collective-permute-done | bytes 294944 | tf_op jit(solution)/shard_map/ppermute | solution.py:1603
  104.7 5.6 %attend.2 = (f32[512,192]{1,0:T(8,128)}, f32[512,128]{1,0:T(8,128)}, bf16[128,192]{1,0:T(8,128)(2,1)}, bf16[128,192]{1,0:T(8,128)(2,1)}, bf16[128,192]{1,0:T(8,128)(2,1)}, /*index=5*/bf16[128,192]{1,0:T(8,128)(2,1)}) custom-call(bf16[128,576]{1,0:T(8,128)(2,1)} %get-tuple-element.187.refs_0_, bf16[128,576]{1,0:T(8,128)(2,1)} %copy-done.89, ...), custom_call_target="tpu_custom_call" | custom-call | flops 805306368 | bytes 4063232 | tf_op jit(solution)/shard_map/attend/pallas_call | solution.py:474
  114.9 4.5 collective-permute-start.30
  120.6 4.3 vectors.1
  128.9 4.6 %mix.1 = (bf16[128,768]{1,0:T(8,128)(2,1)}, f32[128,768]{1,0:T(8,128)}, bf16[128,768]{1,0:T(8,128)(2,1)}, f32[128,768]{1,0:T(8,128)}, f32[128,128]{1,0:T(8,128)}...) custom-call(bf16[128,768]{1,0:T(8,128)(2,1)} %get-tuple-element.178.hidden.low, ...), custom_call_target="tpu_custom_call" | custom-call | flops 603979776 | bytes 11681792 | tf_op jit(solution)/shard_map/mix/pallas_call | solution.py:474
  137.9 4.3 collective-permute-done.33.refs_1_.refs_5_
  142.3 5.6 %collective-permute-done.34.refs_2_.refs_6_ = bf16[128,768]{1,0:T(8,128)(2,1)S(1)} collective-permute-done((bf16[128,768]{1,0:T(8,128)(2,1)S(1)}, bf16[128,768]{1,0:T(8,128)(2,1)S(1)}, u32[]{:S(2)}, u32[]{:S(2)}) %collective-permute-start.34) | collective-permute-done | bytes 196640 | tf_op jit(solution)/shard_map/ppermute | solution.py:1760
  150.7 6.6 %slice_feed.1 = (f32[128,768]{1,0:T(8,128)}, bf16[128,768]{1,0:T(8,128)(2,1)}, bf16[128,768]{1,0:T(8,128)(2,1)}, bf16[128,768]{1,0:T(8,128)(2,1)}, f32[512,768]{1,0:T(8,128)}, /*index=5*/bf16[512,768]{1,0:T(8,128)(2,1)}) custom-call(f32[4,768]{1,0:T(4,128)} %get-tuple-element.203.wide_bias, bf16[128,768]{1,0:T(8,128)(2,1)} %get-tuple-element.204.refs_0_.refs_4_, ...), custom_call_target="tpu_custom_call" | custom-call | flops 2415919104 | bytes 13000704 | tf_op jit(solution)/shard_map/slice_feed/pallas_call | solution.py:474
  161.4 3.2 collective-permute-done.36.refs_1_
  164.6 4.7 %collective-permute-done.37.refs_2_ = bf16[128,768]{1,0:T(8,128)(2,1)S(1)} collective-permute-done((bf16[128,768]{1,0:T(8,128)(2,1)}, bf16[128,768]{1,0:T(8,128)(2,1)S(1)}, u32[]{:S(2)}, u32[]{:S(2)}) %collective-permute-start.37) | collective-permute-done | bytes 196640 | tf_op jit(solution)/shard_map/ppermute | solution.py:1760
  172.7 5.1 %project.3 = (bf16[128,768]{1,0:T(8,128)(2,1)}, bf16[128,576]{1,0:T(8,128)(2,1)}, bf16[128,576]{1,0:T(8,128)(2,1)}, bf16[128,576]{1,0:T(8,128)(2,1)}, bf16[128,576]{1,0:T(8,128)(2,1)}) custom-call(f32[128,768]{1,0:T(8,128)} %get-tuple-element.209.source.hidden, bf16[768,768]{1,0:T(8,128)(2,1)} %constant.70.clone.perm, f32[16,768]{1,0:T(8,128)} %get-tuple-element.210.bias, ...), custom_call_target="tpu_custom_call" | custom-call | flops 905969664 | bytes 14254080 | tf_op jit(solution)/shard_map/project/pallas_call | solution.py:474
  177.9 3.7 collective-permute-start.41
  181.6 3.7 collective-permute-done.39.refs_1_
  185.3 3.9 collective-permute-done.40.refs_2_
  192.0 5.6 %attend.3 = (f32[512,192]{1,0:T(8,128)}, f32[512,128]{1,0:T(8,128)}, bf16[128,192]{1,0:T(8,128)(2,1)}, bf16[128,192]{1,0:T(8,128)(2,1)}, bf16[128,192]{1,0:T(8,128)(2,1)}, /*index=5*/bf16[128,192]{1,0:T(8,128)(2,1)}) custom-call(bf16[128,576]{1,0:T(8,128)(2,1)} %get-tuple-element.214.refs_0_, bf16[128,576]{1,0:T(8,128)(2,1)} %copy-done.97, ...), custom_call_target="tpu_custom_call" | custom-call | flops 805306368 | bytes 4063232 | tf_op jit(solution)/shard_map/attend/pallas_call | solution.py:474
  197.8 3.4 collective-permute-start.46
  203.9 4.2 collective-permute-done.47.refs_2_
  210.4 9.9 %feed.1 = (f32[128,768]{1,0:T(8,128)}, bf16[128,768]{1,0:T(8,128)(2,1)}, bf16[128,768]{1,0:T(8,128)(2,1)}, f32[128,3072]{1,0:T(8,128)}, bf16[128,3072]{1,0:T(8,1...) custom-call(f32[128,768]{1,0:T(8,128)} %get-tuple-element.209.source, ...), custom_call_target="tpu_custom_call" | custom-call | flops 3019898880 | bytes 37199872 | tf_op jit(solution)/shard_map/feed/pallas_call | solution.py:474
  220.3 13.2 %feed_back.1 = (f32[128,768]{1,0:T(8,128)}, bf16[128,3840]{1,0:T(8,128)(2,1)}, bf16[128,768]{1,0:T(8,128)(2,1)}, f32[16,768]{1,0:T(8,128)}, bf16[128,192]{1,0:T(...) custom-call(bf16[128,768]{1,0:T(8,128)(2,1)} %bitcast.64, ...), custom_call_target="tpu_custom_call" | custom-call | flops 3623878656 | bytes 37421056 | tf_op jit(solution)/shard_map/feed_back/pallas_call | solution.py:474
  234.1 3.0 collective-permute-done.50.theirs
  238.3 5.6 %feed_terms.1 = bf16[384,6144]{1,0:T(8,128)(2,1)} custom-call(bf16[128,768]{1,0:T(8,128)(2,1)} %get-tuple-element.235.normed, bf16[128,3072]{1,0:T(8,128)(2,1)} %get-tuple-element.236.act, bf16[128,3840]{1,0:T(8,128)(2,1)} %get-tuple-element.237.gave, bf16[128,2688]{1,0:T(8,128)(2,1)} %copy-done.67, bf16[128,3840]{1,0:T(8,128)(2,1)} %copy-done.66), custom_call_target="tpu_custom_call" | custom-call | flops 48318382080 | bytes 334233600 | tf_op jit(solution)/shard_map/feed_terms/pallas_call | solution.py:474
  254.7 8.3 %attend_back.2 = (bf16[512,192]{1,0:T(8,128)(2,1)}, f32[512,384]{1,0:T(8,128)}, bf16[512,384]{1,0:T(8,128)(2,1)}) custom-call(bf16[128,576]{1,0:T(8,128)(2,1)} %get-tuple-element.214.refs_0_, bf16[128,576]{1,0:T(8,128)(2,1)} %copy-done.97, bf16[128,576]{1,0:T(8,128)(2,1)} %copy-done.98, bf16[128,576]{1,0:T(8,128)(2,1)} %copy-done.99, ...), custom_call_target="tpu_custom_call" | custom-call | flops 2013265920 | bytes 6815744 | tf_op jit(solution)/shard_map/attend_back/pallas_call | solution.py:474
  274.5 11.7 %collective-permute-done.58 = f32[2,3]{1,0:T(2,128)S(1)} collective-permute-done((f32[2,3]{1,0:T(2,128)S(1)}, f32[2,3]{1,0:T(2,128)S(1)}, u32[]{:S(2)}, u32[]{:S(2)}) %collective-permute-start.58) | collective-permute-done | bytes 56 | tf_op jit(solution)/shard_map/ppermute | solution.py:1926
  287.0 6.6 %project_back.1 = (f32[128,768]{1,0:T(8,128)}, bf16[128,2304]{1,0:T(8,128)(2,1)}, f32[16,768]{1,0:T(8,128)}) custom-call(f32[128,768]{1,0:T(8,128)} %get-tuple-element.232.grad_one, bf16[768,768]{1,0:T(8,128)(2,1)} %constant.70.clone.perm, f32[16,768]{1,0:T(8,128)} %get-tuple-element.233.sums, bf16[128,576]{1,0:T(8,128)(2,1)} %get-tuple-element.253.refs_0_, ...), custom_call_target="tpu_custom_call" | custom-call | flops 905969664 | bytes 15925248 | tf_op jit(solution)/shard_map/project_back/pallas_call | solution.py:474
  302.5 3.8 attend_terms.2
  306.3 4.1 collective-permute-done.66.refs_2_
  311.2 7.7 %slice_back.1 = (f32[128,768]{1,0:T(8,128)}, bf16[128,768]{1,0:T(8,128)(2,1)}, bf16[128,768]{1,0:T(8,128)(2,1)}, bf16[128,768]{1,0:T(8,128)(2,1)}, bf16[512,768]...) custom-call(bf16[128,768]{1,0:T(8,128)(2,1)} %get-tuple-element.264.refs_0_, ...), custom_call_target="tpu_custom_call" | custom-call | flops 2415919104 | bytes 20889600 | tf_op jit(solution)/shard_map/slice_back/pallas_call | solution.py:474
  322.8 7.9 %collective-permute-done.68 = f32[2,3]{1,0:T(2,128)S(1)} collective-permute-done((f32[2,3]{1,0:T(2,128)S(1)}, f32[2,3]{1,0:T(2,128)S(1)}, u32[]{:S(2)}, u32[]{:S(2)}) %collective-permute-start.68) | collective-permute-done | bytes 56 | tf_op jit(solution)/shard_map/ppermute | solution.py:1926
  331.6 5.0 %mix_back.1 = (f32[128,768]{1,0:T(8,128)}, bf16[128,768]{1,0:T(8,128)(2,1)}, f32[16,768]{1,0:T(8,128)}, bf16[128,192]{1,0:T(8,128)(2,1)}, bf16[128,192]{1,0:T(8,...) custom-call(f32[128,768]{1,0:T(8,128)} %get-tuple-element.260.grad_two, ...), custom_call_target="tpu_custom_call" | custom-call | flops 905969664 | bytes 13008896 | tf_op jit(solution)/shard_map/mix_back/pallas_call | solution.py:474
  338.0 3.3 collective-permute-start.74
  347.4 8.3 %attend_back.3 = (bf16[512,192]{1,0:T(8,128)(2,1)}, f32[512,384]{1,0:T(8,128)}, bf16[512,384]{1,0:T(8,128)(2,1)}) custom-call(bf16[128,576]{1,0:T(8,128)(2,1)} %get-tuple-element.187.refs_0_, bf16[128,576]{1,0:T(8,128)(2,1)} %copy-done.89, bf16[128,576]{1,0:T(8,128)(2,1)} %copy-done.90, bf16[128,576]{1,0:T(8,128)(2,1)} %copy-done.91, ...), custom_call_target="tpu_custom_call" | custom-call | flops 2013265920 | bytes 6815744 | tf_op jit(solution)/shard_map/attend_back/pallas_call | solution.py:474
  358.7 2.8 fold.2
  370.2 6.7 %slice_terms.1 = bf16[384,1536]{1,0:T(8,128)(2,1)} custom-call(bf16[384,384]{1,0:T(8,128)(2,1)} %constant.72.clone.perm_rows, bf16[384,384]{1,0:T(8,128)(2,1)} %constant.73.clone.perm_units, bf16[128,768]{1,0:T(8,128)(2,1)} %get-tuple-element.264.refs_0_, bf16[128,768]{1,0:T(8,128)(2,1)} %copy-done.81, bf16[128,768]{1,0:T(8,128)(2,1)} %copy-done.82, ...), custom_call_target="tpu_custom_call" | custom-call | flops 48318382080 | bytes 290979840 | tf_op jit(solution)/shard_map/slice_terms/pallas_call | solution.py:474
  383.0 5.1 %collect.1 = (bf16[128,2304]{1,0:T(8,128)(2,1)}, f32[16,768]{1,0:T(8,128)}) custom-call(bf16[768,768]{1,0:T(8,128)(2,1)} %constant.70.clone.perm, bf16[768,768]{1,0:T(8,128)(2,1)} %constant.71.clone.perm_wide, f32[8,768]{1,0:T(8,128)} %get-tuple-element.282.feed_sums, f32[16,768]{1,0:T(8,128)} %get-tuple-element.283.sums, ...), custom_call_target="tpu_custom_call" | custom-call | bytes 7323648 | tf_op jit(solution)/shard_map/collect/pallas_call | solution.py:474
  394.1 3.9 attend_terms.3
  400.2 12.5 %collective-permute-done.89.refs_1_ = bf16[192,1536]{1,0:T(8,128)(2,1)S(1)} collective-permute-done((bf16[192,1536]{1,0:T(8,128)(2,1)}, bf16[192,1536]{1,0:T(8,128)(2,1)S(1)}, u32[]{:S(2)}, u32[]{:S(2)}) %collective-permute-start.89) | collective-permute-done | bytes 589856 | tf_op jit(solution)/shard_map/ppermute | solution.py:1603
  415.2 2.9 fold.3
  420.2 6.5 %input_back.1 = bf16[128,768]{1,0:T(8,128)(2,1)} custom-call(f32[128,768]{1,0:T(8,128)} %get-tuple-element.322.grad_one, bf16[768,768]{1,0:T(8,128)(2,1)} %constant.70.clone.perm, bf16[128,2304]{1,0:T(8,128)(2,1)} %get-tuple-element.313.project, bf16[192,1536]{1,0:T(8,128)(2,1)} %copy-done.17, bf16[192,1536]{1,0:T(8,128)(2,1)} %copy-done.27, ...), custom_call_target="tpu_custom_call" | custom-call | flops 18119393280 | bytes 290979840 | tf_op jit(solution)/shard_map/input_back/pallas_call | solution.py:474
  437.7 3.4 collective-permute-start.98
  446.5 7.1 %collective-permute-done.97 = bf16[24,3200]{1,0:T(8,128)(2,1)S(1)} collective-permute-done((bf16[24,3200]{1,0:T(8,128)(2,1)}, bf16[24,3200]{1,0:T(8,128)(2,1)S(1)}, u32[]{:S(2)}, u32[]{:S(2)}) %collective-permute-start.97) | collective-permute-done | bytes 153632 | tf_op jit(solution)/shard_map/ppermute | solution.py:61
  (506 shorter events, 169.9 us)
Async XLA Ops:
  7.2 79.0 %all-gather.4.cloned.1.call-start = ((), (), s32[]{:S(2)}) async-start(), calls=%async_computation.3 | async-start | bytes 2211840 | tf_op jit(solution)/shard_map/all_gather | solution.py:1578
  10.7 24.4 %collective-permute-start.1 = (bf16[24,3200]{1,0:T(8,128)(2,1)}, bf16[24,3200]{1,0:T(8,128)(2,1)}, u32[]{:S(2)}, u32[]{:S(2)}) collective-permute-start(bf16[24,3200]{1,0:T(8,128)(2,1)} %fusion.6), channel_id=1, source_target_pairs={{0,4},{1,5},{2,6},{3,7},{4,0},{5,1},{6,2},{7,3},{8,12},{9,13},{10,... | collective-permute-start | bytes 460808 | tf_op jit(solution)/shard_map/ppermute | solution.py:61
  14.7 20.3 %collective-permute-start.2 = (bf16[24,3200]{1,0:T(8,128)(2,1)}, bf16[24,3200]{1,0:T(8,128)(2,1)}, u32[]{:S(2)}, u32[]{:S(2)}) collective-permute-start(bf16[24,3200]{1,0:T(8,128)(2,1)} %fusion.6), channel_id=1, source_target_pairs={{0,6},{1,7},{2,0},{3,1},{4,2},{5,3},{6,4},{7,5},{8,14},{9,15},{10,... | collective-permute-start | bytes 460808 | tf_op jit(solution)/shard_map/ppermute | solution.py:61
  16.0 10.7 %collective-permute-start = (bf16[24,3200]{1,0:T(8,128)(2,1)}, bf16[24,3200]{1,0:T(8,128)(2,1)}, u32[]{:S(2)}, u32[]{:S(2)}) collective-permute-start(bf16[24,3200]{1,0:T(8,128)(2,1)} %fusion.6), channel_id=1, source_target_pairs={{0,2},{1,3},{2,4},{3,5},{4,6},{5,7},{6,0},{7,1},{8,10},{9,11},{10,... | collective-permute-start | bytes 460808 | tf_op jit(solution)/shard_map/ppermute | solution.py:61
  36.5 97.0 %all-gather.6.cloned.1.call-start = ((), (), s32[]{:S(2)}) async-start(), calls=%async_computation.4 | async-start | bytes 1474560 | tf_op jit(solution)/shard_map/all_gather | solution.py:1578
  45.5 12.2 %collective-permute-start.9 = (bf16[192,1664]{1,0:T(8,128)(2,1)S(1)}, bf16[192,1664]{1,0:T(8,128)(2,1)S(1)}, u32[]{:S(2)}, u32[]{:S(2)}) collective-permute-start(bf16[192,1664]{1,0:T(8,128)(2,1)S(1)} %maximum_select_fusion.rest_4_.refs_0_.refs_4_), channel_id=1, source_target_pairs={{0,8},{8,0},{16,24},{24,16},{1,9},{9,1},{17,25},{25,17},{2,10},{10... | collective-permute-start | bytes 1916936 | tf_op jit(solution)/shard_map/ppermute | solution.py:1603
  47.4 13.3 %collective-permute-start.12 = (bf16[192,1664]{1,0:T(8,128)(2,1)S(1)}, bf16[192,1664]{1,0:T(8,128)(2,1)S(1)}, u32[]{:S(2)}, u32[]{:S(2)}) collective-permute-start(bf16[192,1664]{1,0:T(8,128)(2,1)S(1)} %maximum_select_fusion.rest_4_.refs_0_.refs_4_), channel_id=1, source_target_pairs={{0,1},{1,0},{2,3},{3,2},{4,5},{5,4},{6,7},{7,6},{8,9},{9,8},{10,11... | collective-permute-start | bytes 1916936 | tf_op jit(solution)/shard_map/ppermute | solution.py:54
  68.3 17.9 %collective-permute-start.14 = (bf16[128,576]{1,0:T(8,128)(2,1)}, bf16[128,576]{1,0:T(8,128)(2,1)S(1)}, u32[]{:S(2)}, u32[]{:S(2)}) collective-permute-start(bf16[128,576]{1,0:T(8,128)(2,1)} %get-tuple-element.181), channel_id=1, source_target_pairs={{0,2},{1,3},{2,4},{3,5},{4,6},{5,7},{6,0},{7,1},{8,10},{9,11},{10,... | collective-permute-start | bytes 442376 | tf_op jit(solution)/shard_map/ppermute | solution.py:61
  71.8 16.1 %collective-permute-start.15 = (bf16[128,576]{1,0:T(8,128)(2,1)}, bf16[128,576]{1,0:T(8,128)(2,1)S(1)}, u32[]{:S(2)}, u32[]{:S(2)}) collective-permute-start(bf16[128,576]{1,0:T(8,128)(2,1)} %get-tuple-element.182), channel_id=1, source_target_pairs={{0,4},{1,5},{2,6},{3,7},{4,0},{5,1},{6,2},{7,3},{8,12},{9,13},{10,... | collective-permute-start | bytes 442376 | tf_op jit(solution)/shard_map/ppermute | solution.py:61
  73.8 14.1 %collective-permute-start.16 = (bf16[128,576]{1,0:T(8,128)(2,1)}, bf16[128,576]{1,0:T(8,128)(2,1)S(1)}, u32[]{:S(2)}, u32[]{:S(2)}) collective-permute-start(bf16[128,576]{1,0:T(8,128)(2,1)} %get-tuple-element.183), channel_id=1, source_target_pairs={{0,6},{1,7},{2,0},{3,1},{4,2},{5,3},{6,4},{7,5},{8,14},{9,15},{10,... | collective-permute-start | bytes 442376 | tf_op jit(solution)/shard_map/ppermute | solution.py:61
  91.5 106.0 %all-gather.8.cloned.1.call-start = ((), (), s32[]{:S(2)}) async-start(), calls=%async_computation.5 | async-start | bytes 5898240 | tf_op jit(solution)/shard_map/all_gather | solution.py:1899
  91.7 28.7 %collective-permute-start.25 = (bf16[96,6144]{1,0:T(8,128)(2,1)S(1)}, bf16[96,6144]{1,0:T(8,128)(2,1)S(1)}, u32[]{:S(2)}, u32[]{:S(2)}) collective-permute-start(bf16[96,6144]{1,0:T(8,128)(2,1)S(1)} %slice.123.refs_4_.refs_10_), channel_id=1, source_target_pairs={{0,1},{1,0},{2,3},{3,2},{4,5},{5,4},{6,7},{7,6},{8,9},{9,8},{10,11... | collective-permute-start | bytes 3538952 | tf_op jit(solution)/shard_map/ppermute | solution.py:54
  98.8 14.1 %collective-permute-start.23 = (bf16[192,1536]{1,0:T(8,128)(2,1)S(1)}, bf16[192,1536]{1,0:T(8,128)(2,1)S(1)}, u32[]{:S(2)}, u32[]{:S(2)}) collective-permute-start(bf16[192,1536]{1,0:T(8,128)(2,1)S(1)} %maximum_select_fusion.2.rest_0_.refs_4_), channel_id=1, source_target_pairs={{0,16},{8,24},{16,0},{24,8},{1,17},{9,25},{17,1},{25,9},{2,18},{10... | collective-permute-start | bytes 1769480 | tf_op jit(solution)/shard_map/ppermute | solution.py:1603
  100.5 13.9 %collective-permute-start.24 = (bf16[192,1536]{1,0:T(8,128)(2,1)S(1)}, bf16[192,1536]{1,0:T(8,128)(2,1)S(1)}, u32[]{:S(2)}, u32[]{:S(2)}) collective-permute-start(bf16[192,1536]{1,0:T(8,128)(2,1)S(1)} %maximum_select_fusion.3.rest_4_.refs_4_.refs_0_.refs_8_), channel_id=1, source_target_pairs={{0,8},{8,0},{16,24},{24,16},{1,9},{9,1},{17,25},{25,17},{2,10},{10... | collective-permute-start | bytes 1769480 | tf_op jit(solution)/shard_map/ppermute | solution.py:1603
  103.8 11.1 %collective-permute-start.26 = (bf16[192,1536]{1,0:T(8,128)(2,1)S(1)}, bf16[192,1536]{1,0:T(8,128)(2,1)S(1)}, u32[]{:S(2)}, u32[]{:S(2)}) collective-permute-start(bf16[192,1536]{1,0:T(8,128)(2,1)S(1)} %maximum_select_fusion.2.rest_0_.refs_4_), channel_id=1, source_target_pairs={{0,1},{1,0},{2,3},{3,2},{4,5},{5,4},{6,7},{7,6},{8,9},{9,8},{10,11... | collective-permute-start | bytes 1769480 | tf_op jit(solution)/shard_map/ppermute | solution.py:54
  104.1 15.4 %collective-permute-start.28 = (bf16[192,1536]{1,0:T(8,128)(2,1)S(1)}, bf16[192,1536]{1,0:T(8,128)(2,1)S(1)}, u32[]{:S(2)}, u32[]{:S(2)}) collective-permute-start(bf16[192,1536]{1,0:T(8,128)(2,1)S(1)} %maximum_select_fusion.3.rest_4_.refs_4_.refs_0_.refs_8_), channel_id=1, source_target_pairs={{0,1},{1,0},{2,3},{3,2},{4,5},{5,4},{6,7},{7,6},{8,9},{9,8},{10,11... | collective-permute-start | bytes 1769480 | tf_op jit(solution)/shard_map/ppermute | solution.py:54
  114.9 11.0 %collective-permute-start.30 = (bf16[128,192]{1,0:T(8,128)(2,1)}, bf16[128,192]{1,0:T(8,128)(2,1)S(1)}, u32[]{:S(2)}, u32[]{:S(2)}) collective-permute-start(bf16[128,192]{1,0:T(8,128)(2,1)} %get-tuple-element.198), channel_id=1, source_target_pairs={{0,6},{1,7},{2,0},{3,1},{4,2},{5,3},{6,4},{7,5},{8,14},{9,15},{10,... | collective-permute-start | bytes 147464 | tf_op jit(solution)/shard_map/ppermute | solution.py:61
  133.6 166.5 %reduce-scatter.4.cloned.1.call-start = ((), (), s32[]{:S(2)}) async-start(), calls=%async_computation.6 | async-start | bytes 5898240 | tf_op jit(solution)/shard_map/reduce_scatter | solution.py:1969
  135.9 11.9 %collective-permute-start.34 = (bf16[128,768]{1,0:T(8,128)(2,1)S(1)}, bf16[128,768]{1,0:T(8,128)(2,1)S(1)}, u32[]{:S(2)}, u32[]{:S(2)}) collective-permute-start(bf16[128,768]{1,0:T(8,128)(2,1)S(1)} %copy-done.75), channel_id=1, source_target_pairs={{0,16},{8,24},{16,0},{24,8},{1,17},{9,25},{17,1},{25,9},{2,18},{10... | collective-permute-start | bytes 589832 | tf_op jit(solution)/shard_map/ppermute | solution.py:1760
  137.4 12.7 %collective-permute-start.35 = (bf16[128,768]{1,0:T(8,128)(2,1)S(1)}, bf16[128,768]{1,0:T(8,128)(2,1)S(1)}, u32[]{:S(2)}, u32[]{:S(2)}) collective-permute-start(bf16[128,768]{1,0:T(8,128)(2,1)S(1)} %copy-done.75), channel_id=1, source_target_pairs={{0,24},{8,16},{16,8},{24,0},{1,25},{9,17},{17,9},{25,1},{2,26},{10... | collective-permute-start | bytes 589832 | tf_op jit(solution)/shard_map/ppermute | solution.py:1760
  177.8 11.4 %collective-permute-start.40 = (bf16[128,576]{1,0:T(8,128)(2,1)}, bf16[128,576]{1,0:T(8,128)(2,1)S(1)}, u32[]{:S(2)}, u32[]{:S(2)}) collective-permute-start(bf16[128,576]{1,0:T(8,128)(2,1)} %get-tuple-element.216), channel_id=1, source_target_pairs={{0,4},{1,5},{2,6},{3,7},{4,0},{5,1},{6,2},{7,3},{8,12},{9,13},{10,... | collective-permute-start | bytes 442376 | tf_op jit(solution)/shard_map/ppermute | solution.py:61
  177.9 11.4 %collective-permute-start.41 = (bf16[128,576]{1,0:T(8,128)(2,1)}, bf16[128,576]{1,0:T(8,128)(2,1)S(1)}, u32[]{:S(2)}, u32[]{:S(2)}) collective-permute-start(bf16[128,576]{1,0:T(8,128)(2,1)} %get-tuple-element.217), channel_id=1, source_target_pairs={{0,6},{1,7},{2,0},{3,1},{4,2},{5,3},{6,4},{7,5},{8,14},{9,15},{10,... | collective-permute-start | bytes 442376 | tf_op jit(solution)/shard_map/ppermute | solution.py:61
  244.0 101.7 %reduce-scatter.6.cloned.1.call-start = ((), (), s32[]{:S(2)}) async-start(), calls=%async_computation.7 | async-start | bytes 1474560 | tf_op jit(solution)/shard_map/reduce_scatter | solution.py:1584
  269.4 16.8 %collective-permute-start.59 = (bf16[128,576]{1,0:T(8,128)(2,1)}, bf16[128,576]{1,0:T(8,128)(2,1)S(1)}, u32[]{:S(2)}, u32[]{:S(2)}) collective-permute-start(bf16[128,576]{1,0:T(8,128)(2,1)} %get-tuple-element.254), channel_id=1, source_target_pairs={{0,6},{1,7},{2,0},{3,1},{4,2},{5,3},{6,4},{7,5},{8,14},{9,15},{10,... | collective-permute-start | bytes 442376 | tf_op jit(solution)/shard_map/ppermute | solution.py:61
  270.3 15.9 %collective-permute-start.60 = (bf16[128,576]{1,0:T(8,128)(2,1)}, bf16[128,576]{1,0:T(8,128)(2,1)S(1)}, u32[]{:S(2)}, u32[]{:S(2)}) collective-permute-start(bf16[128,576]{1,0:T(8,128)(2,1)} %get-tuple-element.255), channel_id=1, source_target_pairs={{0,4},{1,5},{2,6},{3,7},{4,0},{5,1},{6,2},{7,3},{8,12},{9,13},{10,... | collective-permute-start | bytes 442376 | tf_op jit(solution)/shard_map/ppermute | solution.py:61
  271.5 14.7 %collective-permute-start.61 = (bf16[128,576]{1,0:T(8,128)(2,1)}, bf16[128,576]{1,0:T(8,128)(2,1)S(1)}, u32[]{:S(2)}, u32[]{:S(2)}) collective-permute-start(bf16[128,576]{1,0:T(8,128)(2,1)} %get-tuple-element.256), channel_id=1, source_target_pairs={{0,2},{1,3},{2,4},{3,5},{4,6},{5,7},{6,0},{7,1},{8,10},{9,11},{10,... | collective-permute-start | bytes 442376 | tf_op jit(solution)/shard_map/ppermute | solution.py:61
  272.9 13.3 %collective-permute-start.58 = (f32[2,3]{1,0:T(2,128)S(1)}, f32[2,3]{1,0:T(2,128)S(1)}, u32[]{:S(2)}, u32[]{:S(2)}) collective-permute-start(f32[2,3]{1,0:T(2,128)S(1)} %fusion.33), channel_id=1, source_target_pairs={{0,4},{1,5},{2,6},{3,7},{4,0},{5,1},{6,2},{7,3},{8,12},{9,13},{10,... | collective-permute-start | bytes 80 | tf_op jit(solution)/shard_map/ppermute | solution.py:1926
  299.0 11.4 %collective-permute-start.66 = (bf16[128,768]{1,0:T(8,128)(2,1)}, bf16[128,768]{1,0:T(8,128)(2,1)S(1)}, u32[]{:S(2)}, u32[]{:S(2)}) collective-permute-start(bf16[128,768]{1,0:T(8,128)(2,1)} %get-tuple-element.264.refs_0_), channel_id=1, source_target_pairs={{0,16},{8,24},{16,0},{24,8},{1,17},{9,25},{17,1},{25,9},{2,18},{10... | collective-permute-start | bytes 589832 | tf_op jit(solution)/shard_map/ppermute | solution.py:1760
  300.1 126.7 %reduce-scatter.8.cloned.1.call-start = ((), (), s32[]{:S(2)}) async-start(), calls=%async_computation.8 | async-start | bytes 1474560 | tf_op jit(solution)/shard_map/reduce_scatter | solution.py:1584
  318.9 50.1 %collective-permute-start.81 = (bf16[512,2304]{1,0:T(8,128)(2,1)}, bf16[512,2304]{1,0:T(8,128)(2,1)}, u32[]{:S(2)}, u32[]{:S(2)}) collective-permute-start(bf16[512,2304]{1,0:T(8,128)(2,1)} %get-tuple-element.308), channel_id=1, source_target_pairs={{0,1},{1,0},{2,3},{3,2},{4,5},{5,4},{6,7},{7,6},{8,9},{9,8},{10,11... | collective-permute-start | bytes 7077896 | tf_op jit(solution)/shard_map/ppermute | solution.py:54
  319.0 11.8 %collective-permute-start.69 = (bf16[128,768]{1,0:T(8,128)(2,1)}, bf16[128,768]{1,0:T(8,128)(2,1)S(1)}, u32[]{:S(2)}, u32[]{:S(2)}) collective-permute-start(bf16[128,768]{1,0:T(8,128)(2,1)} %get-tuple-element.277), channel_id=1, source_target_pairs={{0,8},{8,0},{16,24},{24,16},{1,9},{9,1},{17,25},{25,17},{2,10},{10... | collective-permute-start | bytes 589832 | tf_op jit(solution)/shard_map/ppermute | solution.py:1760
  319.3 11.4 %collective-permute-start.70 = (bf16[128,768]{1,0:T(8,128)(2,1)}, bf16[128,768]{1,0:T(8,128)(2,1)S(1)}, u32[]{:S(2)}, u32[]{:S(2)}) collective-permute-start(bf16[128,768]{1,0:T(8,128)(2,1)} %get-tuple-element.278), channel_id=1, source_target_pairs={{0,16},{8,24},{16,0},{24,8},{1,17},{9,25},{17,1},{25,9},{2,18},{10... | collective-permute-start | bytes 589832 | tf_op jit(solution)/shard_map/ppermute | solution.py:1760
  342.7 13.8 %collective-permute-start.76 = (bf16[192,1536]{1,0:T(8,128)(2,1)S(1)}, bf16[192,1536]{1,0:T(8,128)(2,1)S(1)}, u32[]{:S(2)}, u32[]{:S(2)}) collective-permute-start(bf16[192,1536]{1,0:T(8,128)(2,1)S(1)} %copy-done.70), channel_id=1, source_target_pairs={{0,8},{8,0},{16,24},{24,16},{1,9},{9,1},{17,25},{25,17},{2,10},{10... | collective-permute-start | bytes 1769480 | tf_op jit(solution)/shard_map/ppermute | solution.py:1603
  343.5 14.3 %collective-permute-start.77 = (bf16[192,1664]{1,0:T(8,128)(2,1)S(1)}, bf16[192,1664]{1,0:T(8,128)(2,1)S(1)}, u32[]{:S(2)}, u32[]{:S(2)}) collective-permute-start(bf16[192,1664]{1,0:T(8,128)(2,1)S(1)} %copy-done.69), channel_id=1, source_target_pairs={{0,16},{8,24},{16,0},{24,8},{1,17},{9,25},{17,1},{25,9},{2,18},{10... | collective-permute-start | bytes 1916936 | tf_op jit(solution)/shard_map/ppermute | solution.py:1603
  361.5 15.4 %collective-permute-start.79 = (bf16[96,1536]{1,0:T(8,128)(2,1)}, bf16[96,1536]{1,0:T(8,128)(2,1)S(1)}, u32[]{:S(2)}, u32[]{:S(2)}) collective-permute-start(bf16[96,1536]{1,0:T(8,128)(2,1)} %get-tuple-element.303), channel_id=1, source_target_pairs={{0,16},{8,24},{16,0},{24,8},{1,17},{9,25},{17,1},{25,9},{2,18},{10... | collective-permute-start | bytes 884744 | tf_op jit(solution)/shard_map/ppermute | solution.py:1603
  362.8 14.0 %collective-permute-start.80 = (bf16[96,1664]{1,0:T(8,128)(2,1)}, bf16[96,1664]{1,0:T(8,128)(2,1)S(1)}, u32[]{:S(2)}, u32[]{:S(2)}) collective-permute-start(bf16[96,1664]{1,0:T(8,128)(2,1)} %get-tuple-element.305), channel_id=1, source_target_pairs={{0,8},{8,0},{16,24},{24,16},{1,9},{9,1},{17,25},{25,17},{2,10},{10... | collective-permute-start | bytes 958472 | tf_op jit(solution)/shard_map/ppermute | solution.py:1603
  366.8 13.2 %collective-permute-start.82 = (bf16[128,576]{1,0:T(8,128)(2,1)}, bf16[128,576]{1,0:T(8,128)(2,1)S(1)}, u32[]{:S(2)}, u32[]{:S(2)}) collective-permute-start(bf16[128,576]{1,0:T(8,128)(2,1)} %get-tuple-element.310), channel_id=1, source_target_pairs={{0,6},{1,7},{2,0},{3,1},{4,2},{5,3},{6,4},{7,5},{8,14},{9,15},{10,... | collective-permute-start | bytes 442376 | tf_op jit(solution)/shard_map/ppermute | solution.py:61
  368.4 13.9 %collective-permute-start.83 = (bf16[128,576]{1,0:T(8,128)(2,1)}, bf16[128,576]{1,0:T(8,128)(2,1)S(1)}, u32[]{:S(2)}, u32[]{:S(2)}) collective-permute-start(bf16[128,576]{1,0:T(8,128)(2,1)} %get-tuple-element.311), channel_id=1, source_target_pairs={{0,4},{1,5},{2,6},{3,7},{4,0},{5,1},{6,2},{7,3},{8,12},{9,13},{10,... | collective-permute-start | bytes 442376 | tf_op jit(solution)/shard_map/ppermute | solution.py:61
  369.0 13.3 %collective-permute-start.84 = (bf16[128,576]{1,0:T(8,128)(2,1)}, bf16[128,576]{1,0:T(8,128)(2,1)S(1)}, u32[]{:S(2)}, u32[]{:S(2)}) collective-permute-start(bf16[128,576]{1,0:T(8,128)(2,1)} %get-tuple-element.312), channel_id=1, source_target_pairs={{0,2},{1,3},{2,4},{3,5},{4,6},{5,7},{6,0},{7,1},{8,10},{9,11},{10,... | collective-permute-start | bytes 442376 | tf_op jit(solution)/shard_map/ppermute | solution.py:61
  389.2 28.8 %collective-permute-start.101 = (bf16[24,3200]{1,0:T(8,128)(2,1)}, bf16[24,3200]{1,0:T(8,128)(2,1)S(1)}, u32[]{:S(2)}, u32[]{:S(2)}) collective-permute-start(bf16[24,3200]{1,0:T(8,128)(2,1)} %get-tuple-element.335), channel_id=1, source_target_pairs={{0,6},{1,7},{2,0},{3,1},{4,2},{5,3},{6,4},{7,5},{8,14},{9,15},{10,... | collective-permute-start | bytes 460808 | tf_op jit(solution)/shard_map/ppermute | solution.py:61
  390.5 27.5 %collective-permute-start.100 = (bf16[24,3200]{1,0:T(8,128)(2,1)}, bf16[24,3200]{1,0:T(8,128)(2,1)S(1)}, u32[]{:S(2)}, u32[]{:S(2)}) collective-permute-start(bf16[24,3200]{1,0:T(8,128)(2,1)} %get-tuple-element.334), channel_id=1, source_target_pairs={{0,4},{1,5},{2,6},{3,7},{4,0},{5,1},{6,2},{7,3},{8,12},{9,13},{10,... | collective-permute-start | bytes 460808 | tf_op jit(solution)/shard_map/ppermute | solution.py:61
  392.2 25.9 %collective-permute-start.99 = (bf16[24,3200]{1,0:T(8,128)(2,1)}, bf16[24,3200]{1,0:T(8,128)(2,1)S(1)}, u32[]{:S(2)}, u32[]{:S(2)}) collective-permute-start(bf16[24,3200]{1,0:T(8,128)(2,1)} %get-tuple-element.333), channel_id=1, source_target_pairs={{0,2},{1,3},{2,4},{3,5},{4,6},{5,7},{6,0},{7,1},{8,10},{9,11},{10,... | collective-permute-start | bytes 460808 | tf_op jit(solution)/shard_map/ppermute | solution.py:61
  398.0 14.7 %collective-permute-start.89 = (bf16[192,1536]{1,0:T(8,128)(2,1)}, bf16[192,1536]{1,0:T(8,128)(2,1)S(1)}, u32[]{:S(2)}, u32[]{:S(2)}) collective-permute-start(bf16[192,1536]{1,0:T(8,128)(2,1)} %get-tuple-element.318), channel_id=1, source_target_pairs={{0,8},{8,0},{16,24},{24,16},{1,9},{9,1},{17,25},{25,17},{2,10},{10... | collective-permute-start | bytes 1769480 | tf_op jit(solution)/shard_map/ppermute | solution.py:1603
  398.8 15.5 %collective-permute-start.90 = (bf16[192,1664]{1,0:T(8,128)(2,1)}, bf16[192,1664]{1,0:T(8,128)(2,1)S(1)}, u32[]{:S(2)}, u32[]{:S(2)}) collective-permute-start(bf16[192,1664]{1,0:T(8,128)(2,1)} %get-tuple-element.320), channel_id=1, source_target_pairs={{0,16},{8,24},{16,0},{24,8},{1,17},{9,25},{17,1},{25,9},{2,18},{10... | collective-permute-start | bytes 1916936 | tf_op jit(solution)/shard_map/ppermute | solution.py:1603
  418.2 16.4 %collective-permute-start.94 = (bf16[96,1536]{1,0:T(8,128)(2,1)}, bf16[96,1536]{1,0:T(8,128)(2,1)S(1)}, u32[]{:S(2)}, u32[]{:S(2)}) collective-permute-start(bf16[96,1536]{1,0:T(8,128)(2,1)} %get-tuple-element.325), channel_id=1, source_target_pairs={{0,16},{8,24},{16,0},{24,8},{1,17},{9,25},{17,1},{25,9},{2,18},{10... | collective-permute-start | bytes 884744 | tf_op jit(solution)/shard_map/ppermute | solution.py:1603
  419.3 15.3 %collective-permute-start.95 = (bf16[96,1664]{1,0:T(8,128)(2,1)S(1)}, bf16[96,1664]{1,0:T(8,128)(2,1)S(1)}, u32[]{:S(2)}, u32[]{:S(2)}) collective-permute-start(bf16[96,1664]{1,0:T(8,128)(2,1)S(1)} %copy-done.73), channel_id=1, source_target_pairs={{0,8},{8,0},{16,24},{24,16},{1,9},{9,1},{17,25},{25,17},{2,10},{10... | collective-permute-start | bytes 958472 | tf_op jit(solution)/shard_map/ppermute | solution.py:1603
  441.1 12.5 %collective-permute-start.97 = (bf16[24,3200]{1,0:T(8,128)(2,1)}, bf16[24,3200]{1,0:T(8,128)(2,1)S(1)}, u32[]{:S(2)}, u32[]{:S(2)}) collective-permute-start(bf16[24,3200]{1,0:T(8,128)(2,1)} %get-tuple-element.330), channel_id=1, source_target_pairs={{0,4},{1,5},{2,6},{3,7},{4,0},{5,1},{6,2},{7,3},{8,12},{9,13},{10,... | collective-permute-start | bytes 460808 | tf_op jit(solution)/shard_map/ppermute | solution.py:61
  441.7 11.9 %collective-permute-start.96 = (bf16[24,3200]{1,0:T(8,128)(2,1)}, bf16[24,3200]{1,0:T(8,128)(2,1)S(1)}, u32[]{:S(2)}, u32[]{:S(2)}) collective-permute-start(bf16[24,3200]{1,0:T(8,128)(2,1)} %get-tuple-element.329), channel_id=1, source_target_pairs={{0,2},{1,3},{2,4},{3,5},{4,6},{5,7},{6,0},{7,1},{8,10},{9,11},{10,... | collective-permute-start | bytes 460808 | tf_op jit(solution)/shard_map/ppermute | solution.py:61
  (176 other events, 824.1 us)
Sparse Core Ops, SparseCore 0:
  36.7 49.4 all-gather.3
  91.6 30.8 all-gather.5
  133.7 60.0 all-gather.7
  244.2 55.8 reduce-scatter.3
  302.2 29.1 reduce-scatter.5
  389.3 34.5 reduce-scatter.7
